TPU v7x, 512 devices: a whole 4x8x8 slice. The times are simulated.
512 devices in a mesh: fsdp: 16 (over y, core), tok: 32 (over x, z).
Axes of the slice: x: 4, y: 8, z: 8, core: 2. Of those that a mesh axis runs over, the one named last changes fastest.
Arguments:
- embedded_pieces: bfloat16 [16, 4096, 1024], P('fsdp', 'tok'), may hold values from -6 to 6
- morton_arrangement: int32 [16, 32, 128], P('fsdp', 'tok'), may hold values from 0 to 127, each once within a row
- unhidden_indicator: int32 [16, 4096], P('fsdp'), may hold values 0 or 1
- bordering_tiles: int32 [16, 64, 4], P('fsdp'), may hold values from 0 to 63, as said below
- bordering_tally: int32 [16, 64], P('fsdp'), may hold values from 3 to 4
- standardizer_multiplier: bfloat16 [1024], replicated, may hold values from 0.099609375 to 1.8984375
- sharpness_coefficient: float32 [8], replicated, may hold values from 2 to 12
- probe_projector: bfloat16 [1024, 512], P('fsdp'), may hold values from -0.1875 to 0.1875
- lookup_projector: bfloat16 [1024, 512], P('fsdp'), may hold values from -0.1875 to 0.1875
- content_projector: bfloat16 [1024, 512], P('fsdp'), may hold values from -0.75 to 0.75
- result_projector: bfloat16 [512, 1024], P(None, 'fsdp'), may hold values from -0.25 to 0.25
- upstream_derivative: bfloat16 [16, 4096, 1024], P('fsdp', 'tok'), may hold values from -6 to 6
Outputs:
- layer_out: bfloat16 [16, 4096, 1024], P('fsdp', 'tok')
- grad_tokens: bfloat16 [16, 4096, 1024], P('fsdp', 'tok')
Inputs may be any that keep to these rules, and one draw needn't show every extreme that they name: `morton_arrangement`: each row is an order of the positions 0 to 127 of one device. `bordering_tiles`: a block's neighbours lie on other devices than its own (device = block // 2); the 8 entries of one device's blocks are distinct blocks, at most 1 of them on any one device, and exactly 1 on some device.
All inputs are finite; a program needn't handle non-finite values. No bound on the sum of `unhidden_indicator` on one device may be relied on, other than what follows from the above.
Results may differ from a plain program's by a relative error of at most 0.0092.
Values may be sent and summed in bfloat16 or wider, within the bound.
No kernel may reach another device: no remote copies, remote signals or barrier semaphores. Data moves between devices by JAX's collectives and lax.ppermute only.
A program may use at most 64 MiB of HBM per device.

v0:
```python
import jax
import jax.numpy as jnp
from jax import lax
from jax.sharding import PartitionSpec as P

NEARBY_ATTN_SETS = 8
HEAD_DIM = 64
BLOCK = 64
KN = 4
HDT = 512


norm_eps = 1e-05
head_eps = 1e-06


def split_heads(matrix):
    return matrix.reshape(matrix.shape[:-1] + (NEARBY_ATTN_SETS, HEAD_DIM))


def inverse_norm(matrix):
    values = matrix.astype(jnp.float32)
    return 1.0 / jnp.sqrt(jnp.sum(values * values, axis=-1) + head_eps)


def body(
    embedded_pieces,
    morton_arrangement,
    unhidden_indicator,
    bordering_tiles,
    bordering_tally,
    standardizer_multiplier,
    sharpness_coefficient,
    probe_projector,
    lookup_projector,
    content_projector,
    result_projector,
    upstream_derivative,
):
    shards = lax.axis_size("tok")
    my_index = lax.axis_index("tok")
    tok_dev = embedded_pieces.shape[1]
    model_width = embedded_pieces.shape[2]
    per_peer = tok_dev // shards
    blocks = tok_dev // BLOCK
    requests = blocks * KN
    capacity = min(blocks, (requests + shards - 2) // (shards - 1))
    key_count = (1 + KN) * BLOCK
    wq_full, wk_full, wv_full, wo_full = (
        lax.all_gather(probe_projector, "fsdp", axis=0, tiled=True),
        lax.all_gather(lookup_projector, "fsdp", axis=0, tiled=True),
        lax.all_gather(content_projector, "fsdp", axis=0, tiled=True),
        lax.all_gather(result_projector, "fsdp", axis=1, tiled=True),
    )
    local_order = morton_arrangement[0, 0]
    arranged = jnp.take(embedded_pieces[0], local_order, axis=0).reshape(
        shards, per_peer, model_width
    )
    grouped = lax.all_to_all(arranged, "tok", split_axis=0, concat_axis=0, tiled=True).reshape(
        tok_dev, model_width
    )
    grouped_f = grouped.astype(jnp.float32)
    centered = grouped_f - jnp.mean(grouped_f, axis=-1, keepdims=True)
    inv_std = 1.0 / jnp.sqrt(jnp.mean(centered * centered, axis=-1, keepdims=True) + norm_eps)
    normed = centered * inv_std
    gain_f = standardizer_multiplier.astype(jnp.float32)
    normalized = (normed * gain_f).astype(jnp.bfloat16)
    queries = jnp.dot(normalized, wq_full, preferred_element_type=jnp.float32).astype(jnp.bfloat16)
    key_rows = jnp.dot(normalized, wk_full, preferred_element_type=jnp.float32).astype(jnp.bfloat16)
    value_rows = jnp.dot(normalized, wv_full, preferred_element_type=jnp.float32).astype(
        jnp.bfloat16
    )
    all_lists = bordering_tiles[0].reshape(shards, requests)
    all_used = (
        jnp.arange(KN)[None, None, :] < bordering_tally[0].reshape(shards, blocks)[:, :, None]
    ).reshape(shards, requests)
    all_source = all_lists // blocks
    all_block = all_lists % blocks
    earlier = jnp.arange(requests)[None, :, None] > jnp.arange(requests)[None, None, :]
    same_source = all_source[:, :, None] == all_source[:, None, :]
    all_slot = jnp.sum((same_source & earlier).astype(jnp.int32), axis=2)
    hits = (all_source == my_index) & all_used
    hit_slot = hits[:, :, None] & (all_slot[:, :, None] == jnp.arange(capacity)[None, None, :])
    slot_valid = jnp.any(hit_slot, axis=1)
    send_block = jnp.sum(hit_slot.astype(jnp.int32) * all_block[:, :, None], axis=1)
    picked = hit_slot[:, :, :, None] & (
        all_block[:, :, None, None] == jnp.arange(blocks)[None, None, None, :]
    )
    select = jnp.sum(picked.astype(jnp.float32), axis=1).astype(jnp.bfloat16)
    pair_blocks = jnp.concatenate([key_rows, value_rows], axis=-1).reshape(blocks, BLOCK, 2 * HDT)
    gathered_pairs = jnp.take(pair_blocks, send_block.reshape(-1), axis=0).reshape(
        shards, capacity, BLOCK, 2 * HDT
    )
    outgoing = jnp.where(slot_valid[:, :, None, None], gathered_pairs, jnp.zeros((), jnp.bfloat16))
    incoming = lax.all_to_all(outgoing, "tok", split_axis=0, concat_axis=0, tiled=True)
    my_lists = lax.dynamic_slice_in_dim(all_lists, my_index, 1, 0)[0]
    my_source = lax.dynamic_slice_in_dim(all_source, my_index, 1, 0)[0]
    my_slot = lax.dynamic_slice_in_dim(all_slot, my_index, 1, 0)[0]
    my_used = lax.dynamic_slice_in_dim(all_used, my_index, 1, 0)[0].reshape(blocks, KN)
    flat_index = my_source * capacity + my_slot
    tiles = jnp.take(
        incoming.reshape(shards * capacity, BLOCK, 2 * HDT), flat_index, axis=0
    ).reshape(blocks, KN, BLOCK, 2 * HDT)
    seen_all = unhidden_indicator[0].reshape(-1, BLOCK) > 0
    own_seen = lax.dynamic_slice_in_dim(seen_all, my_index * blocks, blocks, 0)
    tile_seen = (
        jnp.take(seen_all, my_lists, axis=0).reshape(blocks, KN, BLOCK) & my_used[:, :, None]
    )
    own_allowed = own_seen[:, None, :] | jnp.eye(BLOCK, dtype=bool)[None]
    tile_allowed = jnp.broadcast_to(
        tile_seen.reshape(blocks, 1, KN * BLOCK), (blocks, BLOCK, KN * BLOCK)
    )
    allowed = jnp.concatenate([own_allowed, tile_allowed], axis=-1)
    query_heads = split_heads(queries).reshape(blocks, BLOCK, NEARBY_ATTN_SETS, HEAD_DIM)
    key_own = key_rows.reshape(blocks, 1, BLOCK, HDT)
    value_own = value_rows.reshape(blocks, 1, BLOCK, HDT)
    key_all = jnp.concatenate([key_own, tiles[..., :HDT]], axis=1).reshape(
        blocks, key_count, NEARBY_ATTN_SETS, HEAD_DIM
    )
    value_all = jnp.concatenate([value_own, tiles[..., HDT:]], axis=1).reshape(
        blocks, key_count, NEARBY_ATTN_SETS, HEAD_DIM
    )
    reciprocal_probe_length = inverse_norm(query_heads)
    reciprocal_lookup_length = inverse_norm(key_all)
    multiplier_amount = (
        sharpness_coefficient[None, :, None, None]
        * jnp.transpose(reciprocal_probe_length, (0, 2, 1))[..., None]
        * jnp.transpose(reciprocal_lookup_length, (0, 2, 1))[:, :, None, :]
    )
    raw = jnp.einsum("bihd,bjhd->bhij", query_heads, key_all, preferred_element_type=jnp.float32)
    scores = multiplier_amount * raw
    expo = jnp.where(allowed[:, None], jnp.exp(scores), 0.0)
    prob = expo / jnp.sum(expo, axis=-1, keepdims=True)
    prob_b = prob.astype(jnp.bfloat16)
    attended = jnp.einsum(
        "bhij,bjhd->bihd", prob_b, value_all, preferred_element_type=jnp.float32
    ).astype(jnp.bfloat16)
    attended = attended.reshape(tok_dev, HDT)
    layer_out = (grouped_f + jnp.dot(attended, wo_full, preferred_element_type=jnp.float32)).astype(
        jnp.bfloat16
    )
    grad_in = upstream_derivative[0]
    grad_attn = jnp.dot(grad_in, wo_full.T, preferred_element_type=jnp.float32).astype(jnp.bfloat16)
    grad_heads = split_heads(grad_attn).reshape(blocks, BLOCK, NEARBY_ATTN_SETS, HEAD_DIM)
    dprob = jnp.einsum("bihd,bjhd->bhij", grad_heads, value_all, preferred_element_type=jnp.float32)
    delta = jnp.sum(prob * dprob, axis=-1, keepdims=True)
    dscore = prob * (dprob - delta)
    weighted = (multiplier_amount * dscore).astype(jnp.bfloat16)
    score_grad = scores * dscore
    row_terms = jnp.transpose(jnp.sum(score_grad, axis=-1), (0, 2, 1))
    col_terms = jnp.transpose(jnp.sum(score_grad, axis=2), (0, 2, 1))
    grad_query = jnp.einsum(
        "bhij,bjhd->bihd", weighted, key_all, preferred_element_type=jnp.float32
    )
    grad_query = grad_query - (reciprocal_probe_length * reciprocal_probe_length * row_terms)[
        ..., None
    ] * query_heads.astype(jnp.float32)
    grad_query = grad_query.astype(jnp.bfloat16).reshape(tok_dev, HDT)
    key_part = jnp.einsum(
        "bhij,bihd->bjhd", weighted, query_heads, preferred_element_type=jnp.float32
    )
    key_part = key_part - (reciprocal_lookup_length * reciprocal_lookup_length * col_terms)[
        ..., None
    ] * key_all.astype(jnp.float32)
    value_part = jnp.einsum(
        "bhij,bihd->bjhd", prob_b, grad_heads, preferred_element_type=jnp.float32
    )
    key_part = key_part.reshape(blocks, 1 + KN, BLOCK, HDT)
    value_part = value_part.reshape(blocks, 1 + KN, BLOCK, HDT)
    tile_part = jnp.concatenate([key_part[:, 1:], value_part[:, 1:]], axis=-1).astype(jnp.bfloat16)
    slot_match = jnp.arange(shards * capacity)[:, None] == flat_index[None, :]
    slot_filled = jnp.any(slot_match, axis=1)
    slot_request = jnp.sum(
        slot_match.astype(jnp.int32) * jnp.arange(requests, dtype=jnp.int32)[None, :], axis=1
    )
    placed = jnp.take(tile_part.reshape(requests, BLOCK, 2 * HDT), slot_request, axis=0)
    outgoing_grad = jnp.where(
        slot_filled[:, None, None], placed, jnp.zeros((), jnp.bfloat16)
    ).reshape(shards, capacity, BLOCK, 2 * HDT)
    returned = lax.all_to_all(outgoing_grad, "tok", split_axis=0, concat_axis=0, tiled=True)
    remote = jnp.einsum("dcb,dctf->btf", select, returned, preferred_element_type=jnp.float32)
    grad_key = (key_part[:, 0] + remote[..., :HDT]).astype(jnp.bfloat16).reshape(tok_dev, HDT)
    grad_value = (value_part[:, 0] + remote[..., HDT:]).astype(jnp.bfloat16).reshape(tok_dev, HDT)
    grad_hidden = jnp.dot(grad_query, wq_full.T, preferred_element_type=jnp.float32)
    grad_hidden = grad_hidden + jnp.dot(grad_key, wk_full.T, preferred_element_type=jnp.float32)
    grad_hidden = grad_hidden + jnp.dot(grad_value, wv_full.T, preferred_element_type=jnp.float32)
    grad_normed = grad_hidden * gain_f
    grad_grouped = grad_in.astype(jnp.float32) + inv_std * (
        grad_normed
        - jnp.mean(grad_normed, axis=-1, keepdims=True)
        - normed * jnp.mean(grad_normed * normed, axis=-1, keepdims=True)
    )
    grad_grouped = grad_grouped.astype(jnp.bfloat16).reshape(shards, per_peer, model_width)
    sweep_rows = lax.all_to_all(
        grad_grouped, "tok", split_axis=0, concat_axis=0, tiled=True
    ).reshape(tok_dev, model_width)
    inverse = (
        jnp.zeros((tok_dev,), jnp.int32).at[local_order].set(jnp.arange(tok_dev, dtype=jnp.int32))
    )
    grad_tokens = jnp.take(sweep_rows, inverse, axis=0)
    return (layer_out[None], grad_tokens[None])


def solution(mesh):
    placed = (
        P("fsdp", "tok", None),
        P("fsdp", "tok", None),
        P("fsdp", None),
        P("fsdp", None, None),
        P("fsdp", None),
        P(),
        P(),
        P("fsdp", None),
        P("fsdp", None),
        P("fsdp", None),
        P(None, "fsdp"),
        P("fsdp", "tok", None),
    )
    return jax.shard_map(
        body,
        mesh=mesh,
        in_specs=placed,
        out_specs=(P("fsdp", "tok", None), P("fsdp", "tok", None)),
        check_vma=False,
    )
```

profile of v0, /device:TPU:8, one launch (start us, length us, event | category | flops | bytes accessed | tf_op | source)
XLA Modules:
  0.0 403.8 jit_solution(12963933334013116616)
XLA Ops:
  10.4 13.2 %all-to-all-start = ((bf16[32,4,1024]{2,1,0:T(4,128)(2,1)}), bf16[32,4,1024]{2,1,0:T(4,128)(2,1)S(1)}, u32[]{:S(2)}, u32[]{:S(2)}) async-start(bf16[32,4,1024]{2,1,0:T(4,128)(2,1)} %reshape.569), calls=%async_computation | async-start | bytes 524288 | tf_op jit(solution)/shard_map/all_to_all | solution.py:59
  27.9 8.2 %all-to-all-done = bf16[32,4,1024]{2,1,0:T(4,128)(2,1)S(1)} async-done(((bf16[32,4,1024]{2,1,0:T(4,128)(2,1)}), bf16[32,4,1024]{2,1,0:T(4,128)(2,1)S(1)}, u32[]{:S(2)}, u32[]{:S(2)}) %all-to-all-start) | async-done | bytes 262176 | tf_op jit(solution)/shard_map/all_to_all | solution.py:59
  37.0 18.3 %all-gather.7.cloned.1.call-done = bf16[1024,512]{1,0:T(8,128)(2,1)} async-done(((bf16[64,512]{1,0:T(8,128)(2,1)}), bf16[1024,512]{1,0:T(8,128)(2,1)}) %all-gather.7.cloned.1.call-update) | async-done | bytes 1048592 | tf_op jit(solution)/shard_map/all_gather | solution.py:51
  56.9 40.5 %all-gather.5.cloned.1.call-done = bf16[1024,512]{1,0:T(8,128)(2,1)} async-done(((bf16[64,512]{1,0:T(8,128)(2,1)}), bf16[1024,512]{1,0:T(8,128)(2,1)}) %all-gather.5.cloned.1.call-update) | async-done | bytes 1048592 | tf_op jit(solution)/shard_map/all_gather | solution.py:52
  101.7 4.7 %fusion.6 = bf16[32,1,64,1024]{3,2,1,0:T(8,128)(2,1)} fusion(bf16[32,64,1024]{2,1,0:T(8,128)(2,1)} %gather_fusion, pred[32]{0:T(512)(128)(4,1)S(1)} %compare_and_fusion.4, pred[32]{0:T(512)(128)(4,1)S(1)} %reduce_or.27), kind=kLoop, calls=%fused_computation.15 | loop fusion | flops 4194304 | bytes 8388672 | tf_op jit(solution)/shard_map/jit(_where)/select_n | solution.py:94
  106.4 10.4 %all-to-all-start.1 = ((bf16[32,1,64,1024]{3,2,1,0:T(8,128)(2,1)}), bf16[32,1,64,1024]{3,2,1,0:T(8,128)(2,1)}, u32[]{:S(2)}, u32[]{:S(2)}) async-start(bf16[32,1,64,1024]{3,2,1,0:T(8,128)(2,1)} %fusion.6), calls=%async_computation.1 | async-start | bytes 8388608 | tf_op jit(solution)/shard_map/all_to_all | solution.py:95
  122.7 36.6 %all-gather.11.cloned.1.call-done = bf16[512,1024]{0,1:T(8,128)(2,1)} async-done(((bf16[512,64]{0,1:T(8,128)(2,1)}), bf16[512,1024]{0,1:T(8,128)(2,1)}) %all-gather.11.cloned.1.call-update) | async-done | bytes 1048592 | tf_op jit(solution)/shard_map/all_gather | solution.py:53
  162.0 39.3 %all-gather.9.cloned.1.call-done = bf16[1024,512]{1,0:T(8,128)(2,1)} async-done(((bf16[64,512]{1,0:T(8,128)(2,1)}), bf16[1024,512]{1,0:T(8,128)(2,1)}) %all-gather.9.cloned.1.call-update) | async-done | bytes 1048592 | tf_op jit(solution)/shard_map/all_gather | solution.py:50
  204.1 7.9 %all-to-all-done.1 = bf16[32,1,64,1024]{3,2,1,0:T(8,128)(2,1)} async-done(((bf16[32,1,64,1024]{3,2,1,0:T(8,128)(2,1)}), bf16[32,1,64,1024]{3,2,1,0:T(8,128)(2,1)}, u32[]{:S(2)}, u32[]{:S(2)}) %all-to-all-start.1) | async-done | bytes 4194336 | tf_op jit(solution)/shard_map/all_to_all | solution.py:95
  212.0 2.8 gather_fusion.1
  226.1 6.6 %multiply_reduce_fusion.1 = (f32[2,8,320]{2,1,0:T(8,128)S(1)}, f32[2,8,64]{2,1,0:T(8,128)}) fusion(f32[2,8,64,320]{3,2,1,0:T(8,128)S(1)} %get-tuple-element.19, f32[2,8,64,320]{3,2,1,0:T(8,128)S(1)} %fusion.70, f32[2,8,64]{2,1,0:T(8,128)S(1)} %get-tuple-element.18, pred[2,64,320]{2,1,0:T(8,128)(4,1)S(1)} %copy-done.12), kind=kOutput, calls=%fused_computation.50 | output fusion | flops 3271999 | bytes 2691072 | tf_op jit(solution)/shard_map/sub | solution.py:147
  232.6 8.5 %fusion.9 = f32[2,320,8,64]{1,3,2,0:T(8,128)} fusion(bf16[2,320,8,64]{1,3,2,0:T(8,128)(2,1)S(1)} %copy.133, bf16[2,64,8,64]{1,3,2,0:T(8,128)(2,1)S(1)} %copy.131, f32[2,320,8]{1,2,0:T(8,128)S(1)} %bitcast_multiply_fusion, f32[2,8,320]{2,1,0:T(8,128)S(1)} %fusion.42, f32[2,8,64]{2,1,0:T(8,128)S(1)} %copy-done.13, f32[2,8,64,320]{3,2,1,0:T(8,128)} %copy-done.7, ...), kind=kOutput, calls=%fused_computation.22 | convolution fusion | flops 46204224 | bytes 4808704 | tf_op jit(solution)/shard_map/bhij,bihd->bjhd/dot_general | solution.py:159
  241.2 3.1 copy.146
  244.3 2.9 reshape.579
  248.4 3.1 copy.143
  251.5 2.9 reshape.578
  255.8 2.9 gather_fusion.3
  258.7 4.7 %fusion.4 = bf16[32,1,64,1024]{3,2,1,0:T(8,128)(2,1)} fusion(bf16[32,64,1024]{2,1,0:T(8,128)(2,1)} %gather_fusion.3, pred[32]{0:T(512)(128)(4,1)S(1)} %copy-done.27, pred[32]{0:T(512)(128)(4,1)S(1)} %copy-done.26), kind=kLoop, calls=%fused_computation.12 | loop fusion | flops 4194304 | bytes 8388672 | tf_op jit(solution)/shard_map/jit(_where)/select_n | solution.py:177
  263.4 7.3 %all-to-all-start.2 = ((bf16[32,1,64,1024]{3,2,1,0:T(8,128)(2,1)}), bf16[32,1,64,1024]{3,2,1,0:T(8,128)(2,1)}, u32[]{:S(2)}, u32[]{:S(2)}) async-start(bf16[32,1,64,1024]{3,2,1,0:T(8,128)(2,1)} %fusion.4), calls=%async_computation.2 | async-start | bytes 8388608 | tf_op jit(solution)/shard_map/all_to_all | solution.py:180
  272.1 7.3 %fusion.18 = bf16[2,64,8,64]{1,3,2,0:T(8,128)(2,1)S(1)} fusion(bf16[2,320,8,64]{1,3,2,0:T(8,128)(2,1)S(1)} %copy.133, bf16[2,64,8,64]{1,3,2,0:T(8,128)(2,1)S(1)} %copy.131, f32[2,64,8]{1,2,0:T(8,128)S(1)} %bitcast_multiply_fusion.1, f32[2,8,320]{2,1,0:T(8,128)S(1)} %fusion.42, f32[2,8,64]{2,1,0:T(8,128)S(1)} %copy-done.13, f32[2,8,64,320]{3,2,1,0:T(8,128)} %copy-done.7, ...), kind=kOutput, calls=%fused_computation.37 | convolution fusion | flops 45483328 | bytes 3612672 | tf_op jit(solution)/shard_map/bhij,bjhd->bihd/dot_general | solution.py:152
  280.4 87.6 %all-to-all-done.2 = bf16[32,1,64,1024]{3,2,1,0:T(8,128)(2,1)} async-done(((bf16[32,1,64,1024]{3,2,1,0:T(8,128)(2,1)}), bf16[32,1,64,1024]{3,2,1,0:T(8,128)(2,1)}, u32[]{:S(2)}, u32[]{:S(2)}) %all-to-all-start.2) | async-done | bytes 4194336 | tf_op jit(solution)/shard_map/all_to_all | solution.py:180
  368.0 6.8 %fusion.1 = f32[2,64,1024]{2,0,1:T(2,128)S(1)} fusion(bf16[32,1,64,1024]{3,2,1,0:T(8,128)(2,1)} %all-to-all-done.2, bf16[32,2]{0,1:T(2,128)(2,1)S(1)} %convert_reduce_fusion.2), kind=kOutput, calls=%fused_computation.8 | convolution fusion | flops 8388608 | bytes 4718720 | tf_op jit(solution)/shard_map/dcb,dctf->btf/dot_general | solution.py:181
  378.5 4.6 %all-to-all-start.3 = ((bf16[32,4,1024]{2,1,0:T(4,128)(2,1)}), bf16[32,4,1024]{2,1,0:T(4,128)(2,1)S(1)}, u32[]{:S(2)}, u32[]{:S(2)}) async-start(bf16[32,4,1024]{2,1,0:T(4,128)(2,1)} %reshape.583), calls=%async_computation.3 | async-start | bytes 524288 | tf_op jit(solution)/shard_map/all_to_all | solution.py:194
  386.7 8.8 %all-to-all-done.3 = bf16[32,4,1024]{2,1,0:T(4,128)(2,1)S(1)} async-done(((bf16[32,4,1024]{2,1,0:T(4,128)(2,1)}), bf16[32,4,1024]{2,1,0:T(4,128)(2,1)S(1)}, u32[]{:S(2)}, u32[]{:S(2)}) %all-to-all-start.3) | async-done | bytes 262176 | tf_op jit(solution)/shard_map/all_to_all | solution.py:194
  (202 shorter events, 50.2 us)
Async XLA Ops:
  7.2 48.1 %all-gather.7.cloned.1.call-start = ((), (), s32[]{:S(2)}) async-start(), calls=%async_computation.5 | async-start | bytes 1114112 | tf_op jit(solution)/shard_map/all_gather | solution.py:51
  8.6 16.4 %copy-start.25 = (s32[1,64]{1,0:T(1,128)S(1)}, s32[1,64]{1,0:T(1,128)}, u32[]{:S(2)}) copy-start(s32[1,64]{1,0:T(1,128)} %param.18) | copy-start | bytes 772
  8.6 17.3 %copy-start.23 = (s32[1,64,4]{1,2,0:T(4,128)S(1)}, s32[1,64,4]{1,2,0:T(4,128)}, u32[]{:S(2)}) copy-start(s32[1,64,4]{1,2,0:T(4,128)} %param.17) | copy-start | bytes 3076
  9.5 17.7 %copy-start.24 = (bf16[1024]{0:T(1024)(128)(2,1)S(1)}, bf16[1024]{0:T(1024)(128)(2,1)}, u32[]{:S(2)}) copy-start(bf16[1024]{0:T(1024)(128)(2,1)} %param.19) | copy-start | bytes 6148
  10.4 25.6 %all-to-all-start = ((bf16[32,4,1024]{2,1,0:T(4,128)(2,1)}), bf16[32,4,1024]{2,1,0:T(4,128)(2,1)S(1)}, u32[]{:S(2)}, u32[]{:S(2)}) async-start(bf16[32,4,1024]{2,1,0:T(4,128)(2,1)} %reshape.569), calls=%async_computation | async-start | bytes 524288 | tf_op jit(solution)/shard_map/all_to_all | solution.py:59
  23.6 73.8 %all-gather.5.cloned.1.call-start = ((), (), s32[]{:S(2)}) async-start(), calls=%async_computation.4 | async-start | bytes 1114112 | tf_op jit(solution)/shard_map/all_gather | solution.py:52
  36.3 20.5 %copy-start.17 = (f32[128]{0:T(128)}, f32[128]{0:T(128)S(1)}, u32[]{:S(2)}) copy-start(f32[128]{0:T(128)S(1)} %div.45) | copy-start | bytes 1540
  36.8 62.1 %copy-start.19 = (f32[128]{0:T(128)}, f32[128]{0:T(128)S(1)}, u32[]{:S(2)}) copy-start(f32[128]{0:T(128)S(1)} %sqrt.14) | copy-start | bytes 1540
  106.4 12.2 %copy-start.14 = (s32[1,4096]{1,0:T(1,128)S(1)}, s32[1,4096]{1,0:T(1,128)}, u32[]{:S(2)}) copy-start(s32[1,4096]{1,0:T(1,128)} %param.16) | copy-start | bytes 49156
  106.4 53.0 %copy-start.10 = (bf16[1,128,1024]{2,1,0:T(8,128)(2,1)S(1)}, bf16[1,128,1024]{2,1,0:T(8,128)(2,1)}, u32[]{:S(2)}) copy-start(bf16[1,128,1024]{2,1,0:T(8,128)(2,1)} %param.25) | copy-start | bytes 786436
  106.4 105.6 %all-to-all-start.1 = ((bf16[32,1,64,1024]{3,2,1,0:T(8,128)(2,1)}), bf16[32,1,64,1024]{3,2,1,0:T(8,128)(2,1)}, u32[]{:S(2)}, u32[]{:S(2)}) async-start(bf16[32,1,64,1024]{3,2,1,0:T(8,128)(2,1)} %fusion.6), calls=%async_computation.1 | async-start | bytes 8388608 | tf_op jit(solution)/shard_map/all_to_all | solution.py:95
  116.9 42.5 %all-gather.11.cloned.1.call-start = ((), (), s32[]{:S(2)}) async-start(), calls=%async_computation.7 | async-start | bytes 1114112 | tf_op jit(solution)/shard_map/all_gather | solution.py:53
  117.6 83.7 %all-gather.9.cloned.1.call-start = ((), (), s32[]{:S(2)}) async-start(), calls=%async_computation.6 | async-start | bytes 1114112 | tf_op jit(solution)/shard_map/all_gather | solution.py:50
  161.1 42.3 %copy-start.28 = (f32[8]{0:T(128)S(1)}, f32[8]{0:T(128)}, u32[]{:S(2)}) copy-start(f32[8]{0:T(128)} %param.20) | copy-start | bytes 100
  224.2 8.4 %copy-start.15 = (f32[2,8,64]{2,1,0:T(8,128)}, f32[2,8,64]{2,1,0:T(8,128)S(1)}, u32[]{:S(2)}) copy-start(f32[2,8,64]{2,1,0:T(8,128)S(1)} %get-tuple-element.18) | copy-start | bytes 12292
  263.4 7.3 %copy-start.30 = (s32[1,1,128]{2,1,0:T(1,128)S(1)}, s32[1,1,128]{2,1,0:T(1,128)}, u32[]{:S(2)}) copy-start(s32[1,1,128]{2,1,0:T(1,128)} %param.15) | copy-start | bytes 1540
  263.4 8.6 %copy-start.22 = (pred[32,8]{0,1:T(8,128)(4,1)S(1)}, pred[32,8]{0,1:T(8,128)(4,1)}, u32[]{:S(2)}) copy-start(pred[32,8]{0,1:T(8,128)(4,1)} %get-tuple-element.7) | copy-start | bytes 772
  263.4 8.6 %copy-start.21 = (f32[2,8,64]{2,1,0:T(8,128)S(1)}, f32[2,8,64]{2,1,0:T(8,128)}, u32[]{:S(2)}) copy-start(f32[2,8,64]{2,1,0:T(8,128)} %get-tuple-element.4) | copy-start | bytes 12292
  263.4 8.6 %copy-start.16 = (f32[2,8,64]{2,1,0:T(8,128)S(1)}, f32[2,8,64]{2,1,0:T(8,128)}, u32[]{:S(2)}) copy-start(f32[2,8,64]{2,1,0:T(8,128)} %copy-done.15) | copy-start | bytes 12292
  263.4 104.6 %all-to-all-start.2 = ((bf16[32,1,64,1024]{3,2,1,0:T(8,128)(2,1)}), bf16[32,1,64,1024]{3,2,1,0:T(8,128)(2,1)}, u32[]{:S(2)}, u32[]{:S(2)}) async-start(bf16[32,1,64,1024]{3,2,1,0:T(8,128)(2,1)} %fusion.4), calls=%async_computation.2 | async-start | bytes 8388608 | tf_op jit(solution)/shard_map/all_to_all | solution.py:180
  272.1 7.8 %copy-start.4 = (bf16[1024,512]{1,0:T(8,128)(2,1)S(1)}, bf16[1024,512]{1,0:T(8,128)(2,1)}, u32[]{:S(2)}) copy-start(bf16[1024,512]{1,0:T(8,128)(2,1)} %all-gather.9.cloned.1.call-done) | copy-start | bytes 3145732
  280.3 94.4 %slice-start = ((f32[2,5,64,512]{3,2,1,0:T(8,128)}), f32[2,1,64,512]{3,2,1,0:T(8,128)S(1)}, s32[]{:S(2)}) async-start(f32[2,5,64,512]{3,2,1,0:T(8,128)} %reshape.578), calls=%async_computation.8 | async-start | bytes 524288 | tf_op jit(solution)/shard_map/slice | solution.py:182
  280.3 94.4 %slice-start.1 = ((f32[2,5,64,512]{3,2,1,0:T(8,128)}), f32[2,1,64,512]{3,2,1,0:T(8,128)S(1)}, s32[]{:S(2)}) async-start(f32[2,5,64,512]{3,2,1,0:T(8,128)} %reshape.579), calls=%async_computation.9 | async-start | bytes 524288 | tf_op jit(solution)/shard_map/slice | solution.py:183
  378.5 17.1 %all-to-all-start.3 = ((bf16[32,4,1024]{2,1,0:T(4,128)(2,1)}), bf16[32,4,1024]{2,1,0:T(4,128)(2,1)S(1)}, u32[]{:S(2)}, u32[]{:S(2)}) async-start(bf16[32,4,1024]{2,1,0:T(4,128)(2,1)} %reshape.583), calls=%async_computation.3 | async-start | bytes 524288 | tf_op jit(solution)/shard_map/all_to_all | solution.py:194
  (17 other events, 37.4 us)
Sparse Core Ops, SparseCore 0:
  10.1 45.1 all-gather.6
  57.4 39.8 all-gather.4
  119.8 39.5 all-gather.10
  161.3 39.9 all-gather.8
where the time goes:
time: 405 us; the launch traced here: 404 us
  waiting for transfers between devices  250 us (62%)
  local copies, waits for them, and re-layouts  40.7 us (10%)
  matrix products  36.4 us (9%)
  starting transfers between devices  35.6 us (9%)
  other arithmetic  26.5 us (7%)
  between operations  14.6 us (4%)
    all_to_all x1, waiting for transfers between devices, body(): lax.all_to_all(outgoing_grad, 'tok', split_axis=0, concat_axis=0, tiled=T...  87.6 us
    all_gather x1, waiting for transfers between devices, body(): lax.all_gather(content_projector, 'fsdp', axis=0, tiled=True)  40.5 us
    all_gather x1, waiting for transfers between devices, body(): lax.all_gather(probe_projector, 'fsdp', axis=0, tiled=True)  39.3 us
    all_gather x1, waiting for transfers between devices, body(): lax.all_gather(result_projector, 'fsdp', axis=1, tiled=True)  36.6 us
    all_gather x1, waiting for transfers between devices, body(): lax.all_gather(lookup_projector, 'fsdp', axis=0, tiled=True)  18.3 us
    all_to_all x1, starting transfers between devices, body(): lax.all_to_all(arranged, 'tok', split_axis=0, concat_axis=0, tiled=True)  13.2 us
    all_to_all x1, starting transfers between devices, body(): lax.all_to_all(outgoing, 'tok', split_axis=0, concat_axis=0, tiled=True)  10.4 us
    all_to_all x1, waiting for transfers between devices, body(): lax.all_to_all(grad_grouped, 'tok', split_axis=0, concat_axis=0, tiled=True)  8.84 us
  transfers between devices with their start and end apart: 8, of which 8 were waited for; matrix products, arithmetic and copies ran while one was open for 8% of the time, Pallas kernels for 0%

commit v1 on v0

v1 whole, which is shorter than its diff:
```python
import jax
import jax.numpy as jnp
from jax import lax
from jax.experimental import pallas as pl
from jax.experimental.pallas import tpu as pltpu
from jax.sharding import PartitionSpec as P

HEADS = 8
HEAD_DIM = 64
BLOCK = 64
KN = 4
D = 1024
HDT = 512
SHARDS = 32
TOK = 128
NB = 2
CHUNK = 4
SLOTS = 1 + KN
ITEMS = NB * SLOTS
ROWS = ITEMS * BLOCK
KEYS = SLOTS * BLOCK
HALF = D // 2
PACK = ITEMS * CHUNK
GROUP = 4
GL = GROUP * HEAD_DIM
GR = GROUP * BLOCK

norm_eps = 1e-05
head_eps = 1e-06
F32 = jnp.float32
BF16 = jnp.bfloat16
VM = pl.BlockSpec(memory_space=pltpu.VMEM)
SM = pl.BlockSpec(memory_space=pltpu.SMEM)
NN = (((1,), (0,)), ((), ()))
NT = (((1,), (1,)), ((), ()))
TN = (((0,), (0,)), ((), ()))


def dot(a, b, dims, **kw):
    return lax.dot_general(a, b, dims, preferred_element_type=F32, **kw)


def one_hot(row_ref, rows):
    idx = row_ref[...]
    iota = lax.broadcasted_iota(jnp.int32, (rows, idx.shape[1]), 0)
    return jnp.where(iota == idx, 1.0, 0.0).astype(BF16)


def arrange_kernel(side_ref, order_ref, x_ref, keep_ref, send_ref):
    a = dot(one_hot(order_ref, TOK), x_ref[...], TN).astype(BF16)
    lower = side_ref[0] == 0
    left, right = a[:, :HALF], a[:, HALF:]
    keep_ref[...] = jnp.where(lower, left, right)
    send_ref[...] = jnp.where(lower, right, left)


def pack_kernel(side_ref, target_ref, keep_ref, recv_ref, out_ref):
    lower = side_ref[0] == 0
    keep, recv = keep_ref[...], recv_ref[...]
    table = jnp.concatenate(
        [jnp.where(lower, keep, recv), jnp.where(lower, recv, keep)], axis=0
    )
    out_ref[...] = dot(one_hot(target_ref, 2 * TOK), table, TN).astype(BF16)


def collect_kernel(side_ref, target_ref, in_ref, keep_ref, send_ref):
    total = dot(one_hot(target_ref, 2 * TOK), in_ref[...], NN).astype(BF16)
    lower = side_ref[0] == 0
    even, odd = total[:TOK], total[TOK:]
    keep_ref[...] = jnp.where(lower, even, odd)
    send_ref[...] = jnp.where(lower, odd, even)


def restore_kernel(side_ref, order_ref, keep_ref, recv_ref, out_ref):
    lower = side_ref[0] == 0
    keep, recv = keep_ref[...], recv_ref[...]
    both = jnp.concatenate(
        [jnp.where(lower, keep, recv), jnp.where(lower, recv, keep)], axis=1
    )
    out_ref[...] = dot(one_hot(order_ref, TOK), both, NN).astype(BF16)


def main_kernel(
    sharp_ref,
    in_ref,
    perm_ref,
    back_ref,
    w_ref,
    up_ref,
    gain_ref,
    seen_ref,
    out_ref,
    att_ref,
    own_ref,
    normed_ref,
    rstd_ref,
    xn_ref,
    k_ref,
    v_ref,
    gkv_ref,
    gq_ref,
    gh_ref,
):
    x_in = jnp.concatenate([in_ref[:ROWS], in_ref[ROWS:]], axis=1)
    normed_ref[...] = dot(perm_ref[...], x_in, NN)
    gain = gain_ref[...].astype(F32)
    for t in range(ITEMS):
        rows = pl.ds(t * BLOCK, BLOCK)
        x = normed_ref[rows, :]
        if t % SLOTS == 0:
            own_ref[pl.ds(t // SLOTS * BLOCK, BLOCK), :] = x.astype(BF16)
        centered = x - jnp.mean(x, axis=1, keepdims=True)
        rstd = 1.0 / jnp.sqrt(jnp.mean(centered * centered, axis=1, keepdims=True) + norm_eps)
        normed = centered * rstd
        normed_ref[rows, :] = normed
        rstd_ref[rows, :] = jnp.broadcast_to(rstd, (BLOCK, 128))
        xn_ref[rows, :] = (normed * gain).astype(BF16)
    xn = xn_ref[...]
    k_ref[...] = dot(xn, w_ref[:, HDT : 2 * HDT], NN).astype(BF16)
    v_ref[...] = dot(xn, w_ref[:, 2 * HDT : 3 * HDT], NN).astype(BF16)
    xn_own = jnp.concatenate([xn_ref[pl.ds(b * KEYS, BLOCK), :] for b in range(NB)], axis=0)
    queries = dot(xn_own, w_ref[:, :HDT], NN).astype(BF16)
    grad_attn = dot(up_ref[...], w_ref[:, 3 * HDT :], NN).astype(BF16)

    lane_head = lax.broadcasted_iota(jnp.int32, (BLOCK, GL), 1) // HEAD_DIM
    head_pick = (
        lax.broadcasted_iota(jnp.int32, (HEADS, HDT), 1) // HEAD_DIM
        == lax.broadcasted_iota(jnp.int32, (HEADS, HDT), 0)
    ).astype(F32)
    group_pick = (
        lax.broadcasted_iota(jnp.int32, (8, GL), 1) // HEAD_DIM
        == lax.broadcasted_iota(jnp.int32, (8, GL), 0)
    ).astype(F32)
    diagonal = lax.broadcasted_iota(jnp.int32, (BLOCK, KEYS), 0) == lax.broadcasted_iota(
        jnp.int32, (BLOCK, KEYS), 1
    )

    def spread(m):
        return jnp.concatenate(
            [jnp.where(lane_head == h, m, jnp.zeros_like(m)) for h in range(GROUP)], axis=0
        )

    def gather_heads(m):
        total = jnp.where(lane_head == 0, m[:BLOCK], 0.0)
        for h in range(1, GROUP):
            total = jnp.where(lane_head == h, m[h * BLOCK : (h + 1) * BLOCK], total)
        return total

    for b in range(NB):
        keys = pl.ds(b * KEYS, KEYS)
        own = slice(b * BLOCK, (b + 1) * BLOCK)
        kf = k_ref[keys, :].astype(F32)
        norm2 = dot(head_pick, kf * kf, NT, precision=lax.Precision.HIGHEST)
        inv_k = 1.0 / jnp.sqrt(norm2 + head_eps)
        allowed = (seen_ref[b : b + 1, :] > 0.0) | diagonal
        mask = jnp.concatenate([allowed] * GROUP, axis=0)
        for g in range(HEADS // GROUP):
            lanes = slice(g * GL, (g + 1) * GL)
            qm = spread(queries[own, lanes])
            gm = spread(grad_attn[own, lanes])
            k4 = k_ref[keys, lanes]
            v4 = v_ref[keys, lanes]
            qf = qm.astype(F32)
            inv_q = 1.0 / jnp.sqrt(jnp.sum(qf * qf, axis=1, keepdims=True) + head_eps)
            sharp = jnp.concatenate(
                [jnp.full((BLOCK, 1), sharp_ref[g * GROUP + h], F32) for h in range(GROUP)], axis=0
            )
            ik = inv_k[g * GROUP : (g + 1) * GROUP]
            ik_rows = jnp.concatenate(
                [jnp.broadcast_to(ik[h : h + 1], (BLOCK, KEYS)) for h in range(GROUP)], axis=0
            )
            factor = (sharp * inv_q) * ik_rows
            scores = factor * dot(qm, k4, NT)
            expo = jnp.where(mask, jnp.exp(scores), 0.0)
            prob = expo * (1.0 / jnp.sum(expo, axis=1, keepdims=True))
            prob_b = prob.astype(BF16)
            att_ref[own, lanes] = gather_heads(dot(prob_b, v4, NN)).astype(BF16)
            dprob = dot(gm, v4, NT)
            delta = jnp.sum(prob * dprob, axis=1, keepdims=True)
            dscore = prob * (dprob - delta)
            weighted = (factor * dscore).astype(BF16)
            score_grad = scores * dscore
            row_terms = jnp.sum(score_grad, axis=1, keepdims=True)
            gq = dot(weighted, k4, NN) - (inv_q * inv_q * row_terms) * qf
            gq_ref[own, lanes] = gather_heads(gq).astype(BF16)
            col_terms = jnp.concatenate(
                [
                    jnp.sum(score_grad[h * BLOCK : (h + 1) * BLOCK], axis=0, keepdims=True)
                    for h in range(GROUP)
                ],
                axis=0,
            )
            coef = ik * ik * col_terms
            coef = jnp.concatenate([coef, jnp.zeros_like(coef)], axis=0)
            coef = dot(coef, group_pick, TN, precision=lax.Precision.HIGHEST)
            gk = dot(weighted, qm, TN) - coef * k4.astype(F32)
            gkv_ref[keys, g * GL : (g + 1) * GL] = gk.astype(BF16)
            gkv_ref[keys, HDT + g * GL : HDT + (g + 1) * GL] = dot(prob_b, gm, TN).astype(BF16)

    gh_ref[...] = dot(gkv_ref[...], w_ref[:, HDT : 3 * HDT], NT)
    gq_hidden = dot(gq_ref[...], w_ref[:, :HDT], NT)
    for t in range(ITEMS):
        rows = pl.ds(t * BLOCK, BLOCK)
        hidden = gh_ref[rows, :]
        b = t // SLOTS
        if t % SLOTS == 0:
            hidden = hidden + gq_hidden[b * BLOCK : (b + 1) * BLOCK]
        grad = hidden * gain
        normed = normed_ref[rows, :]
        m1 = jnp.mean(grad, axis=1, keepdims=True)
        m2 = jnp.mean(grad * normed, axis=1, keepdims=True)
        grad = rstd_ref[rows, 0:1] * (grad - m1 - normed * m2)
        if t % SLOTS == 0:
            grad = grad + up_ref[pl.ds(b * BLOCK, BLOCK), :].astype(F32)
        xn_ref[rows, :] = grad.astype(BF16)
    back = dot(back_ref[...], xn_ref[...], NN).astype(BF16)
    out_ref[:ROWS] = back[:, :HALF]
    out_ref[ROWS:] = back[:, HALF:]


def output_kernel(att_ref, own_ref, w_ref, out_ref):
    out_ref[...] = (
        own_ref[...].astype(F32) + dot(att_ref[...], w_ref[:, 3 * HDT :], NT)
    ).astype(BF16)


def call(kernel, outs, args, specs, flops, scratch=(), limit=16):
    outs = [jax.ShapeDtypeStruct(shape, BF16) for shape in outs]
    moved = sum(a.size * a.dtype.itemsize for a in list(args) + outs)
    return pl.pallas_call(
        kernel,
        out_shape=outs,
        in_specs=specs,
        out_specs=[VM] * len(outs),
        scratch_shapes=list(scratch),
        compiler_params=pltpu.CompilerParams(vmem_limit_bytes=limit * 2**20),
        cost_estimate=pl.CostEstimate(flops=flops, bytes_accessed=moved, transcendentals=0),
    )(*args)


def body(
    embedded_pieces,
    morton_arrangement,
    unhidden_indicator,
    bordering_tiles,
    bordering_tally,
    standardizer_multiplier,
    sharpness_coefficient,
    probe_projector,
    lookup_projector,
    content_projector,
    result_projector,
    upstream_derivative,
):
    me = lax.axis_index("tok")
    side = (me // (SHARDS // 2)).reshape(1).astype(jnp.int32)
    partner = [(i, i ^ (SHARDS // 2)) for i in range(SHARDS)]
    shares = jnp.concatenate(
        [probe_projector, lookup_projector, content_projector, result_projector.T], axis=1
    )
    weights = lax.all_gather(shares, "fsdp", axis=0, tiled=True)

    order = morton_arrangement[0]
    keep, send = call(
        arrange_kernel,
        [(TOK, HALF)] * 2,
        (side, order, embedded_pieces[0]),
        [SM, VM, VM],
        2 * TOK * TOK * D,
    )
    recv = lax.ppermute(send, "tok", partner)

    lists = bordering_tiles[0].reshape(SHARDS, NB, KN)
    own_blocks = jnp.arange(SHARDS * NB, dtype=jnp.int32).reshape(SHARDS, NB, 1)
    named = jnp.concatenate([own_blocks, lists], axis=2).reshape(SHARDS, ITEMS)
    target = (named % 2) * TOK + (named // 2) * CHUNK
    target = (target[:, :, None] + jnp.arange(CHUNK, dtype=jnp.int32)).reshape(
        1, SHARDS * PACK
    )
    (packed,) = call(
        pack_kernel,
        [(SHARDS * PACK, HALF)],
        (side, target, keep, recv),
        [SM, VM, VM, VM],
        2 * SHARDS * PACK * 2 * TOK * HALF,
    )
    arrived = lax.all_to_all(
        packed.reshape(SHARDS, PACK, HALF), "tok", split_axis=0, concat_axis=0, tiled=True
    ).reshape(SHARDS * PACK, HALF)

    seen_all = unhidden_indicator[0].reshape(SHARDS * NB, BLOCK).astype(F32)
    used = jnp.arange(SLOTS)[None, :] <= bordering_tally[0][:, None]
    used = used.reshape(SHARDS, ITEMS)
    picks = (
        (named[:, :, None] == jnp.arange(SHARDS * NB)) & used[:, :, None]
    ).astype(F32)
    picks = jnp.sum(picks * (jnp.arange(SHARDS) == me)[:, None, None], axis=0)
    seen = jnp.dot(picks, seen_all).reshape(NB, KEYS)

    dest = jnp.arange(ROWS)
    source = (dest % BLOCK // CHUNK) * PACK + (dest // BLOCK) * CHUNK + dest % CHUNK
    perm = (source[:, None] == jnp.arange(ROWS)[None, :]).astype(BF16)
    back = (source[None, :] == jnp.arange(ROWS)[:, None]).astype(BF16)
    leaving, attended, own = call(
        main_kernel,
        [(SHARDS * PACK, HALF), (TOK, HDT), (TOK, D)],
        (
            sharpness_coefficient,
            arrived,
            perm,
            back,
            weights,
            upstream_derivative[0],
            standardizer_multiplier.reshape(1, D),
            seen,
        ),
        [SM] + [VM] * 7,
        4 * 10**9,
        scratch=[
            pltpu.VMEM((ROWS, D), F32),
            pltpu.VMEM((ROWS, 128), F32),
            pltpu.VMEM((ROWS, D), BF16),
            pltpu.VMEM((ROWS, HDT), BF16),
            pltpu.VMEM((ROWS, HDT), BF16),
            pltpu.VMEM((ROWS, D), BF16),
            pltpu.VMEM((TOK, HDT), BF16),
            pltpu.VMEM((ROWS, D), F32),
        ],
        limit=48,
    )
    returned = lax.all_to_all(
        leaving.reshape(SHARDS, PACK, HALF), "tok", split_axis=0, concat_axis=0, tiled=True
    ).reshape(SHARDS * PACK, HALF)
    (layer_out,) = call(
        output_kernel,
        [(TOK, D)],
        (attended, own, weights),
        [VM] * 3,
        2 * TOK * HDT * D,
    )
    keep, send = call(
        collect_kernel,
        [(TOK, HALF)] * 2,
        (side, target, returned),
        [SM, VM, VM],
        2 * SHARDS * PACK * 2 * TOK * HALF,
    )
    recv = lax.ppermute(send, "tok", partner)
    (grad_tokens,) = call(
        restore_kernel,
        [(TOK, D)],
        (side, order, keep, recv),
        [SM, VM, VM, VM],
        2 * TOK * TOK * D,
    )
    return (layer_out[None], grad_tokens[None])


def solution(mesh):
    placed = (
        P("fsdp", "tok", None),
        P("fsdp", "tok", None),
        P("fsdp", None),
        P("fsdp", None, None),
        P("fsdp", None),
        P(),
        P(),
        P("fsdp", None),
        P("fsdp", None),
        P("fsdp", None),
        P(None, "fsdp"),
        P("fsdp", "tok", None),
    )
    return jax.shard_map(
        body,
        mesh=mesh,
        in_specs=placed,
        out_specs=(P("fsdp", "tok", None), P("fsdp", "tok", None)),
        check_vma=False,
    )
```

time: 405 us -> 139 us (0.34)
  the two profiles are of different devices: /device:TPU:8 before, /device:TPU:40 now
where the time goes in v1:
time: 139 us
  blocking collectives  39.5 us (28%)
  waiting for transfers between devices  37 us (27%)
  starting transfers between devices  21.6 us (16%)
  Pallas kernels  19.4 us (14%)
  between operations  14.2 us (10%)
  local copies, waits for them, and re-layouts  3.67 us (3%)
  other arithmetic  3.36 us (2%)
    all_to_all x1, blocking collectives, body(): lax.all_to_all(leaving.reshape(SHARDS, PACK, HALF), 'tok', split_axis=0,...  39.5 us
    all_to_all x1, waiting for transfers between devices, body(): lax.all_to_all(packed.reshape(SHARDS, PACK, HALF), 'tok', split_axis=0, c...  30.8 us
    pallas_call x6, Pallas kernels, call(): pl.pallas_call(kernel, out_shape=outs, in_specs=specs, out_specs=[VM] * l...  19.4 us
    all_to_all x1, starting transfers between devices, body(): lax.all_to_all(packed.reshape(SHARDS, PACK, HALF), 'tok', split_axis=0, c...  13.3 us
    ppermute x2, starting transfers between devices, body(): recv = lax.ppermute(send, 'tok', partner)  8.25 us
    ppermute x2, waiting for transfers between devices, body(): recv = lax.ppermute(send, 'tok', partner)  6.15 us
    unnamed x20, local copies, waits for them, and re-layouts  2.92 us
  transfers between devices with their start and end apart: 4, of which 3 were waited for; matrix products, arithmetic and copies ran while one was open for 3% of the time, Pallas kernels for 2%

profile of v1, /device:TPU:40, one launch (start us, length us, event | category | flops | bytes accessed | tf_op | source)
XLA Modules:
  0.0 138.9 jit_solution(18396476361328447947)
XLA Ops:
  7.2 1.7 %pad_maximum_fusion = bf16[64,2048]{1,0:T(8,128)(2,1)} fusion(bf16[64,512]{1,0:T(8,128)(2,1)} %bitcast.30, bf16[64,512]{1,0:T(8,128)(2,1)} %param.21, bf16[64,512]{1,0:T(8,128)(2,1)} %param.20, bf16[64,512]{1,0:T(8,128)(2,1)} %param.19), kind=kLoop, calls=%fused_computation.4 | loop fusion | flops 1048576 | bytes 524288 | tf_op jit(solution)/shard_map/concatenate | solution.py:258
  8.9 0.9 copy-done.1
  9.9 0.7 copy-done.2
  10.5 0.3 shard_map.131
  10.8 4.9 %collective-permute-start = (bf16[128,512]{1,0:T(8,128)(2,1)S(1)}, bf16[128,512]{1,0:T(8,128)(2,1)S(1)}, u32[]{:S(2)}, u32[]{:S(2)}) collective-permute-start(bf16[128,512]{1,0:T(8,128)(2,1)S(1)} %get-tuple-element.10), channel_id=1, source_target_pairs={{0,16},{1,17},{2,18},{3,19},{4,20},{5,21},{6,22},{7,23},{8,24},{9,... | collective-permute-start | bytes 393224 | tf_op jit(solution)/shard_map/ppermute | solution.py:271
  15.7 0.8 copy.27
  16.8 0.1 iota_add_fusion
  17.0 0.1 add.134.target_ref
  17.1 2.3 %collective-permute-done.recv_ref = bf16[128,512]{1,0:T(8,128)(2,1)S(1)} collective-permute-done((bf16[128,512]{1,0:T(8,128)(2,1)S(1)}, bf16[128,512]{1,0:T(8,128)(2,1)S(1)}, u32[]{:S(2)}, u32[]{:S(2)}) %collective-permute-start) | collective-permute-done | bytes 131104 | tf_op jit(solution)/shard_map/ppermute | solution.py:271
  19.4 1.6 %shard_map.132 = bf16[1280,512]{1,0:T(8,128)(2,1)} custom-call(s32[1]{0:T(128)} %bitcast.side_ref, s32[1,1280]{1,0:T(1,128)S(1)} %add.134.target_ref, bf16[128,512]{1,0:T(8,128)(2,1)S(1)} %get-tuple-element.9.keep_ref, bf16[128,512]{1,0:T(8,128)(2,1)S(1)} %collective-permute-done.recv_ref), custom_call_target="tpu_custom_call" | custom-call | flops 335544320 | bytes 1577988 | tf_op jit(solution)/shard_map/pallas_call | solution.py:230
  21.1 13.3 %all-to-all-start = ((bf16[32,40,512]{2,1,0:T(8,128)(2,1)}), bf16[32,40,512]{2,1,0:T(8,128)(2,1)S(1)}, u32[]{:S(2)}, u32[]{:S(2)}) async-start(bf16[32,40,512]{2,1,0:T(8,128)(2,1)} %bitcast.4), calls=%async_computation | async-start | bytes 2621440 | tf_op jit(solution)/shard_map/all_to_all | solution.py:287
  34.6 0.5 broadcast.305
  35.1 0.7 reduce.7
  36.1 0.2 select_reduce_fusion
  36.3 0.1 fusion.31
  36.5 0.5 fusion.1
  36.9 30.8 %all-to-all-done = bf16[32,40,512]{2,1,0:T(8,128)(2,1)S(1)} async-done(((bf16[32,40,512]{2,1,0:T(8,128)(2,1)}), bf16[32,40,512]{2,1,0:T(8,128)(2,1)S(1)}, u32[]{:S(2)}, u32[]{:S(2)}) %all-to-all-start) | async-done | bytes 1310752 | tf_op jit(solution)/shard_map/all_to_all | solution.py:287
  67.8 15.0 %shard_map.133 = (bf16[1280,512]{1,0:T(8,128)(2,1)S(1)}, bf16[128,512]{1,0:T(8,128)(2,1)S(1)}, bf16[128,1024]{1,0:T(8,128)(2,1)S(1)}) custom-call(f32[8]{0:T(128)S(1)} %copy-done.5, bf16[1280,512]{1,0:T(8,128)(2,1)S(1)} %bitcast.21, bf16[640,640]{1,0:T(8,128)(2,1)S(1)} %get-tuple-element.17.perm_ref, bf16[640,640]{1,0:T(8,128)(2,1)S(1)} %get-tuple-element.16.back_ref, ...), custom_call_target="tpu_custom_call" | custom-call | flops 4000000000 | bytes 9114144 | tf_op jit(solution)/shard_map/pallas_call | solution.py:230
  82.7 39.5 %all_to_all.10 = bf16[32,40,512]{2,1,0:T(8,128)(2,1)S(1)} all-to-all(bf16[32,40,512]{2,1,0:T(8,128)(2,1)S(1)} %bitcast.22), channel_id=1, replica_groups=mesh['fsdp'=16,'tok'=32] {'tok'}, dimensions={0} | all-to-all | bytes 2621440 | tf_op jit(solution)/shard_map/all_to_all | solution.py:331
  122.3 0.5 shard_map.135
  122.8 3.3 %collective-permute-start.1 = (bf16[128,512]{1,0:T(8,128)(2,1)S(1)}, bf16[128,512]{1,0:T(8,128)(2,1)S(1)}, u32[]{:S(2)}, u32[]{:S(2)}) collective-permute-start(bf16[128,512]{1,0:T(8,128)(2,1)S(1)} %get-tuple-element.15), channel_id=1, source_target_pairs={{0,16},{1,17},{2,18},{3,19},{4,20},{5,21},{6,22},{7,23},{8,24},{9,... | collective-permute-start | bytes 393224 | tf_op jit(solution)/shard_map/ppermute | solution.py:348
  126.1 1.2 shard_map.134
  127.3 3.8 %collective-permute-done.1.recv_ref = bf16[128,512]{1,0:T(8,128)(2,1)S(1)} collective-permute-done((bf16[128,512]{1,0:T(8,128)(2,1)S(1)}, bf16[128,512]{1,0:T(8,128)(2,1)S(1)}, u32[]{:S(2)}, u32[]{:S(2)}) %collective-permute-start.1) | collective-permute-done | bytes 131104 | tf_op jit(solution)/shard_map/ppermute | solution.py:348
  131.2 0.9 shard_map.136
  (38 shorter events, 1.0 us)
Async XLA Ops:
  7.2 60.6 %all-gather.2.cloned.1.call-start = ((), (), s32[]{:S(2)}) async-start(), calls=%async_computation.2 | async-start | bytes 4456448 | tf_op jit(solution)/shard_map/all_gather | solution.py:261
  8.9 1.0 copy-start.1
  9.9 0.7 copy-start.2
  10.8 8.6 %collective-permute-start = (bf16[128,512]{1,0:T(8,128)(2,1)S(1)}, bf16[128,512]{1,0:T(8,128)(2,1)S(1)}, u32[]{:S(2)}, u32[]{:S(2)}) collective-permute-start(bf16[128,512]{1,0:T(8,128)(2,1)S(1)} %get-tuple-element.10), channel_id=1, source_target_pairs={{0,16},{1,17},{2,18},{3,19},{4,20},{5,21},{6,22},{7,23},{8,24},{9,... | collective-permute-start | bytes 393224 | tf_op jit(solution)/shard_map/ppermute | solution.py:271
  21.0 13.4 %copy-start.7 = (bf16[1024]{0:T(1024)(128)(2,1)S(1)}, bf16[1024]{0:T(1024)(128)(2,1)}, u32[]{:S(2)}) copy-start(bf16[1024]{0:T(1024)(128)(2,1)} %param.17) | copy-start | bytes 6148
  21.0 13.4 %copy-start.6 = (s32[1,4096]{1,0:T(1,128)S(1)}, s32[1,4096]{1,0:T(1,128)}, u32[]{:S(2)}) copy-start(s32[1,4096]{1,0:T(1,128)} %param.14) | copy-start | bytes 49156
  21.0 14.1 %copy-start.8 = (s32[1,64]{1,0:T(1,128)S(1)}, s32[1,64]{1,0:T(1,128)}, u32[]{:S(2)}) copy-start(s32[1,64]{1,0:T(1,128)} %param.16) | copy-start | bytes 772
  21.0 46.7 %copy-start.4 = (bf16[1,128,1024]{2,1,0:T(8,128)(2,1)S(1)}, bf16[1,128,1024]{2,1,0:T(8,128)(2,1)}, u32[]{:S(2)}) copy-start(bf16[1,128,1024]{2,1,0:T(8,128)(2,1)} %param.23) | copy-start | bytes 786436
  21.0 46.7 %copy-start.5 = (f32[8]{0:T(128)S(1)}, f32[8]{0:T(128)}, u32[]{:S(2)}) copy-start(f32[8]{0:T(128)} %sharp_ref.1) | copy-start | bytes 100
  21.1 46.7 %all-to-all-start = ((bf16[32,40,512]{2,1,0:T(8,128)(2,1)}), bf16[32,40,512]{2,1,0:T(8,128)(2,1)S(1)}, u32[]{:S(2)}, u32[]{:S(2)}) async-start(bf16[32,40,512]{2,1,0:T(8,128)(2,1)} %bitcast.4), calls=%async_computation | async-start | bytes 2621440 | tf_op jit(solution)/shard_map/all_to_all | solution.py:287
  67.8 58.3 %copy-start = (bf16[1024,2048]{1,0:T(8,128)(2,1)S(1)}, bf16[1024,2048]{1,0:T(8,128)(2,1)}, u32[]{:S(2)}) copy-start(bf16[1024,2048]{1,0:T(8,128)(2,1)} %all-gather.2.cloned.1.call-done.w_ref) | copy-start | bytes 12582916
  122.8 8.4 %collective-permute-start.1 = (bf16[128,512]{1,0:T(8,128)(2,1)S(1)}, bf16[128,512]{1,0:T(8,128)(2,1)S(1)}, u32[]{:S(2)}, u32[]{:S(2)}) collective-permute-start(bf16[128,512]{1,0:T(8,128)(2,1)S(1)} %get-tuple-element.15), channel_id=1, source_target_pairs={{0,16},{1,17},{2,18},{3,19},{4,20},{5,21},{6,22},{7,23},{8,24},{9,... | collective-permute-start | bytes 393224 | tf_op jit(solution)/shard_map/ppermute | solution.py:348
  126.1 5.0 %copy-start.3 = (s32[1,1,128]{2,1,0:T(1,128)S(1)}, s32[1,1,128]{2,1,0:T(1,128)}, u32[]{:S(2)}) copy-start(s32[1,1,128]{2,1,0:T(1,128)} %param.13) | copy-start | bytes 1540
Sparse Core Ops, SparseCore 0:
  10.7 47.0 all-gather.1

commit v2 on v1

--- a/solution.py
+++ b/solution.py
@@ -8,6 +8,7 @@
 HEADS = 8
 HEAD_DIM = 64
 BLOCK = 64
+HB = BLOCK // 2
 KN = 4
 D = 1024
 HDT = 512
@@ -20,10 +21,15 @@
 ROWS = ITEMS * BLOCK
 KEYS = SLOTS * BLOCK
 HALF = D // 2
+FAR = ROWS + ROWS // 2
 PACK = ITEMS * CHUNK
 GROUP = 4
 GL = GROUP * HEAD_DIM
 GR = GROUP * BLOCK
+
+CHIPS = 8
+SHARE = 64
+STEPS = (0, 1, -1, 2, -2, 3, -3, 4)
 
 norm_eps = 1e-05
 head_eps = 1e-06
@@ -40,18 +46,42 @@
     return lax.dot_general(a, b, dims, preferred_element_type=F32, **kw)
 
 
+def rolled(m):
+    return jnp.concatenate([m[:BLOCK], m[BLOCK + HB :], m[BLOCK : BLOCK + HB]], axis=0)
+
+
 def one_hot(row_ref, rows):
     idx = row_ref[...]
     iota = lax.broadcasted_iota(jnp.int32, (rows, idx.shape[1]), 0)
     return jnp.where(iota == idx, 1.0, 0.0).astype(BF16)
 
 
-def arrange_kernel(side_ref, order_ref, x_ref, keep_ref, send_ref):
+def arrange_kernel(
+    side_ref, order_ref, x_ref, wq_ref, wk_ref, wv_ref, wo_ref, keep_ref, send_ref, share_ref
+):
+    for n, part in enumerate((wq_ref, wk_ref, wv_ref, wo_ref)):
+        share_ref[:, n * HDT : (n + 1) * HDT] = part[...]
     a = dot(one_hot(order_ref, TOK), x_ref[...], TN).astype(BF16)
     lower = side_ref[0] == 0
     left, right = a[:, :HALF], a[:, HALF:]
     keep_ref[...] = jnp.where(lower, left, right)
     send_ref[...] = jnp.where(lower, right, left)
+
+
+def stack_kernel(place_ref, *refs):
+    out_ref = refs[-1]
+    for step, ref in zip(STEPS, refs[:-1]):
+        place = lax.rem(place_ref[0] + (CHIPS - step), CHIPS)
+        out_ref[pl.ds(place * SHARE, SHARE), :] = ref[...]
+
+
+def merge_kernel(place_ref, mine_ref, other_ref, out_ref):
+    first = place_ref[1] == 0
+    for y in range(CHIPS):
+        rows = slice(y * SHARE, (y + 1) * SHARE)
+        mine, other = mine_ref[rows, :], other_ref[rows, :]
+        out_ref[2 * y * SHARE : (2 * y + 1) * SHARE, :] = jnp.where(first, mine, other)
+        out_ref[(2 * y + 1) * SHARE : (2 * y + 2) * SHARE, :] = jnp.where(first, other, mine)
 
 
 def pack_kernel(side_ref, target_ref, keep_ref, recv_ref, out_ref):
@@ -101,7 +131,9 @@
     gq_ref,
     gh_ref,
 ):
-    x_in = jnp.concatenate([in_ref[:ROWS], in_ref[ROWS:]], axis=1)
+    x_in = jnp.concatenate(
+        [in_ref[:ROWS], jnp.concatenate([in_ref[FAR:], in_ref[ROWS:FAR]], axis=0)], axis=1
+    )
     normed_ref[...] = dot(perm_ref[...], x_in, NN)
     gain = gain_ref[...].astype(F32)
     for t in range(ITEMS):
@@ -120,7 +152,8 @@
     v_ref[...] = dot(xn, w_ref[:, 2 * HDT : 3 * HDT], NN).astype(BF16)
     xn_own = jnp.concatenate([xn_ref[pl.ds(b * KEYS, BLOCK), :] for b in range(NB)], axis=0)
     queries = dot(xn_own, w_ref[:, :HDT], NN).astype(BF16)
-    grad_attn = dot(up_ref[...], w_ref[:, 3 * HDT :], NN).astype(BF16)
+    up = rolled(up_ref[...])
+    grad_attn = dot(up, w_ref[:, 3 * HDT :], NN).astype(BF16)
 
     lane_head = lax.broadcasted_iota(jnp.int32, (BLOCK, GL), 1) // HEAD_DIM
     head_pick = (
@@ -211,17 +244,17 @@
         m2 = jnp.mean(grad * normed, axis=1, keepdims=True)
         grad = rstd_ref[rows, 0:1] * (grad - m1 - normed * m2)
         if t % SLOTS == 0:
-            grad = grad + up_ref[pl.ds(b * BLOCK, BLOCK), :].astype(F32)
+            grad = grad + up[b * BLOCK : (b + 1) * BLOCK].astype(F32)
         xn_ref[rows, :] = grad.astype(BF16)
     back = dot(back_ref[...], xn_ref[...], NN).astype(BF16)
     out_ref[:ROWS] = back[:, :HALF]
-    out_ref[ROWS:] = back[:, HALF:]
+    out_ref[FAR:] = back[: ROWS // 2, HALF:]
+    out_ref[ROWS:FAR] = back[ROWS // 2 :, HALF:]
 
 
 def output_kernel(att_ref, own_ref, w_ref, out_ref):
-    out_ref[...] = (
-        own_ref[...].astype(F32) + dot(att_ref[...], w_ref[:, 3 * HDT :], NT)
-    ).astype(BF16)
+    out = own_ref[...].astype(F32) + dot(att_ref[...], w_ref[:, 3 * HDT :], NT)
+    out_ref[...] = rolled(out.astype(BF16))
 
 
 def call(kernel, outs, args, specs, flops, scratch=(), limit=16):
@@ -236,6 +269,24 @@
         compiler_params=pltpu.CompilerParams(vmem_limit_bytes=limit * 2**20),
         cost_estimate=pl.CostEstimate(flops=flops, bytes_accessed=moved, transcendentals=0),
     )(*args)
+
+
+def gather_weights(share, place):
+    members = 2 * CHIPS
+    upward = [(i, (i + 2) % members) for i in range(members)]
+    downward = [(i, (i - 2) % members) for i in range(members)]
+    pieces, up, down = [share], share, share
+    for _ in range(CHIPS // 2 - 1):
+        up = lax.ppermute(up, "fsdp", upward)
+        down = lax.ppermute(down, "fsdp", downward)
+        pieces += [up, down]
+    pieces.append(lax.ppermute(up, "fsdp", upward))
+    (mine,) = call(
+        stack_kernel, [(CHIPS * SHARE, 4 * HDT)], (place, *pieces), [SM] + [VM] * CHIPS, 0
+    )
+    other = lax.ppermute(mine, "fsdp", [(i, i ^ 1) for i in range(members)])
+    (weights,) = call(merge_kernel, [(D, 4 * HDT)], (place, mine, other), [SM, VM, VM], 0)
+    return weights
 
 
 def body(
@@ -254,21 +305,29 @@
 ):
     me = lax.axis_index("tok")
     side = (me // (SHARDS // 2)).reshape(1).astype(jnp.int32)
-    partner = [(i, i ^ (SHARDS // 2)) for i in range(SHARDS)]
-    shares = jnp.concatenate(
-        [probe_projector, lookup_projector, content_projector, result_projector.T], axis=1
-    )
-    weights = lax.all_gather(shares, "fsdp", axis=0, tiled=True)
+    column = SHARDS // 4
+    partner = [(i, (3 - i // column) * column + i % column) for i in range(SHARDS)]
+    member = lax.axis_index("fsdp").astype(jnp.int32)
+    place = jnp.stack([member // 2, member % 2])
 
     order = morton_arrangement[0]
-    keep, send = call(
+    keep, send, share = call(
         arrange_kernel,
-        [(TOK, HALF)] * 2,
-        (side, order, embedded_pieces[0]),
-        [SM, VM, VM],
+        [(TOK, HALF)] * 2 + [(SHARE, 4 * HDT)],
+        (
+            side,
+            order,
+            embedded_pieces[0],
+            probe_projector,
+            lookup_projector,
+            content_projector,
+            result_projector.T,
+        ),
+        [SM] + [VM] * 6,
         2 * TOK * TOK * D,
     )
     recv = lax.ppermute(send, "tok", partner)
+    weights = gather_weights(share, place)
 
     lists = bordering_tiles[0].reshape(SHARDS, NB, KN)
     own_blocks = jnp.arange(SHARDS * NB, dtype=jnp.int32).reshape(SHARDS, NB, 1)
@@ -288,7 +347,14 @@
         packed.reshape(SHARDS, PACK, HALF), "tok", split_axis=0, concat_axis=0, tiled=True
     ).reshape(SHARDS * PACK, HALF)
 
-    seen_all = unhidden_indicator[0].reshape(SHARDS * NB, BLOCK).astype(F32)
+    seen_all = unhidden_indicator[0].reshape(SHARDS, NB, BLOCK).astype(F32)
+    seen_all = jnp.stack(
+        [
+            seen_all[:, 0],
+            jnp.concatenate([seen_all[:, 1, HB:], seen_all[:, 1, :HB]], axis=1),
+        ],
+        axis=1,
+    ).reshape(SHARDS * NB, BLOCK)
     used = jnp.arange(SLOTS)[None, :] <= bordering_tally[0][:, None]
     used = used.reshape(SHARDS, ITEMS)
     picks = (

time: 139 us -> 153 us (1.10)
  the two profiles are of different devices: /device:TPU:40 before, /device:TPU:64 now
where the time goes in v2:
time: 153 us; the launch traced here: 152 us
  starting transfers between devices  44.7 us (29%)
  blocking collectives  44.7 us (29%)
  local copies, waits for them, and re-layouts  22.8 us (15%)
  Pallas kernels  22.1 us (14%)
  waiting for transfers between devices  13.3 us (9%)
  other arithmetic  2.84 us (2%)
    all_to_all x1, blocking collectives, body(): lax.all_to_all(leaving.reshape(SHARDS, PACK, HALF), 'tok', split_axis=0,...  44.7 us
    pallas_call x8, Pallas kernels, call(): pl.pallas_call(kernel, out_shape=outs, in_specs=specs, out_specs=[VM] * l...  22.1 us
    unnamed x66, local copies, waits for them, and re-layouts  21.9 us
    ppermute x3, starting transfers between devices, gather_weights(): down = lax.ppermute(down, 'fsdp', downward)  14 us
    all_to_all x1, starting transfers between devices, body(): lax.all_to_all(packed.reshape(SHARDS, PACK, HALF), 'tok', split_axis=0, c...  11.5 us
    ppermute x2, starting transfers between devices, body(): recv = lax.ppermute(send, 'tok', partner)  7.82 us
    ppermute x3, starting transfers between devices, gather_weights(): up = lax.ppermute(up, 'fsdp', upward)  7.42 us
    ppermute x1, waiting for transfers between devices, gather_weights(): pieces.append(lax.ppermute(up, 'fsdp', upward))  5.62 us
  transfers between devices with their start and end apart: 11, of which 5 were waited for; matrix products, arithmetic and copies ran while one was open for 3% of the time, Pallas kernels for 4%

profile of v2, /device:TPU:64, one launch (start us, length us, event | category | flops | bytes accessed | tf_op | source)
XLA Modules:
  0.0 151.5 jit_solution(2334122076003472666)
XLA Ops:
  5.9 3.5 %collective-permute-start.1 = (bf16[64,2048]{1,0:T(8,128)(2,1)S(1)}, bf16[64,2048]{1,0:T(8,128)(2,1)S(1)}, u32[]{:S(2)}, u32[]{:S(2)}) collective-permute-start(bf16[64,2048]{1,0:T(8,128)(2,1)S(1)} %get-tuple-element.12.refs_0_), channel_id=1, source_target_pairs={{0,64},{32,96},{64,128},{96,160},{128,192},{160,224},{192,256},{22... | collective-permute-start | bytes 786440 | tf_op jit(solution)/shard_map/ppermute | solution.py:280
  9.4 3.8 %collective-permute-start.2 = (bf16[64,2048]{1,0:T(8,128)(2,1)S(1)}, bf16[64,2048]{1,0:T(8,128)(2,1)S(1)}, u32[]{:S(2)}, u32[]{:S(2)}) collective-permute-start(bf16[64,2048]{1,0:T(8,128)(2,1)S(1)} %get-tuple-element.12.refs_0_), channel_id=1, source_target_pairs={{0,448},{32,480},{64,0},{96,32},{128,64},{160,96},{192,128},{224,1... | collective-permute-start | bytes 786440 | tf_op jit(solution)/shard_map/ppermute | solution.py:281
  13.2 4.7 %collective-permute-start = (bf16[128,512]{1,0:T(8,128)(2,1)S(1)}, bf16[128,512]{1,0:T(8,128)(2,1)S(1)}, u32[]{:S(2)}, u32[]{:S(2)}) collective-permute-start(bf16[128,512]{1,0:T(8,128)(2,1)S(1)} %get-tuple-element.11), channel_id=1, source_target_pairs={{0,24},{1,25},{2,26},{3,27},{4,28},{5,29},{6,30},{7,31},{8,16},{9,... | collective-permute-start | bytes 393224 | tf_op jit(solution)/shard_map/ppermute | solution.py:329
  18.7 2.0 %collective-permute-start.3 = (bf16[64,2048]{1,0:T(8,128)(2,1)S(1)}, bf16[64,2048]{1,0:T(8,128)(2,1)S(1)}, u32[]{:S(2)}, u32[]{:S(2)}) collective-permute-start(bf16[64,2048]{1,0:T(8,128)(2,1)S(1)} %collective-permute-done.1.refs_1_), channel_id=1, source_target_pairs={{0,64},{32,96},{64,128},{96,160},{128,192},{160,224},{192,256},{22... | collective-permute-start | bytes 786440 | tf_op jit(solution)/shard_map/ppermute | solution.py:280
  21.1 5.0 %collective-permute-start.4 = (bf16[64,2048]{1,0:T(8,128)(2,1)S(1)}, bf16[64,2048]{1,0:T(8,128)(2,1)S(1)}, u32[]{:S(2)}, u32[]{:S(2)}) collective-permute-start(bf16[64,2048]{1,0:T(8,128)(2,1)S(1)} %collective-permute-done.2.refs_2_), channel_id=1, source_target_pairs={{0,448},{32,480},{64,0},{96,32},{128,64},{160,96},{192,128},{224,1... | collective-permute-start | bytes 786440 | tf_op jit(solution)/shard_map/ppermute | solution.py:281
  26.1 3.2 %collective-permute-done.3.refs_3_ = bf16[64,2048]{1,0:T(8,128)(2,1)S(1)} collective-permute-done((bf16[64,2048]{1,0:T(8,128)(2,1)S(1)}, bf16[64,2048]{1,0:T(8,128)(2,1)S(1)}, u32[]{:S(2)}, u32[]{:S(2)}) %collective-permute-start.3) | collective-permute-done | bytes 262176 | tf_op jit(solution)/shard_map/ppermute | solution.py:280
  29.3 1.9 %collective-permute-start.5 = (bf16[64,2048]{1,0:T(8,128)(2,1)S(1)}, bf16[64,2048]{1,0:T(8,128)(2,1)S(1)}, u32[]{:S(2)}, u32[]{:S(2)}) collective-permute-start(bf16[64,2048]{1,0:T(8,128)(2,1)S(1)} %collective-permute-done.3.refs_3_), channel_id=1, source_target_pairs={{0,64},{32,96},{64,128},{96,160},{128,192},{160,224},{192,256},{22... | collective-permute-start | bytes 786440 | tf_op jit(solution)/shard_map/ppermute | solution.py:280
  31.5 1.6 %shard_map.132 = bf16[1280,512]{1,0:T(8,128)(2,1)} custom-call(s32[1]{0:T(128)} %bitcast.side_ref, s32[1,1280]{1,0:T(1,128)S(1)} %add.139.target_ref, bf16[128,512]{1,0:T(8,128)(2,1)S(1)} %get-tuple-element.10.keep_ref, bf16[128,512]{1,0:T(8,128)(2,1)S(1)} %collective-permute-done.recv_ref), custom_call_target="tpu_custom_call" | custom-call | flops 335544320 | bytes 1577988 | tf_op jit(solution)/shard_map/pallas_call | solution.py:263
  33.2 11.5 %all-to-all-start = ((bf16[32,40,512]{2,1,0:T(8,128)(2,1)}), bf16[32,40,512]{2,1,0:T(8,128)(2,1)S(1)}, u32[]{:S(2)}, u32[]{:S(2)}) async-start(bf16[32,40,512]{2,1,0:T(8,128)(2,1)} %bitcast.5), calls=%async_computation | async-start | bytes 2621440 | tf_op jit(solution)/shard_map/all_to_all | solution.py:346
  44.6 5.1 %collective-permute-start.6 = (bf16[64,2048]{1,0:T(8,128)(2,1)S(1)}, bf16[64,2048]{1,0:T(8,128)(2,1)S(1)}, u32[]{:S(2)}, u32[]{:S(2)}) collective-permute-start(bf16[64,2048]{1,0:T(8,128)(2,1)S(1)} %collective-permute-done.4.refs_4_), channel_id=1, source_target_pairs={{0,448},{32,480},{64,0},{96,32},{128,64},{160,96},{192,128},{224,1... | collective-permute-start | bytes 786440 | tf_op jit(solution)/shard_map/ppermute | solution.py:281
  50.5 1.9 %collective-permute-start.7 = (bf16[64,2048]{1,0:T(8,128)(2,1)S(1)}, bf16[64,2048]{1,0:T(8,128)(2,1)S(1)}, u32[]{:S(2)}, u32[]{:S(2)}) collective-permute-start(bf16[64,2048]{1,0:T(8,128)(2,1)S(1)} %collective-permute-done.5.refs_5_), channel_id=1, source_target_pairs={{0,64},{32,96},{64,128},{96,160},{128,192},{160,224},{192,256},{22... | collective-permute-start | bytes 786440 | tf_op jit(solution)/shard_map/ppermute | solution.py:283
  54.3 5.6 %collective-permute-done.7.refs_7_ = bf16[64,2048]{1,0:T(8,128)(2,1)S(1)} collective-permute-done((bf16[64,2048]{1,0:T(8,128)(2,1)S(1)}, bf16[64,2048]{1,0:T(8,128)(2,1)S(1)}, u32[]{:S(2)}, u32[]{:S(2)}) %collective-permute-start.7) | collective-permute-done | bytes 262176 | tf_op jit(solution)/shard_map/ppermute | solution.py:283
  60.7 0.9 copy-done.5
  69.0 2.1 %collective-permute-start.8 = (bf16[512,2048]{1,0:T(8,128)(2,1)S(1)}, bf16[512,2048]{1,0:T(8,128)(2,1)}, u32[]{:S(2)}, u32[]{:S(2)}) collective-permute-start(bf16[512,2048]{1,0:T(8,128)(2,1)S(1)} %shard_map.133.mine_ref), channel_id=1, source_target_pairs={{0,32},{32,0},{64,96},{96,64},{128,160},{160,128},{192,224},{224,1... | collective-permute-start | bytes 6291464 | tf_op jit(solution)/shard_map/ppermute | solution.py:287
  73.5 1.4 fusion.1
  75.2 1.9 %shard_map.134.w_ref = bf16[1024,2048]{1,0:T(8,128)(2,1)S(1)} custom-call(s32[2]{0:T(128)S(1)} %pad_add_fusion.1.place_ref, bf16[512,2048]{1,0:T(8,128)(2,1)S(1)} %shard_map.133.mine_ref, bf16[512,2048]{1,0:T(8,128)(2,1)} %collective-permute-done.8.other_ref), custom_call_target="tpu_custom_call" | custom-call | bytes 8388616 | tf_op jit(solution)/shard_map/pallas_call | solution.py:263
  77.1 2.0 %copy-done = bf16[1024,2048]{1,0:T(8,128)(2,1)} copy-done((bf16[1024,2048]{1,0:T(8,128)(2,1)}, bf16[1024,2048]{1,0:T(8,128)(2,1)S(1)}, u32[]{:S(2)}) %copy-start) | copy-done | bytes 4194328
  79.0 1.1 copy-done.2
  80.2 1.1 copy-done.3
  82.3 15.0 %shard_map.135 = (bf16[1280,512]{1,0:T(8,128)(2,1)S(1)}, bf16[128,512]{1,0:T(8,128)(2,1)S(1)}, bf16[128,1024]{1,0:T(8,128)(2,1)S(1)}) custom-call(f32[8]{0:T(128)S(1)} %copy-done.28, bf16[1280,512]{1,0:T(8,128)(2,1)S(1)} %bitcast.31, bf16[640,640]{1,0:T(8,128)(2,1)S(1)} %copy-done.3, bf16[640,640]{1,0:T(8,128)(2,1)S(1)} %copy-done.2, ...), custom_call_target="tpu_custom_call" | custom-call | flops 4000000000 | bytes 9114144 | tf_op jit(solution)/shard_map/pallas_call | solution.py:263
  97.3 44.7 %all_to_all.10 = bf16[32,40,512]{2,1,0:T(8,128)(2,1)S(1)} all-to-all(bf16[32,40,512]{2,1,0:T(8,128)(2,1)S(1)} %bitcast.32), channel_id=1, replica_groups=mesh['fsdp'=16,'tok'=32] {'tok'}, dimensions={0} | all-to-all | bytes 2621440 | tf_op jit(solution)/shard_map/all_to_all | solution.py:397
  142.5 3.2 %collective-permute-start.9 = (bf16[128,512]{1,0:T(8,128)(2,1)S(1)}, bf16[128,512]{1,0:T(8,128)(2,1)S(1)}, u32[]{:S(2)}, u32[]{:S(2)}) collective-permute-start(bf16[128,512]{1,0:T(8,128)(2,1)S(1)} %get-tuple-element.17), channel_id=1, source_target_pairs={{0,24},{1,25},{2,26},{3,27},{4,28},{5,29},{6,30},{7,31},{8,16},{9,... | collective-permute-start | bytes 393224 | tf_op jit(solution)/shard_map/ppermute | solution.py:414
  145.7 1.2 shard_map.136
  146.9 3.7 %collective-permute-done.9.recv_ref = bf16[128,512]{1,0:T(8,128)(2,1)S(1)} collective-permute-done((bf16[128,512]{1,0:T(8,128)(2,1)S(1)}, bf16[128,512]{1,0:T(8,128)(2,1)S(1)}, u32[]{:S(2)}, u32[]{:S(2)}) %collective-permute-start.9) | collective-permute-done | bytes 131104 | tf_op jit(solution)/shard_map/ppermute | solution.py:414
  (103 shorter events, 22.3 us)
Async XLA Ops:
  5.9 27.3 %copy-start.4 = (bf16[64,2048]{1,0:T(8,128)(2,1)}, bf16[64,2048]{1,0:T(8,128)(2,1)S(1)}, u32[]{:S(2)}) copy-start(bf16[64,2048]{1,0:T(8,128)(2,1)S(1)} %get-tuple-element.12.refs_0_) | copy-start | bytes 786436
  5.9 12.8 %collective-permute-start.1 = (bf16[64,2048]{1,0:T(8,128)(2,1)S(1)}, bf16[64,2048]{1,0:T(8,128)(2,1)S(1)}, u32[]{:S(2)}, u32[]{:S(2)}) collective-permute-start(bf16[64,2048]{1,0:T(8,128)(2,1)S(1)} %get-tuple-element.12.refs_0_), channel_id=1, source_target_pairs={{0,64},{32,96},{64,128},{96,160},{128,192},{160,224},{192,256},{22... | collective-permute-start | bytes 786440 | tf_op jit(solution)/shard_map/ppermute | solution.py:280
  9.4 11.7 %collective-permute-start.2 = (bf16[64,2048]{1,0:T(8,128)(2,1)S(1)}, bf16[64,2048]{1,0:T(8,128)(2,1)S(1)}, u32[]{:S(2)}, u32[]{:S(2)}) collective-permute-start(bf16[64,2048]{1,0:T(8,128)(2,1)S(1)} %get-tuple-element.12.refs_0_), channel_id=1, source_target_pairs={{0,448},{32,480},{64,0},{96,32},{128,64},{160,96},{192,128},{224,1... | collective-permute-start | bytes 786440 | tf_op jit(solution)/shard_map/ppermute | solution.py:281
  13.2 18.3 %collective-permute-start = (bf16[128,512]{1,0:T(8,128)(2,1)S(1)}, bf16[128,512]{1,0:T(8,128)(2,1)S(1)}, u32[]{:S(2)}, u32[]{:S(2)}) collective-permute-start(bf16[128,512]{1,0:T(8,128)(2,1)S(1)} %get-tuple-element.11), channel_id=1, source_target_pairs={{0,24},{1,25},{2,26},{3,27},{4,28},{5,29},{6,30},{7,31},{8,16},{9,... | collective-permute-start | bytes 393224 | tf_op jit(solution)/shard_map/ppermute | solution.py:329
  18.7 14.5 %copy-start.6 = (bf16[64,2048]{1,0:T(8,128)(2,1)}, bf16[64,2048]{1,0:T(8,128)(2,1)S(1)}, u32[]{:S(2)}) copy-start(bf16[64,2048]{1,0:T(8,128)(2,1)S(1)} %collective-permute-done.1.refs_1_) | copy-start | bytes 786436
  18.7 10.6 %collective-permute-start.3 = (bf16[64,2048]{1,0:T(8,128)(2,1)S(1)}, bf16[64,2048]{1,0:T(8,128)(2,1)S(1)}, u32[]{:S(2)}, u32[]{:S(2)}) collective-permute-start(bf16[64,2048]{1,0:T(8,128)(2,1)S(1)} %collective-permute-done.1.refs_1_), channel_id=1, source_target_pairs={{0,64},{32,96},{64,128},{96,160},{128,192},{160,224},{192,256},{22... | collective-permute-start | bytes 786440 | tf_op jit(solution)/shard_map/ppermute | solution.py:280
  21.1 12.1 %copy-start.8 = (bf16[64,2048]{1,0:T(8,128)(2,1)}, bf16[64,2048]{1,0:T(8,128)(2,1)S(1)}, u32[]{:S(2)}) copy-start(bf16[64,2048]{1,0:T(8,128)(2,1)S(1)} %collective-permute-done.2.refs_2_) | copy-start | bytes 786436
  21.1 23.6 %collective-permute-start.4 = (bf16[64,2048]{1,0:T(8,128)(2,1)S(1)}, bf16[64,2048]{1,0:T(8,128)(2,1)S(1)}, u32[]{:S(2)}, u32[]{:S(2)}) collective-permute-start(bf16[64,2048]{1,0:T(8,128)(2,1)S(1)} %collective-permute-done.2.refs_2_), channel_id=1, source_target_pairs={{0,448},{32,480},{64,0},{96,32},{128,64},{160,96},{192,128},{224,1... | collective-permute-start | bytes 786440 | tf_op jit(solution)/shard_map/ppermute | solution.py:281
  29.3 3.9 %copy-start.10 = (bf16[64,2048]{1,0:T(8,128)(2,1)}, bf16[64,2048]{1,0:T(8,128)(2,1)S(1)}, u32[]{:S(2)}) copy-start(bf16[64,2048]{1,0:T(8,128)(2,1)S(1)} %collective-permute-done.3.refs_3_) | copy-start | bytes 786436
  29.3 21.2 %collective-permute-start.5 = (bf16[64,2048]{1,0:T(8,128)(2,1)S(1)}, bf16[64,2048]{1,0:T(8,128)(2,1)S(1)}, u32[]{:S(2)}, u32[]{:S(2)}) collective-permute-start(bf16[64,2048]{1,0:T(8,128)(2,1)S(1)} %collective-permute-done.3.refs_3_), channel_id=1, source_target_pairs={{0,64},{32,96},{64,128},{96,160},{128,192},{160,224},{192,256},{22... | collective-permute-start | bytes 786440 | tf_op jit(solution)/shard_map/ppermute | solution.py:280
  33.2 45.9 %all-to-all-start = ((bf16[32,40,512]{2,1,0:T(8,128)(2,1)}), bf16[32,40,512]{2,1,0:T(8,128)(2,1)S(1)}, u32[]{:S(2)}, u32[]{:S(2)}) async-start(bf16[32,40,512]{2,1,0:T(8,128)(2,1)} %bitcast.5), calls=%async_computation | async-start | bytes 2621440 | tf_op jit(solution)/shard_map/all_to_all | solution.py:346
  44.6 9.0 %collective-permute-start.6 = (bf16[64,2048]{1,0:T(8,128)(2,1)S(1)}, bf16[64,2048]{1,0:T(8,128)(2,1)S(1)}, u32[]{:S(2)}, u32[]{:S(2)}) collective-permute-start(bf16[64,2048]{1,0:T(8,128)(2,1)S(1)} %collective-permute-done.4.refs_4_), channel_id=1, source_target_pairs={{0,448},{32,480},{64,0},{96,32},{128,64},{160,96},{192,128},{224,1... | collective-permute-start | bytes 786440 | tf_op jit(solution)/shard_map/ppermute | solution.py:281
  50.5 9.5 %collective-permute-start.7 = (bf16[64,2048]{1,0:T(8,128)(2,1)S(1)}, bf16[64,2048]{1,0:T(8,128)(2,1)S(1)}, u32[]{:S(2)}, u32[]{:S(2)}) collective-permute-start(bf16[64,2048]{1,0:T(8,128)(2,1)S(1)} %collective-permute-done.5.refs_5_), channel_id=1, source_target_pairs={{0,64},{32,96},{64,128},{96,160},{128,192},{160,224},{192,256},{22... | collective-permute-start | bytes 786440 | tf_op jit(solution)/shard_map/ppermute | solution.py:283
  53.1 18.5 %copy-start.31 = (s32[1,64]{1,0:T(1,128)S(1)}, s32[1,64]{1,0:T(1,128)}, u32[]{:S(2)}) copy-start(s32[1,64]{1,0:T(1,128)} %param.16) | copy-start | bytes 772
  68.3 4.3 %copy-start.29 = (s32[1,4096]{1,0:T(1,128)S(1)}, s32[1,4096]{1,0:T(1,128)}, u32[]{:S(2)}) copy-start(s32[1,4096]{1,0:T(1,128)} %param.14) | copy-start | bytes 49156
  68.3 5.1 %copy-start.30 = (bf16[1024]{0:T(1024)(128)(2,1)S(1)}, bf16[1024]{0:T(1024)(128)(2,1)}, u32[]{:S(2)}) copy-start(bf16[1024]{0:T(1024)(128)(2,1)} %param.17) | copy-start | bytes 6148
  69.0 6.2 %collective-permute-start.8 = (bf16[512,2048]{1,0:T(8,128)(2,1)S(1)}, bf16[512,2048]{1,0:T(8,128)(2,1)}, u32[]{:S(2)}, u32[]{:S(2)}) collective-permute-start(bf16[512,2048]{1,0:T(8,128)(2,1)S(1)} %shard_map.133.mine_ref), channel_id=1, source_target_pairs={{0,32},{32,0},{64,96},{96,64},{128,160},{160,128},{192,224},{224,1... | collective-permute-start | bytes 6291464 | tf_op jit(solution)/shard_map/ppermute | solution.py:287
  74.9 4.2 %copy-start.28 = (f32[8]{0:T(128)S(1)}, f32[8]{0:T(128)}, u32[]{:S(2)}) copy-start(f32[8]{0:T(128)} %sharp_ref.1) | copy-start | bytes 100
  77.1 2.0 %copy-start = (bf16[1024,2048]{1,0:T(8,128)(2,1)}, bf16[1024,2048]{1,0:T(8,128)(2,1)S(1)}, u32[]{:S(2)}) copy-start(bf16[1024,2048]{1,0:T(8,128)(2,1)S(1)} %shard_map.134.w_ref) | copy-start | bytes 12582916
  79.0 1.1 copy-start.2
  80.2 1.1 copy-start.3
  82.3 63.4 %copy-start.1 = (bf16[1024,2048]{1,0:T(8,128)(2,1)S(1)}, bf16[1024,2048]{1,0:T(8,128)(2,1)}, u32[]{:S(2)}) copy-start(bf16[1024,2048]{1,0:T(8,128)(2,1)} %copy-done) | copy-start | bytes 12582916
  142.5 8.1 %collective-permute-start.9 = (bf16[128,512]{1,0:T(8,128)(2,1)S(1)}, bf16[128,512]{1,0:T(8,128)(2,1)S(1)}, u32[]{:S(2)}, u32[]{:S(2)}) collective-permute-start(bf16[128,512]{1,0:T(8,128)(2,1)S(1)} %get-tuple-element.17), channel_id=1, source_target_pairs={{0,24},{1,25},{2,26},{3,27},{4,28},{5,29},{6,30},{7,31},{8,16},{9,... | collective-permute-start | bytes 393224 | tf_op jit(solution)/shard_map/ppermute | solution.py:414
  145.7 4.9 %copy-start.26 = (s32[1,1,128]{2,1,0:T(1,128)S(1)}, s32[1,1,128]{2,1,0:T(1,128)}, u32[]{:S(2)}) copy-start(s32[1,1,128]{2,1,0:T(1,128)} %param.13) | copy-start | bytes 1540
  (19 other events, 16.3 us)

commit v3 on v2

--- a/solution.py
+++ b/solution.py
@@ -27,9 +27,7 @@
 GL = GROUP * HEAD_DIM
 GR = GROUP * BLOCK
 
-CHIPS = 8
 SHARE = 64
-STEPS = (0, 1, -1, 2, -2, 3, -3, 4)
 
 norm_eps = 1e-05
 head_eps = 1e-06
@@ -37,6 +35,7 @@
 BF16 = jnp.bfloat16
 VM = pl.BlockSpec(memory_space=pltpu.VMEM)
 SM = pl.BlockSpec(memory_space=pltpu.SMEM)
+HB_SPEC = pl.BlockSpec(memory_space=pltpu.HBM)
 NN = (((1,), (0,)), ((), ()))
 NT = (((1,), (1,)), ((), ()))
 TN = (((0,), (0,)), ((), ()))
@@ -57,31 +56,36 @@
 
 
 def arrange_kernel(
-    side_ref, order_ref, x_ref, wq_ref, wk_ref, wv_ref, wo_ref, keep_ref, send_ref, share_ref
+    side_ref,
+    order_hbm,
+    x_hbm,
+    wq_hbm,
+    wk_hbm,
+    wv_hbm,
+    wo_hbm,
+    keep_ref,
+    send_ref,
+    share_ref,
+    order_ref,
+    x_ref,
+    sems,
 ):
-    for n, part in enumerate((wq_ref, wk_ref, wv_ref, wo_ref)):
-        share_ref[:, n * HDT : (n + 1) * HDT] = part[...]
+    copies = [
+        pltpu.make_async_copy(x_hbm, x_ref, sems.at[0]),
+        pltpu.make_async_copy(order_hbm, order_ref, sems.at[1]),
+    ]
+    for n, part in enumerate((wq_hbm, wk_hbm, wv_hbm, wo_hbm)):
+        lanes = pl.ds(n * HDT, HDT)
+        copies.append(pltpu.make_async_copy(part, share_ref.at[:, lanes], sems.at[2 + n]))
+    for copy in copies:
+        copy.start()
+    for copy in copies:
+        copy.wait()
     a = dot(one_hot(order_ref, TOK), x_ref[...], TN).astype(BF16)
     lower = side_ref[0] == 0
     left, right = a[:, :HALF], a[:, HALF:]
     keep_ref[...] = jnp.where(lower, left, right)
     send_ref[...] = jnp.where(lower, right, left)
-
-
-def stack_kernel(place_ref, *refs):
-    out_ref = refs[-1]
-    for step, ref in zip(STEPS, refs[:-1]):
-        place = lax.rem(place_ref[0] + (CHIPS - step), CHIPS)
-        out_ref[pl.ds(place * SHARE, SHARE), :] = ref[...]
-
-
-def merge_kernel(place_ref, mine_ref, other_ref, out_ref):
-    first = place_ref[1] == 0
-    for y in range(CHIPS):
-        rows = slice(y * SHARE, (y + 1) * SHARE)
-        mine, other = mine_ref[rows, :], other_ref[rows, :]
-        out_ref[2 * y * SHARE : (2 * y + 1) * SHARE, :] = jnp.where(first, mine, other)
-        out_ref[(2 * y + 1) * SHARE : (2 * y + 2) * SHARE, :] = jnp.where(first, other, mine)
 
 
 def pack_kernel(side_ref, target_ref, keep_ref, recv_ref, out_ref):
@@ -110,31 +114,51 @@
     out_ref[...] = dot(one_hot(order_ref, TOK), both, NN).astype(BF16)
 
 
+def source(dest):
+    return (dest % BLOCK // CHUNK) * PACK + (dest // BLOCK) * CHUNK + dest % CHUNK
+
+
 def main_kernel(
     sharp_ref,
     in_ref,
-    perm_ref,
-    back_ref,
-    w_ref,
-    up_ref,
+    w_hbm,
+    up_hbm,
     gain_ref,
     seen_ref,
     out_ref,
     att_ref,
     own_ref,
+    wo_ref,
+    w_ref,
+    up_ref,
+    sems,
     normed_ref,
     rstd_ref,
     xn_ref,
+    back_ref,
     k_ref,
     v_ref,
     gkv_ref,
     gq_ref,
     gh_ref,
 ):
+    copies = [
+        pltpu.make_async_copy(w_hbm.at[:, pl.ds(0, 3 * HDT)], w_ref, sems.at[0]),
+        pltpu.make_async_copy(w_hbm.at[:, pl.ds(3 * HDT, HDT)], wo_ref, sems.at[1]),
+        pltpu.make_async_copy(up_hbm, up_ref, sems.at[2]),
+    ]
+    for copy in copies:
+        copy.start()
+    shape = (ROWS, ROWS)
+    row = source(lax.broadcasted_iota(jnp.int32, (ROWS, 1), 0))
+    perm = row == lax.broadcasted_iota(jnp.int32, shape, 1)
+    column = source(lax.broadcasted_iota(jnp.int32, (1, ROWS), 1))
+    back = column == lax.broadcasted_iota(jnp.int32, shape, 0)
+    back_ref[...] = jnp.where(back, 1.0, 0.0).astype(BF16)
     x_in = jnp.concatenate(
         [in_ref[:ROWS], jnp.concatenate([in_ref[FAR:], in_ref[ROWS:FAR]], axis=0)], axis=1
     )
-    normed_ref[...] = dot(perm_ref[...], x_in, NN)
+    normed_ref[...] = dot(jnp.where(perm, 1.0, 0.0).astype(BF16), x_in, NN)
     gain = gain_ref[...].astype(F32)
     for t in range(ITEMS):
         rows = pl.ds(t * BLOCK, BLOCK)
@@ -147,13 +171,15 @@
         normed_ref[rows, :] = normed
         rstd_ref[rows, :] = jnp.broadcast_to(rstd, (BLOCK, 128))
         xn_ref[rows, :] = (normed * gain).astype(BF16)
+    for copy in copies:
+        copy.wait()
     xn = xn_ref[...]
     k_ref[...] = dot(xn, w_ref[:, HDT : 2 * HDT], NN).astype(BF16)
     v_ref[...] = dot(xn, w_ref[:, 2 * HDT : 3 * HDT], NN).astype(BF16)
     xn_own = jnp.concatenate([xn_ref[pl.ds(b * KEYS, BLOCK), :] for b in range(NB)], axis=0)
     queries = dot(xn_own, w_ref[:, :HDT], NN).astype(BF16)
     up = rolled(up_ref[...])
-    grad_attn = dot(up, w_ref[:, 3 * HDT :], NN).astype(BF16)
+    grad_attn = dot(up, wo_ref[...], NN).astype(BF16)
 
     lane_head = lax.broadcasted_iota(jnp.int32, (BLOCK, GL), 1) // HEAD_DIM
     head_pick = (
@@ -252,41 +278,30 @@
     out_ref[ROWS:FAR] = back[ROWS // 2 :, HALF:]
 
 
-def output_kernel(att_ref, own_ref, w_ref, out_ref):
-    out = own_ref[...].astype(F32) + dot(att_ref[...], w_ref[:, 3 * HDT :], NT)
+def output_kernel(att_ref, own_ref, wo_ref, out_ref):
+    out = own_ref[...].astype(F32) + dot(att_ref[...], wo_ref[...], NT)
     out_ref[...] = rolled(out.astype(BF16))
 
 
-def call(kernel, outs, args, specs, flops, scratch=(), limit=16):
-    outs = [jax.ShapeDtypeStruct(shape, BF16) for shape in outs]
-    moved = sum(a.size * a.dtype.itemsize for a in list(args) + outs)
+def call(kernel, outs, args, specs, flops, scratch=(), limit=8, out_spec=VM):
+    place = pltpu.HBM if out_spec is HB_SPEC else jax.ShapeDtypeStruct
+    moved = sum(a.size * a.dtype.itemsize for a in args)
+    moved += sum(2 * o[0] * o[1] for o in outs)
+    if flops == 0:
+        moved = 0
+    args = [
+        pltpu.with_memory_space_constraint(a, pltpu.HBM) if spec is HB_SPEC else a
+        for a, spec in zip(args, specs)
+    ]
     return pl.pallas_call(
         kernel,
-        out_shape=outs,
+        out_shape=[place(o[:2], o[2] if len(o) > 2 else BF16) for o in outs],
         in_specs=specs,
-        out_specs=[VM] * len(outs),
+        out_specs=[out_spec] * len(outs),
         scratch_shapes=list(scratch),
         compiler_params=pltpu.CompilerParams(vmem_limit_bytes=limit * 2**20),
         cost_estimate=pl.CostEstimate(flops=flops, bytes_accessed=moved, transcendentals=0),
     )(*args)
-
-
-def gather_weights(share, place):
-    members = 2 * CHIPS
-    upward = [(i, (i + 2) % members) for i in range(members)]
-    downward = [(i, (i - 2) % members) for i in range(members)]
-    pieces, up, down = [share], share, share
-    for _ in range(CHIPS // 2 - 1):
-        up = lax.ppermute(up, "fsdp", upward)
-        down = lax.ppermute(down, "fsdp", downward)
-        pieces += [up, down]
-    pieces.append(lax.ppermute(up, "fsdp", upward))
-    (mine,) = call(
-        stack_kernel, [(CHIPS * SHARE, 4 * HDT)], (place, *pieces), [SM] + [VM] * CHIPS, 0
-    )
-    other = lax.ppermute(mine, "fsdp", [(i, i ^ 1) for i in range(members)])
-    (weights,) = call(merge_kernel, [(D, 4 * HDT)], (place, mine, other), [SM, VM, VM], 0)
-    return weights
 
 
 def body(
@@ -307,8 +322,6 @@
     side = (me // (SHARDS // 2)).reshape(1).astype(jnp.int32)
     column = SHARDS // 4
     partner = [(i, (3 - i // column) * column + i % column) for i in range(SHARDS)]
-    member = lax.axis_index("fsdp").astype(jnp.int32)
-    place = jnp.stack([member // 2, member % 2])
 
     order = morton_arrangement[0]
     keep, send, share = call(
@@ -323,11 +336,16 @@
             content_projector,
             result_projector.T,
         ),
-        [SM] + [VM] * 6,
+        [SM] + [HB_SPEC] * 6,
         2 * TOK * TOK * D,
-    )
+        scratch=[
+            pltpu.VMEM((1, TOK), jnp.int32),
+            pltpu.VMEM((TOK, D), BF16),
+            pltpu.SemaphoreType.DMA((6,)),
+        ],
+    )
+    weights = lax.all_gather(share, "fsdp", axis=0, tiled=True)
     recv = lax.ppermute(send, "tok", partner)
-    weights = gather_weights(share, place)
 
     lists = bordering_tiles[0].reshape(SHARDS, NB, KN)
     own_blocks = jnp.arange(SHARDS * NB, dtype=jnp.int32).reshape(SHARDS, NB, 1)
@@ -363,36 +381,34 @@
     picks = jnp.sum(picks * (jnp.arange(SHARDS) == me)[:, None, None], axis=0)
     seen = jnp.dot(picks, seen_all).reshape(NB, KEYS)
 
-    dest = jnp.arange(ROWS)
-    source = (dest % BLOCK // CHUNK) * PACK + (dest // BLOCK) * CHUNK + dest % CHUNK
-    perm = (source[:, None] == jnp.arange(ROWS)[None, :]).astype(BF16)
-    back = (source[None, :] == jnp.arange(ROWS)[:, None]).astype(BF16)
-    leaving, attended, own = call(
+    leaving, attended, own, out_weight = call(
         main_kernel,
-        [(SHARDS * PACK, HALF), (TOK, HDT), (TOK, D)],
+        [(SHARDS * PACK, HALF), (TOK, HDT), (TOK, D), (D, HDT)],
         (
             sharpness_coefficient,
             arrived,
-            perm,
-            back,
             weights,
             upstream_derivative[0],
             standardizer_multiplier.reshape(1, D),
             seen,
         ),
-        [SM] + [VM] * 7,
+        [SM, VM, HB_SPEC, HB_SPEC, VM, VM],
         4 * 10**9,
         scratch=[
+            pltpu.VMEM((D, 3 * HDT), BF16),
+            pltpu.VMEM((TOK, D), BF16),
+            pltpu.SemaphoreType.DMA((3,)),
             pltpu.VMEM((ROWS, D), F32),
             pltpu.VMEM((ROWS, 128), F32),
             pltpu.VMEM((ROWS, D), BF16),
+            pltpu.VMEM((ROWS, ROWS), BF16),
             pltpu.VMEM((ROWS, HDT), BF16),
             pltpu.VMEM((ROWS, HDT), BF16),
             pltpu.VMEM((ROWS, D), BF16),
             pltpu.VMEM((TOK, HDT), BF16),
             pltpu.VMEM((ROWS, D), F32),
         ],
-        limit=48,
+        limit=40,
     )
     returned = lax.all_to_all(
         leaving.reshape(SHARDS, PACK, HALF), "tok", split_axis=0, concat_axis=0, tiled=True
@@ -400,7 +416,7 @@
     (layer_out,) = call(
         output_kernel,
         [(TOK, D)],
-        (attended, own, weights),
+        (attended, own, out_weight),
         [VM] * 3,
         2 * TOK * HDT * D,
     )

time: 153 us -> 137 us (0.90)
  the two profiles are of different devices: /device:TPU:64 before, /device:TPU:8 now
where the time goes in v3:
time: 137 us
  blocking collectives  39.7 us (29%)
  waiting for transfers between devices  37.2 us (27%)
  Pallas kernels  21.5 us (16%)
  starting transfers between devices  20.8 us (15%)
  between operations  14.2 us (10%)
  local copies, waits for them, and re-layouts  2.17 us (2%)
    all_to_all x1, blocking collectives, body(): lax.all_to_all(leaving.reshape(SHARDS, PACK, HALF), 'tok', split_axis=0,...  39.7 us
    all_to_all x1, waiting for transfers between devices, body(): lax.all_to_all(packed.reshape(SHARDS, PACK, HALF), 'tok', split_axis=0, c...  31 us
    pallas_call x6, Pallas kernels, call(): pl.pallas_call(kernel, out_shape=[place(o[:2], o[2] if len(o) > 2 else BF...  21.5 us
    all_to_all x1, starting transfers between devices, body(): lax.all_to_all(packed.reshape(SHARDS, PACK, HALF), 'tok', split_axis=0, c...  13 us
    ppermute x2, starting transfers between devices, body(): recv = lax.ppermute(send, 'tok', partner)  7.73 us
    ppermute x2, waiting for transfers between devices, body(): recv = lax.ppermute(send, 'tok', partner)  6.1 us
  transfers between devices with their start and end apart: 4, of which 3 were waited for; matrix products, arithmetic and copies ran while one was open for 3% of the time, Pallas kernels for 2%

profile of v3, /device:TPU:8, one launch (start us, length us, event | category | flops | bytes accessed | tf_op | source)
XLA Modules:
  0.0 137.0 jit_solution(11429435881375622596)
XLA Ops:
  7.2 1.8 %shard_map.131 = (bf16[128,512]{1,0:T(8,128)(2,1)S(1)}, bf16[128,512]{1,0:T(8,128)(2,1)S(1)}, bf16[64,2048]{1,0:T(8,128)(2,1)}) custom-call(s32[1]{0:T(128)} %bitcast.side_ref, s32[1,128]{1,0:T(1,128)} %bitcast.31, bf16[128,1024]{1,0:T(8,128)(2,1)} %bitcast.33, bf16[64,512]{1,0:T(8,128)(2,1)} %wq_hbm.1, bf16[64,512]{1,0:T(8,128)(2,1)} %wk_hbm.1, ...), custom_call_target="tpu_custom_call" | custom-call | flops 33554432 | bytes 1049092 | tf_op jit(solution)/shard_map/pallas_call | solution.py:296
  9.0 4.7 %collective-permute-start = (bf16[128,512]{1,0:T(8,128)(2,1)S(1)}, bf16[128,512]{1,0:T(8,128)(2,1)S(1)}, u32[]{:S(2)}, u32[]{:S(2)}) collective-permute-start(bf16[128,512]{1,0:T(8,128)(2,1)S(1)} %get-tuple-element.12), channel_id=1, source_target_pairs={{0,24},{1,25},{2,26},{3,27},{4,28},{5,29},{6,30},{7,31},{8,16},{9,... | collective-permute-start | bytes 393224 | tf_op jit(solution)/shard_map/ppermute | solution.py:348
  13.7 0.8 copy.33
  14.5 0.1 pad_add_fusion
  14.6 0.1 copy.34
  14.8 0.1 iota_add_fusion
  15.0 0.1 add.60.target_ref
  15.1 2.3 %collective-permute-done.recv_ref = bf16[128,512]{1,0:T(8,128)(2,1)S(1)} collective-permute-done((bf16[128,512]{1,0:T(8,128)(2,1)S(1)}, bf16[128,512]{1,0:T(8,128)(2,1)S(1)}, u32[]{:S(2)}, u32[]{:S(2)}) %collective-permute-start) | collective-permute-done | bytes 131104 | tf_op jit(solution)/shard_map/ppermute | solution.py:348
  17.4 1.6 %shard_map.132 = bf16[1280,512]{1,0:T(8,128)(2,1)} custom-call(s32[1]{0:T(128)} %bitcast.side_ref, s32[1,1280]{1,0:T(1,128)S(1)} %add.60.target_ref, bf16[128,512]{1,0:T(8,128)(2,1)S(1)} %get-tuple-element.11.keep_ref, bf16[128,512]{1,0:T(8,128)(2,1)S(1)} %collective-permute-done.recv_ref), custom_call_target="tpu_custom_call" | custom-call | flops 335544320 | bytes 1577988 | tf_op jit(solution)/shard_map/pallas_call | solution.py:296
  19.0 13.0 %all-to-all-start = ((bf16[32,40,512]{2,1,0:T(8,128)(2,1)}), bf16[32,40,512]{2,1,0:T(8,128)(2,1)S(1)}, u32[]{:S(2)}, u32[]{:S(2)}) async-start(bf16[32,40,512]{2,1,0:T(8,128)(2,1)} %bitcast.5), calls=%async_computation | async-start | bytes 2621440 | tf_op jit(solution)/shard_map/all_to_all | solution.py:364
  32.1 0.5 broadcast.102
  32.7 0.7 reduce.7
  33.3 0.1 le.28
  33.7 0.1 fusion.8
  34.0 0.2 select_reduce_fusion
  34.2 0.1 fusion.9
  34.4 31.0 %all-to-all-done = bf16[32,40,512]{2,1,0:T(8,128)(2,1)S(1)} async-done(((bf16[32,40,512]{2,1,0:T(8,128)(2,1)}), bf16[32,40,512]{2,1,0:T(8,128)(2,1)S(1)}, u32[]{:S(2)}, u32[]{:S(2)}) %all-to-all-start) | async-done | bytes 1310752 | tf_op jit(solution)/shard_map/all_to_all | solution.py:364
  65.4 15.5 %shard_map.133 = (bf16[1280,512]{1,0:T(8,128)(2,1)S(1)}, bf16[128,512]{1,0:T(8,128)(2,1)S(1)}, bf16[128,1024]{1,0:T(8,128)(2,1)S(1)}, bf16[1024,512]{1,0:T(8,128)(2,1)S(1)}) custom-call(f32[8]{0:T(128)S(1)} %copy-done.1, bf16[1280,512]{1,0:T(8,128)(2,1)S(1)} %bitcast.29, bf16[1024,2048]{1,0:T(8,128)(2,1)} %all-gather.2.cloned.1.call-done.w_hbm, ...), custom_call_target="tpu_custom_call" | custom-call | flops 4000000000 | bytes 8524320 | tf_op jit(solution)/shard_map/pallas_call | solution.py:296
  80.9 39.7 %all_to_all.10 = bf16[32,40,512]{2,1,0:T(8,128)(2,1)S(1)} all-to-all(bf16[32,40,512]{2,1,0:T(8,128)(2,1)S(1)} %bitcast.30), channel_id=1, replica_groups=mesh['fsdp'=16,'tok'=32] {'tok'}, dimensions={0} | all-to-all | bytes 2621440 | tf_op jit(solution)/shard_map/all_to_all | solution.py:413
  120.6 0.5 shard_map.135
  121.1 3.1 %collective-permute-start.1 = (bf16[128,512]{1,0:T(8,128)(2,1)S(1)}, bf16[128,512]{1,0:T(8,128)(2,1)S(1)}, u32[]{:S(2)}, u32[]{:S(2)}) collective-permute-start(bf16[128,512]{1,0:T(8,128)(2,1)S(1)} %get-tuple-element.19), channel_id=1, source_target_pairs={{0,24},{1,25},{2,26},{3,27},{4,28},{5,29},{6,30},{7,31},{8,16},{9,... | collective-permute-start | bytes 393224 | tf_op jit(solution)/shard_map/ppermute | solution.py:430
  124.2 1.2 shard_map.134
  125.4 3.8 %collective-permute-done.1.recv_ref = bf16[128,512]{1,0:T(8,128)(2,1)S(1)} collective-permute-done((bf16[128,512]{1,0:T(8,128)(2,1)S(1)}, bf16[128,512]{1,0:T(8,128)(2,1)S(1)}, u32[]{:S(2)}, u32[]{:S(2)}) %collective-permute-start.1) | collective-permute-done | bytes 131104 | tf_op jit(solution)/shard_map/ppermute | solution.py:430
  129.2 0.9 shard_map.136
  (31 shorter events, 0.8 us)
Async XLA Ops:
  7.2 58.3 %all-gather.2.cloned.1.call-start = ((), (), s32[]{:S(2)}) async-start(), calls=%async_computation.2 | async-start | bytes 4456448 | tf_op jit(solution)/shard_map/all_gather | solution.py:347
  9.0 8.3 %collective-permute-start = (bf16[128,512]{1,0:T(8,128)(2,1)S(1)}, bf16[128,512]{1,0:T(8,128)(2,1)S(1)}, u32[]{:S(2)}, u32[]{:S(2)}) collective-permute-start(bf16[128,512]{1,0:T(8,128)(2,1)S(1)} %get-tuple-element.12), channel_id=1, source_target_pairs={{0,24},{1,25},{2,26},{3,27},{4,28},{5,29},{6,30},{7,31},{8,16},{9,... | collective-permute-start | bytes 393224 | tf_op jit(solution)/shard_map/ppermute | solution.py:348
  19.0 13.2 %copy-start.3 = (bf16[1024]{0:T(1024)(128)(2,1)S(1)}, bf16[1024]{0:T(1024)(128)(2,1)}, u32[]{:S(2)}) copy-start(bf16[1024]{0:T(1024)(128)(2,1)} %param.17) | copy-start | bytes 6148
  19.0 13.7 %copy-start.4 = (s32[1,64]{1,0:T(1,128)S(1)}, s32[1,64]{1,0:T(1,128)}, u32[]{:S(2)}) copy-start(s32[1,64]{1,0:T(1,128)} %param.16) | copy-start | bytes 772
  19.0 14.5 %copy-start.2 = (s32[1,4096]{1,0:T(1,128)S(1)}, s32[1,4096]{1,0:T(1,128)}, u32[]{:S(2)}) copy-start(s32[1,4096]{1,0:T(1,128)} %param.14) | copy-start | bytes 49156
  19.0 46.5 %copy-start.1 = (f32[8]{0:T(128)S(1)}, f32[8]{0:T(128)}, u32[]{:S(2)}) copy-start(f32[8]{0:T(128)} %sharp_ref.1) | copy-start | bytes 100
  19.0 46.4 %all-to-all-start = ((bf16[32,40,512]{2,1,0:T(8,128)(2,1)}), bf16[32,40,512]{2,1,0:T(8,128)(2,1)S(1)}, u32[]{:S(2)}, u32[]{:S(2)}) async-start(bf16[32,40,512]{2,1,0:T(8,128)(2,1)} %bitcast.5), calls=%async_computation | async-start | bytes 2621440 | tf_op jit(solution)/shard_map/all_to_all | solution.py:364
  120.6 8.6 %copy-start = (s32[1,1,128]{2,1,0:T(1,128)S(1)}, s32[1,1,128]{2,1,0:T(1,128)}, u32[]{:S(2)}) copy-start(s32[1,1,128]{2,1,0:T(1,128)} %param.13) | copy-start | bytes 1540
  121.1 8.1 %collective-permute-start.1 = (bf16[128,512]{1,0:T(8,128)(2,1)S(1)}, bf16[128,512]{1,0:T(8,128)(2,1)S(1)}, u32[]{:S(2)}, u32[]{:S(2)}) collective-permute-start(bf16[128,512]{1,0:T(8,128)(2,1)S(1)} %get-tuple-element.19), channel_id=1, source_target_pairs={{0,24},{1,25},{2,26},{3,27},{4,28},{5,29},{6,30},{7,31},{8,16},{9,... | collective-permute-start | bytes 393224 | tf_op jit(solution)/shard_map/ppermute | solution.py:430
Sparse Core Ops, SparseCore 0:
  10.7 48.9 all-gather.1

commit v4 on v3

--- a/solution.py
+++ b/solution.py
@@ -21,6 +21,8 @@
 ROWS = ITEMS * BLOCK
 KEYS = SLOTS * BLOCK
 HALF = D // 2
+QB = BLOCK // 4
+QROWS = ROWS // 4
 FAR = ROWS + ROWS // 2
 PACK = ITEMS * CHUNK
 GROUP = 4
@@ -47,6 +49,15 @@
 
 def rolled(m):
     return jnp.concatenate([m[:BLOCK], m[BLOCK + HB :], m[BLOCK : BLOCK + HB]], axis=0)
+
+
+def split_dot(a, b, dims, which):
+    exact = a if which == 0 else b
+    high = exact.astype(BF16)
+    low = (exact - high.astype(F32)).astype(BF16)
+    if which == 0:
+        return dot(high, b, dims) + dot(low, b, dims)
+    return dot(a, high, dims) + dot(a, low, dims)
 
 
 def one_hot(row_ref, rows):
@@ -115,7 +126,12 @@
 
 
 def source(dest):
-    return (dest % BLOCK // CHUNK) * PACK + (dest // BLOCK) * CHUNK + dest % CHUNK
+    return (dest % QB // CHUNK) * PACK + (dest // QB) * CHUNK + dest % CHUNK
+
+
+def quarter(q):
+    right = FAR + q * QROWS if q < 2 else ROWS + (q - 2) * QROWS
+    return slice(q * QROWS, (q + 1) * QROWS), slice(right, right + QROWS)
 
 
 def main_kernel(
@@ -135,7 +151,6 @@
     normed_ref,
     rstd_ref,
     xn_ref,
-    back_ref,
     k_ref,
     v_ref,
     gkv_ref,
@@ -149,16 +164,18 @@
     ]
     for copy in copies:
         copy.start()
-    shape = (ROWS, ROWS)
-    row = source(lax.broadcasted_iota(jnp.int32, (ROWS, 1), 0))
-    perm = row == lax.broadcasted_iota(jnp.int32, shape, 1)
-    column = source(lax.broadcasted_iota(jnp.int32, (1, ROWS), 1))
-    back = column == lax.broadcasted_iota(jnp.int32, shape, 0)
-    back_ref[...] = jnp.where(back, 1.0, 0.0).astype(BF16)
-    x_in = jnp.concatenate(
-        [in_ref[:ROWS], jnp.concatenate([in_ref[FAR:], in_ref[ROWS:FAR]], axis=0)], axis=1
-    )
-    normed_ref[...] = dot(jnp.where(perm, 1.0, 0.0).astype(BF16), x_in, NN)
+    shape = (QROWS, QROWS)
+    row = source(lax.broadcasted_iota(jnp.int32, (QROWS, 1), 0))
+    perm = jnp.where(row == lax.broadcasted_iota(jnp.int32, shape, 1), 1.0, 0.0).astype(BF16)
+    column = source(lax.broadcasted_iota(jnp.int32, (1, QROWS), 1))
+    back = jnp.where(column == lax.broadcasted_iota(jnp.int32, shape, 0), 1.0, 0.0).astype(BF16)
+    for q in range(4):
+        left, right = quarter(q)
+        x_in = jnp.concatenate([in_ref[left, :], in_ref[right, :]], axis=1)
+        x = dot(perm, x_in, NN)
+        for t in range(ITEMS):
+            at = t * BLOCK + q * QB
+            normed_ref[at : at + QB, :] = x[t * QB : (t + 1) * QB]
     gain = gain_ref[...].astype(F32)
     for t in range(ITEMS):
         rows = pl.ds(t * BLOCK, BLOCK)
@@ -182,14 +199,14 @@
     grad_attn = dot(up, wo_ref[...], NN).astype(BF16)
 
     lane_head = lax.broadcasted_iota(jnp.int32, (BLOCK, GL), 1) // HEAD_DIM
-    head_pick = (
-        lax.broadcasted_iota(jnp.int32, (HEADS, HDT), 1) // HEAD_DIM
-        == lax.broadcasted_iota(jnp.int32, (HEADS, HDT), 0)
-    ).astype(F32)
-    group_pick = (
-        lax.broadcasted_iota(jnp.int32, (8, GL), 1) // HEAD_DIM
-        == lax.broadcasted_iota(jnp.int32, (8, GL), 0)
-    ).astype(F32)
+    def picks(shape):
+        hit = lax.broadcasted_iota(jnp.int32, shape, 1) // HEAD_DIM == lax.broadcasted_iota(
+            jnp.int32, shape, 0
+        )
+        return jnp.where(hit, 1.0, 0.0).astype(BF16)
+
+    head_pick = picks((16, HDT))
+    group_pick = picks((16, GL))
     diagonal = lax.broadcasted_iota(jnp.int32, (BLOCK, KEYS), 0) == lax.broadcasted_iota(
         jnp.int32, (BLOCK, KEYS), 1
     )
@@ -209,7 +226,7 @@
         keys = pl.ds(b * KEYS, KEYS)
         own = slice(b * BLOCK, (b + 1) * BLOCK)
         kf = k_ref[keys, :].astype(F32)
-        norm2 = dot(head_pick, kf * kf, NT, precision=lax.Precision.HIGHEST)
+        norm2 = split_dot(head_pick, kf * kf, NT, 1)
         inv_k = 1.0 / jnp.sqrt(norm2 + head_eps)
         allowed = (seen_ref[b : b + 1, :] > 0.0) | diagonal
         mask = jnp.concatenate([allowed] * GROUP, axis=0)
@@ -250,8 +267,8 @@
                 axis=0,
             )
             coef = ik * ik * col_terms
-            coef = jnp.concatenate([coef, jnp.zeros_like(coef)], axis=0)
-            coef = dot(coef, group_pick, TN, precision=lax.Precision.HIGHEST)
+            coef = jnp.concatenate([coef] + [jnp.zeros_like(coef)] * 3, axis=0)
+            coef = split_dot(coef, group_pick, TN, 0)
             gk = dot(weighted, qm, TN) - coef * k4.astype(F32)
             gkv_ref[keys, g * GL : (g + 1) * GL] = gk.astype(BF16)
             gkv_ref[keys, HDT + g * GL : HDT + (g + 1) * GL] = dot(prob_b, gm, TN).astype(BF16)
@@ -272,10 +289,14 @@
         if t % SLOTS == 0:
             grad = grad + up[b * BLOCK : (b + 1) * BLOCK].astype(F32)
         xn_ref[rows, :] = grad.astype(BF16)
-    back = dot(back_ref[...], xn_ref[...], NN).astype(BF16)
-    out_ref[:ROWS] = back[:, :HALF]
-    out_ref[FAR:] = back[: ROWS // 2, HALF:]
-    out_ref[ROWS:FAR] = back[ROWS // 2 :, HALF:]
+    for q in range(4):
+        left, right = quarter(q)
+        x = jnp.concatenate(
+            [xn_ref[t * BLOCK + q * QB : t * BLOCK + (q + 1) * QB, :] for t in range(ITEMS)], axis=0
+        )
+        x = dot(back, x, NN).astype(BF16)
+        out_ref[left, :] = x[:, :HALF]
+        out_ref[right, :] = x[:, HALF:]
 
 
 def output_kernel(att_ref, own_ref, wo_ref, out_ref):
@@ -302,6 +323,37 @@
         compiler_params=pltpu.CompilerParams(vmem_limit_bytes=limit * 2**20),
         cost_estimate=pl.CostEstimate(flops=flops, bytes_accessed=moved, transcendentals=0),
     )(*args)
+
+
+def main_call(sharpness_coefficient, arrived, weights, upstream_derivative, gain, seen):
+    return call(
+        main_kernel,
+        [(SHARDS * PACK, HALF), (TOK, HDT), (TOK, D), (D, HDT)],
+        (
+            sharpness_coefficient,
+            arrived,
+            weights,
+            upstream_derivative,
+            gain,
+            seen,
+        ),
+        [SM, VM, HB_SPEC, HB_SPEC, VM, VM],
+        4 * 10**9,
+        scratch=[
+            pltpu.VMEM((D, 3 * HDT), BF16),
+            pltpu.VMEM((TOK, D), BF16),
+            pltpu.SemaphoreType.DMA((3,)),
+            pltpu.VMEM((ROWS, D), F32),
+            pltpu.VMEM((ROWS, 128), F32),
+            pltpu.VMEM((ROWS, D), BF16),
+            pltpu.VMEM((ROWS, HDT), BF16),
+            pltpu.VMEM((ROWS, HDT), BF16),
+            pltpu.VMEM((ROWS, D), BF16),
+            pltpu.VMEM((TOK, HDT), BF16),
+            pltpu.VMEM((ROWS, D), F32),
+        ],
+        limit=40,
+    )
 
 
 def body(
@@ -381,34 +433,13 @@
     picks = jnp.sum(picks * (jnp.arange(SHARDS) == me)[:, None, None], axis=0)
     seen = jnp.dot(picks, seen_all).reshape(NB, KEYS)
 
-    leaving, attended, own, out_weight = call(
-        main_kernel,
-        [(SHARDS * PACK, HALF), (TOK, HDT), (TOK, D), (D, HDT)],
-        (
-            sharpness_coefficient,
-            arrived,
-            weights,
-            upstream_derivative[0],
-            standardizer_multiplier.reshape(1, D),
-            seen,
-        ),
-        [SM, VM, HB_SPEC, HB_SPEC, VM, VM],
-        4 * 10**9,
-        scratch=[
-            pltpu.VMEM((D, 3 * HDT), BF16),
-            pltpu.VMEM((TOK, D), BF16),
-            pltpu.SemaphoreType.DMA((3,)),
-            pltpu.VMEM((ROWS, D), F32),
-            pltpu.VMEM((ROWS, 128), F32),
-            pltpu.VMEM((ROWS, D), BF16),
-            pltpu.VMEM((ROWS, ROWS), BF16),
-            pltpu.VMEM((ROWS, HDT), BF16),
-            pltpu.VMEM((ROWS, HDT), BF16),
-            pltpu.VMEM((ROWS, D), BF16),
-            pltpu.VMEM((TOK, HDT), BF16),
-            pltpu.VMEM((ROWS, D), F32),
-        ],
-        limit=40,
+    leaving, attended, own, out_weight = main_call(
+        sharpness_coefficient,
+        arrived,
+        weights,
+        upstream_derivative[0],
+        standardizer_multiplier.reshape(1, D),
+        seen,
     )
     returned = lax.all_to_all(
         leaving.reshape(SHARDS, PACK, HALF), "tok", split_axis=0, concat_axis=0, tiled=True

time: 137 us -> 133 us (0.971)
  Pallas kernels: 21.5 us -> 17.3 us
    pallas_call x6, Pallas kernels: 21.5 us -> 17.3 us  [call(): pl.pallas_call(kernel, out_shape=[place(o[:2], o[2] if len(o) > 2 else BF...]
where the time goes in v4:
time: 133 us
  blocking collectives  39.7 us (30%)
  waiting for transfers between devices  37.2 us (28%)
  starting transfers between devices  20.8 us (16%)
  Pallas kernels  17.3 us (13%)
  between operations  14.2 us (11%)
  local copies, waits for them, and re-layouts  2.17 us (2%)
  other arithmetic  1.36 us (1%)
    all_to_all x1, blocking collectives, body(): lax.all_to_all(leaving.reshape(SHARDS, PACK, HALF), 'tok', split_axis=0,...  39.7 us
    all_to_all x1, waiting for transfers between devices, body(): lax.all_to_all(packed.reshape(SHARDS, PACK, HALF), 'tok', split_axis=0, c...  31 us
    pallas_call x6, Pallas kernels, call(): pl.pallas_call(kernel, out_shape=[place(o[:2], o[2] if len(o) > 2 else BF...  17.3 us
    all_to_all x1, starting transfers between devices, body(): lax.all_to_all(packed.reshape(SHARDS, PACK, HALF), 'tok', split_axis=0, c...  13 us
    ppermute x2, starting transfers between devices, body(): recv = lax.ppermute(send, 'tok', partner)  7.73 us
    ppermute x2, waiting for transfers between devices, body(): recv = lax.ppermute(send, 'tok', partner)  6.1 us
  transfers between devices with their start and end apart: 4, of which 3 were waited for; matrix products, arithmetic and copies ran while one was open for 3% of the time, Pallas kernels for 2%

profile of v4, /device:TPU:8, one launch (start us, length us, event | category | flops | bytes accessed | tf_op | source)
XLA Modules:
  0.0 132.8 jit_solution(2612797832006067273)
XLA Ops:
  7.2 1.8 %shard_map.131 = (bf16[128,512]{1,0:T(8,128)(2,1)S(1)}, bf16[128,512]{1,0:T(8,128)(2,1)S(1)}, bf16[64,2048]{1,0:T(8,128)(2,1)}) custom-call(s32[1]{0:T(128)} %bitcast.side_ref, s32[1,128]{1,0:T(1,128)} %bitcast.31, bf16[128,1024]{1,0:T(8,128)(2,1)} %bitcast.33, bf16[64,512]{1,0:T(8,128)(2,1)} %wq_hbm.1, bf16[64,512]{1,0:T(8,128)(2,1)} %wk_hbm.1, ...), custom_call_target="tpu_custom_call" | custom-call | flops 33554432 | bytes 1049092 | tf_op jit(solution)/shard_map/pallas_call | solution.py:317
  9.0 4.7 %collective-permute-start = (bf16[128,512]{1,0:T(8,128)(2,1)S(1)}, bf16[128,512]{1,0:T(8,128)(2,1)S(1)}, u32[]{:S(2)}, u32[]{:S(2)}) collective-permute-start(bf16[128,512]{1,0:T(8,128)(2,1)S(1)} %get-tuple-element.12), channel_id=1, source_target_pairs={{0,24},{1,25},{2,26},{3,27},{4,28},{5,29},{6,30},{7,31},{8,16},{9,... | collective-permute-start | bytes 393224 | tf_op jit(solution)/shard_map/ppermute | solution.py:400
  13.7 0.8 copy.33
  14.5 0.1 pad_add_fusion
  14.6 0.1 copy.34
  14.8 0.1 iota_add_fusion
  15.0 0.1 add.60.target_ref
  15.1 2.3 %collective-permute-done.recv_ref = bf16[128,512]{1,0:T(8,128)(2,1)S(1)} collective-permute-done((bf16[128,512]{1,0:T(8,128)(2,1)S(1)}, bf16[128,512]{1,0:T(8,128)(2,1)S(1)}, u32[]{:S(2)}, u32[]{:S(2)}) %collective-permute-start) | collective-permute-done | bytes 131104 | tf_op jit(solution)/shard_map/ppermute | solution.py:400
  17.4 1.6 %shard_map.132 = bf16[1280,512]{1,0:T(8,128)(2,1)} custom-call(s32[1]{0:T(128)} %bitcast.side_ref, s32[1,1280]{1,0:T(1,128)S(1)} %add.60.target_ref, bf16[128,512]{1,0:T(8,128)(2,1)S(1)} %get-tuple-element.11.keep_ref, bf16[128,512]{1,0:T(8,128)(2,1)S(1)} %collective-permute-done.recv_ref), custom_call_target="tpu_custom_call" | custom-call | flops 335544320 | bytes 1577988 | tf_op jit(solution)/shard_map/pallas_call | solution.py:317
  19.0 13.0 %all-to-all-start = ((bf16[32,40,512]{2,1,0:T(8,128)(2,1)}), bf16[32,40,512]{2,1,0:T(8,128)(2,1)S(1)}, u32[]{:S(2)}, u32[]{:S(2)}) async-start(bf16[32,40,512]{2,1,0:T(8,128)(2,1)} %bitcast.5), calls=%async_computation | async-start | bytes 2621440 | tf_op jit(solution)/shard_map/all_to_all | solution.py:416
  32.1 0.5 broadcast.102
  32.7 0.7 reduce.7
  33.3 0.1 le.28
  33.7 0.1 fusion.8
  34.0 0.2 select_reduce_fusion
  34.2 0.1 fusion.9
  34.4 31.0 %all-to-all-done = bf16[32,40,512]{2,1,0:T(8,128)(2,1)S(1)} async-done(((bf16[32,40,512]{2,1,0:T(8,128)(2,1)}), bf16[32,40,512]{2,1,0:T(8,128)(2,1)S(1)}, u32[]{:S(2)}, u32[]{:S(2)}) %all-to-all-start) | async-done | bytes 1310752 | tf_op jit(solution)/shard_map/all_to_all | solution.py:416
  65.4 11.3 %shard_map.133 = (bf16[1280,512]{1,0:T(8,128)(2,1)S(1)}, bf16[128,512]{1,0:T(8,128)(2,1)S(1)}, bf16[128,1024]{1,0:T(8,128)(2,1)S(1)}, bf16[1024,512]{1,0:T(8,128)(2,1)S(1)}) custom-call(f32[8]{0:T(128)S(1)} %copy-done.1, bf16[1280,512]{1,0:T(8,128)(2,1)S(1)} %bitcast.29, bf16[1024,2048]{1,0:T(8,128)(2,1)} %all-gather.2.cloned.1.call-done.w_hbm, ...), custom_call_target="tpu_custom_call" | custom-call | flops 4000000000 | bytes 8524320 | tf_op jit(solution)/shard_map/pallas_call | solution.py:317
  76.7 39.7 %all_to_all.10 = bf16[32,40,512]{2,1,0:T(8,128)(2,1)S(1)} all-to-all(bf16[32,40,512]{2,1,0:T(8,128)(2,1)S(1)} %bitcast.30), channel_id=1, replica_groups=mesh['fsdp'=16,'tok'=32] {'tok'}, dimensions={0} | all-to-all | bytes 2621440 | tf_op jit(solution)/shard_map/all_to_all | solution.py:444
  116.4 0.5 shard_map.135
  116.9 3.1 %collective-permute-start.1 = (bf16[128,512]{1,0:T(8,128)(2,1)S(1)}, bf16[128,512]{1,0:T(8,128)(2,1)S(1)}, u32[]{:S(2)}, u32[]{:S(2)}) collective-permute-start(bf16[128,512]{1,0:T(8,128)(2,1)S(1)} %get-tuple-element.19), channel_id=1, source_target_pairs={{0,24},{1,25},{2,26},{3,27},{4,28},{5,29},{6,30},{7,31},{8,16},{9,... | collective-permute-start | bytes 393224 | tf_op jit(solution)/shard_map/ppermute | solution.py:461
  120.0 1.2 shard_map.134
  121.2 3.8 %collective-permute-done.1.recv_ref = bf16[128,512]{1,0:T(8,128)(2,1)S(1)} collective-permute-done((bf16[128,512]{1,0:T(8,128)(2,1)S(1)}, bf16[128,512]{1,0:T(8,128)(2,1)S(1)}, u32[]{:S(2)}, u32[]{:S(2)}) %collective-permute-start.1) | collective-permute-done | bytes 131104 | tf_op jit(solution)/shard_map/ppermute | solution.py:461
  125.0 0.9 shard_map.136
  (31 shorter events, 0.8 us)
Async XLA Ops:
  7.2 58.3 %all-gather.2.cloned.1.call-start = ((), (), s32[]{:S(2)}) async-start(), calls=%async_computation.2 | async-start | bytes 4456448 | tf_op jit(solution)/shard_map/all_gather | solution.py:399
  9.0 8.3 %collective-permute-start = (bf16[128,512]{1,0:T(8,128)(2,1)S(1)}, bf16[128,512]{1,0:T(8,128)(2,1)S(1)}, u32[]{:S(2)}, u32[]{:S(2)}) collective-permute-start(bf16[128,512]{1,0:T(8,128)(2,1)S(1)} %get-tuple-element.12), channel_id=1, source_target_pairs={{0,24},{1,25},{2,26},{3,27},{4,28},{5,29},{6,30},{7,31},{8,16},{9,... | collective-permute-start | bytes 393224 | tf_op jit(solution)/shard_map/ppermute | solution.py:400
  19.0 13.2 %copy-start.3 = (bf16[1024]{0:T(1024)(128)(2,1)S(1)}, bf16[1024]{0:T(1024)(128)(2,1)}, u32[]{:S(2)}) copy-start(bf16[1024]{0:T(1024)(128)(2,1)} %param.17) | copy-start | bytes 6148
  19.0 13.7 %copy-start.4 = (s32[1,64]{1,0:T(1,128)S(1)}, s32[1,64]{1,0:T(1,128)}, u32[]{:S(2)}) copy-start(s32[1,64]{1,0:T(1,128)} %param.16) | copy-start | bytes 772
  19.0 14.5 %copy-start.2 = (s32[1,4096]{1,0:T(1,128)S(1)}, s32[1,4096]{1,0:T(1,128)}, u32[]{:S(2)}) copy-start(s32[1,4096]{1,0:T(1,128)} %param.14) | copy-start | bytes 49156
  19.0 46.5 %copy-start.1 = (f32[8]{0:T(128)S(1)}, f32[8]{0:T(128)}, u32[]{:S(2)}) copy-start(f32[8]{0:T(128)} %sharp_ref.1) | copy-start | bytes 100
  19.0 46.4 %all-to-all-start = ((bf16[32,40,512]{2,1,0:T(8,128)(2,1)}), bf16[32,40,512]{2,1,0:T(8,128)(2,1)S(1)}, u32[]{:S(2)}, u32[]{:S(2)}) async-start(bf16[32,40,512]{2,1,0:T(8,128)(2,1)} %bitcast.5), calls=%async_computation | async-start | bytes 2621440 | tf_op jit(solution)/shard_map/all_to_all | solution.py:416
  116.4 8.6 %copy-start = (s32[1,1,128]{2,1,0:T(1,128)S(1)}, s32[1,1,128]{2,1,0:T(1,128)}, u32[]{:S(2)}) copy-start(s32[1,1,128]{2,1,0:T(1,128)} %param.13) | copy-start | bytes 1540
  116.9 8.1 %collective-permute-start.1 = (bf16[128,512]{1,0:T(8,128)(2,1)S(1)}, bf16[128,512]{1,0:T(8,128)(2,1)S(1)}, u32[]{:S(2)}, u32[]{:S(2)}) collective-permute-start(bf16[128,512]{1,0:T(8,128)(2,1)S(1)} %get-tuple-element.19), channel_id=1, source_target_pairs={{0,24},{1,25},{2,26},{3,27},{4,28},{5,29},{6,30},{7,31},{8,16},{9,... | collective-permute-start | bytes 393224 | tf_op jit(solution)/shard_map/ppermute | solution.py:461
Sparse Core Ops, SparseCore 0:
  10.7 48.9 all-gather.1

commit v5 on v4

--- a/solution.py
+++ b/solution.py
@@ -29,7 +29,10 @@
 GL = GROUP * HEAD_DIM
 GR = GROUP * BLOCK
 
+CHIPS = 8
 SHARE = 64
+CHIP = 2 * SHARE
+HOPS = 3
 
 norm_eps = 1e-05
 head_eps = 1e-06
@@ -37,6 +40,7 @@
 BF16 = jnp.bfloat16
 VM = pl.BlockSpec(memory_space=pltpu.VMEM)
 SM = pl.BlockSpec(memory_space=pltpu.SMEM)
+ANY = pl.BlockSpec(memory_space=pl.ANY)
 HB_SPEC = pl.BlockSpec(memory_space=pltpu.HBM)
 NN = (((1,), (0,)), ((), ()))
 NT = (((1,), (1,)), ((), ()))
@@ -99,6 +103,19 @@
     send_ref[...] = jnp.where(lower, right, left)
 
 
+def stack_kernel(*refs):
+    out_ref, sems = refs[-2:]
+    copies, at = [], 0
+    for n, ref in enumerate(refs[:-2]):
+        rows = ref.shape[0]
+        copies.append(pltpu.make_async_copy(ref, out_ref.at[pl.ds(at, rows), :], sems.at[n]))
+        at += rows
+    for copy in copies:
+        copy.start()
+    for copy in copies:
+        copy.wait()
+
+
 def pack_kernel(side_ref, target_ref, keep_ref, recv_ref, out_ref):
     lower = side_ref[0] == 0
     keep, recv = keep_ref[...], recv_ref[...]
@@ -136,8 +153,11 @@
 
 def main_kernel(
     sharp_ref,
+    place_ref,
     in_ref,
-    w_hbm,
+    chip_any,
+    mine_any,
+    other_any,
     up_hbm,
     gain_ref,
     seen_ref,
@@ -157,11 +177,23 @@
     gq_ref,
     gh_ref,
 ):
-    copies = [
-        pltpu.make_async_copy(w_hbm.at[:, pl.ds(0, 3 * HDT)], w_ref, sems.at[0]),
-        pltpu.make_async_copy(w_hbm.at[:, pl.ds(3 * HDT, HDT)], wo_ref, sems.at[1]),
-        pltpu.make_async_copy(up_hbm, up_ref, sems.at[2]),
-    ]
+    copies = [pltpu.make_async_copy(up_hbm, up_ref, sems.at[0])]
+
+    def bring(part, at, chip, rows, first):
+        chip = lax.rem(chip + CHIPS, CHIPS)
+        dst = pl.ds(pl.multiple_of(chip * CHIP + first, SHARE), rows)
+        src = pl.ds(at, rows)
+        for lanes, ref in ((pl.ds(0, 3 * HDT), w_ref), (pl.ds(3 * HDT, HDT), wo_ref)):
+            copies.append(
+                pltpu.make_async_copy(part.at[src, lanes], ref.at[dst, :], sems.at[len(copies)])
+            )
+
+    y, core = place_ref[0], place_ref[1]
+    bring(chip_any, 0, y, CHIP, 0)
+    for part, side in ((mine_any, core), (other_any, 1 - core)):
+        for hop in range(HOPS):
+            bring(part, hop * CHIP, y + (2 * side - 1) * (hop + 1), CHIP, 0)
+        bring(part, HOPS * CHIP, y + CHIPS // 2, SHARE, side * SHARE)
     for copy in copies:
         copy.start()
     shape = (QROWS, QROWS)
@@ -325,24 +357,54 @@
     )(*args)
 
 
-def main_call(sharpness_coefficient, arrived, weights, upstream_derivative, gain, seen):
+def gather_weights(share, place):
+    members = 2 * CHIPS
+    sibling = [(i, i ^ 1) for i in range(members)]
+
+    def onward(part, hops):
+        pairs = [(i, (i + hops * (2 - 4 * (i % 2))) % members) for i in range(members)]
+        return lax.ppermute(part, "fsdp", pairs)
+
+    first = place[1] == 0
+    beside = lax.ppermute(share, "fsdp", sibling)
+    chip = jnp.concatenate(
+        [jnp.where(first, share, beside), jnp.where(first, beside, share)], axis=0
+    )
+    near, far = onward(chip, 1), onward(chip, 2)
+    half = jnp.where(first, far[:SHARE], far[SHARE:])
+    pieces = [near, far, onward(far, 1), onward(half, 2)]
+    (mine,) = call(
+        stack_kernel,
+        [(HOPS * CHIP + SHARE, 4 * HDT)],
+        pieces,
+        [HB_SPEC] * (HOPS + 1),
+        0,
+        scratch=[pltpu.SemaphoreType.DMA((HOPS + 1,))],
+    )
+    return chip, mine, lax.ppermute(mine, "fsdp", sibling)
+
+
+def main_call(sharpness_coefficient, place, arrived, chip, mine, other, upstream_derivative, gain, seen):
     return call(
         main_kernel,
         [(SHARDS * PACK, HALF), (TOK, HDT), (TOK, D), (D, HDT)],
         (
             sharpness_coefficient,
+            place,
             arrived,
-            weights,
+            chip,
+            mine,
+            other,
             upstream_derivative,
             gain,
             seen,
         ),
-        [SM, VM, HB_SPEC, HB_SPEC, VM, VM],
+        [SM, SM, VM, HB_SPEC, ANY, ANY, HB_SPEC, VM, VM],
         4 * 10**9,
         scratch=[
             pltpu.VMEM((D, 3 * HDT), BF16),
             pltpu.VMEM((TOK, D), BF16),
-            pltpu.SemaphoreType.DMA((3,)),
+            pltpu.SemaphoreType.DMA((7 + 4 * (HOPS + 1),)),
             pltpu.VMEM((ROWS, D), F32),
             pltpu.VMEM((ROWS, 128), F32),
             pltpu.VMEM((ROWS, D), BF16),
@@ -396,7 +458,9 @@
             pltpu.SemaphoreType.DMA((6,)),
         ],
     )
-    weights = lax.all_gather(share, "fsdp", axis=0, tiled=True)
+    member = lax.axis_index("fsdp").astype(jnp.int32)
+    place = jnp.stack([member // 2, member % 2])
+    chip, mine, other = gather_weights(share, place)
     recv = lax.ppermute(send, "tok", partner)
 
     lists = bordering_tiles[0].reshape(SHARDS, NB, KN)
@@ -435,8 +499,11 @@
 
     leaving, attended, own, out_weight = main_call(
         sharpness_coefficient,
+        place,
         arrived,
-        weights,
+        chip,
+        mine,
+        other,
         upstream_derivative[0],
         standardizer_multiplier.reshape(1, D),
         seen,

time: 133 us -> 126 us (0.947)
  the two profiles are of different devices: /device:TPU:8 before, /device:TPU:40 now
where the time goes in v5:
time: 126 us; the launch traced here: 125 us
  blocking collectives  43.4 us (34%)
  starting transfers between devices  35.4 us (28%)
  waiting for transfers between devices  22.2 us (18%)
  Pallas kernels  18 us (14%)
  local copies, waits for them, and re-layouts  3.7 us (3%)
  other arithmetic  1.54 us (1%)
    all_to_all x1, blocking collectives, body(): lax.all_to_all(leaving.reshape(SHARDS, PACK, HALF), 'tok', split_axis=0,...  43.4 us
    pallas_call x7, Pallas kernels, call(): pl.pallas_call(kernel, out_shape=[place(o[:2], o[2] if len(o) > 2 else BF...  18 us
    ppermute x4, waiting for transfers between devices, onward(): return lax.ppermute(part, 'fsdp', pairs)  16.2 us
    all_to_all x1, starting transfers between devices, body(): lax.all_to_all(packed.reshape(SHARDS, PACK, HALF), 'tok', split_axis=0, c...  12.9 us
    ppermute x4, starting transfers between devices, onward(): return lax.ppermute(part, 'fsdp', pairs)  10.7 us
    ppermute x2, starting transfers between devices, body(): recv = lax.ppermute(send, 'tok', partner)  8.01 us
    ppermute x2, waiting for transfers between devices, body(): recv = lax.ppermute(send, 'tok', partner)  3.65 us
    unnamed x22, local copies, waits for them, and re-layouts  2.84 us
  transfers between devices with their start and end apart: 9, of which 5 were waited for; matrix products, arithmetic and copies ran while one was open for 3% of the time, Pallas kernels for 3%

profile of v5, /device:TPU:40, one launch (start us, length us, event | category | flops | bytes accessed | tf_op | source)
XLA Modules:
  0.0 125.3 jit_solution(18219784843228029804)
XLA Ops:
  0.6 1.3 %shard_map.131 = (bf16[128,512]{1,0:T(8,128)(2,1)S(1)}, bf16[128,512]{1,0:T(8,128)(2,1)S(1)}, bf16[64,2048]{1,0:T(8,128)(2,1)S(1)}) custom-call(s32[1]{0:T(128)} %bitcast.2.side_ref, s32[1,128]{1,0:T(1,128)} %bitcast.33, bf16[128,1024]{1,0:T(8,128)(2,1)} %bitcast.35, bf16[64,512]{1,0:T(8,128)(2,1)} %wq_hbm.1, bf16[64,512]{1,0:T(8,128)(2,1)} %wk_hbm.1, ...), custom_call_target="tpu_custom_call" | custom-call | flops 33554432 | bytes 1049092 | tf_op jit(solution)/shard_map/pallas_call | solution.py:349
  2.0 1.9 %collective-permute-start.1 = (bf16[64,2048]{1,0:T(8,128)(2,1)S(1)}, bf16[64,2048]{1,0:T(8,128)(2,1)S(1)}, u32[]{:S(2)}, u32[]{:S(2)}) collective-permute-start(bf16[64,2048]{1,0:T(8,128)(2,1)S(1)} %get-tuple-element.13), channel_id=1, source_target_pairs={{0,32},{32,0},{64,96},{96,64},{128,160},{160,128},{192,224},{224,1... | collective-permute-start | bytes 786440 | tf_op jit(solution)/shard_map/ppermute | solution.py:369
  3.9 4.7 %collective-permute-start = (bf16[128,512]{1,0:T(8,128)(2,1)S(1)}, bf16[128,512]{1,0:T(8,128)(2,1)S(1)}, u32[]{:S(2)}, u32[]{:S(2)}) collective-permute-start(bf16[128,512]{1,0:T(8,128)(2,1)S(1)} %get-tuple-element.12), channel_id=1, source_target_pairs={{0,24},{1,25},{2,26},{3,27},{4,28},{5,29},{6,30},{7,31},{8,16},{9,... | collective-permute-start | bytes 393224 | tf_op jit(solution)/shard_map/ppermute | solution.py:464
  8.6 0.8 copy.33
  9.5 2.7 %collective-permute-start.3 = (bf16[128,2048]{1,0:T(8,128)(2,1)S(1)}, bf16[128,2048]{1,0:T(8,128)(2,1)S(1)}, u32[]{:S(2)}, u32[]{:S(2)}) collective-permute-start(bf16[128,2048]{1,0:T(8,128)(2,1)S(1)} %pad_maximum_fusion.chip_any), channel_id=1, source_target_pairs={{0,128},{32,416},{64,192},{96,480},{128,256},{160,32},{192,320},{2... | collective-permute-start | bytes 1572872 | tf_op jit(solution)/shard_map/ppermute | solution.py:366
  12.9 1.6 %shard_map.132 = bf16[1280,512]{1,0:T(8,128)(2,1)} custom-call(s32[1]{0:T(128)} %bitcast.2.side_ref, s32[1,1280]{1,0:T(1,128)S(1)} %add.66.target_ref, bf16[128,512]{1,0:T(8,128)(2,1)S(1)} %get-tuple-element.11.keep_ref, bf16[128,512]{1,0:T(8,128)(2,1)S(1)} %collective-permute-done.recv_ref), custom_call_target="tpu_custom_call" | custom-call | flops 335544320 | bytes 1577988 | tf_op jit(solution)/shard_map/pallas_call | solution.py:349
  14.5 12.9 %all-to-all-start = ((bf16[32,40,512]{2,1,0:T(8,128)(2,1)}), bf16[32,40,512]{2,1,0:T(8,128)(2,1)S(1)}, u32[]{:S(2)}, u32[]{:S(2)}) async-start(bf16[32,40,512]{2,1,0:T(8,128)(2,1)} %bitcast.7), calls=%async_computation | async-start | bytes 2621440 | tf_op jit(solution)/shard_map/all_to_all | solution.py:480
  27.5 2.6 %collective-permute-start.2 = (bf16[128,2048]{1,0:T(8,128)(2,1)S(1)}, bf16[128,2048]{1,0:T(8,128)(2,1)S(1)}, u32[]{:S(2)}, u32[]{:S(2)}) collective-permute-start(bf16[128,2048]{1,0:T(8,128)(2,1)S(1)} %pad_maximum_fusion.chip_any), channel_id=1, source_target_pairs={{0,64},{32,480},{64,128},{96,32},{128,192},{160,96},{192,256},{224... | collective-permute-start | bytes 1572872 | tf_op jit(solution)/shard_map/ppermute | solution.py:366
  30.1 2.6 %collective-permute-start.4 = (bf16[128,2048]{1,0:T(8,128)(2,1)S(1)}, bf16[128,2048]{1,0:T(8,128)(2,1)S(1)}, u32[]{:S(2)}, u32[]{:S(2)}) collective-permute-start(bf16[128,2048]{1,0:T(8,128)(2,1)S(1)} %collective-permute-done.3.refs_1_), channel_id=1, source_target_pairs={{0,64},{32,480},{64,128},{96,32},{128,192},{160,96},{192,256},{224... | collective-permute-start | bytes 1572872 | tf_op jit(solution)/shard_map/ppermute | solution.py:366
  32.8 2.8 %collective-permute-start.5 = (bf16[64,2048]{1,0:T(8,128)(2,1)S(1)}, bf16[64,2048]{1,0:T(8,128)(2,1)S(1)}, u32[]{:S(2)}, u32[]{:S(2)}) collective-permute-start(bf16[64,2048]{1,0:T(8,128)(2,1)S(1)} %slice_select_fusion), channel_id=1, source_target_pairs={{0,128},{32,416},{64,192},{96,480},{128,256},{160,32},{192,320},{2... | collective-permute-start | bytes 786440 | tf_op jit(solution)/shard_map/ppermute | solution.py:366
  35.6 3.0 %collective-permute-done.2.refs_0_ = bf16[128,2048]{1,0:T(8,128)(2,1)S(1)} collective-permute-done((bf16[128,2048]{1,0:T(8,128)(2,1)S(1)}, bf16[128,2048]{1,0:T(8,128)(2,1)S(1)}, u32[]{:S(2)}, u32[]{:S(2)}) %collective-permute-start.2) | collective-permute-done | bytes 524320 | tf_op jit(solution)/shard_map/ppermute | solution.py:366
  38.5 13.2 %collective-permute-done.5.refs_3_ = bf16[64,2048]{1,0:T(8,128)(2,1)S(1)} collective-permute-done((bf16[64,2048]{1,0:T(8,128)(2,1)S(1)}, bf16[64,2048]{1,0:T(8,128)(2,1)S(1)}, u32[]{:S(2)}, u32[]{:S(2)}) %collective-permute-start.5) | collective-permute-done | bytes 262176 | tf_op jit(solution)/shard_map/ppermute | solution.py:366
  51.8 0.7 copy-done.6
  52.5 0.8 copy-done.4
  53.3 1.5 %shard_map.133.mine_any = bf16[448,2048]{1,0:T(8,128)(2,1)S(1)} custom-call(bf16[128,2048]{1,0:T(8,128)(2,1)} %copy-done.3, bf16[128,2048]{1,0:T(8,128)(2,1)} %copy-done.2, bf16[128,2048]{1,0:T(8,128)(2,1)} %copy-done.4, bf16[64,2048]{1,0:T(8,128)(2,1)} %copy-done.6), custom_call_target="tpu_custom_call" | custom-call | tf_op jit(solution)/shard_map/pallas_call | solution.py:349
  54.8 1.9 %collective-permute-start.6 = (bf16[448,2048]{1,0:T(8,128)(2,1)S(1)}, bf16[448,2048]{1,0:T(8,128)(2,1)}, u32[]{:S(2)}, u32[]{:S(2)}) collective-permute-start(bf16[448,2048]{1,0:T(8,128)(2,1)S(1)} %shard_map.133.mine_any), channel_id=1, source_target_pairs={{0,32},{32,0},{64,96},{96,64},{128,160},{160,128},{192,224},{224,1... | collective-permute-start | bytes 5505032 | tf_op jit(solution)/shard_map/ppermute | solution.py:384
  57.3 0.7 reduce.7
  59.1 2.3 %all-to-all-done = bf16[32,40,512]{2,1,0:T(8,128)(2,1)S(1)} async-done(((bf16[32,40,512]{2,1,0:T(8,128)(2,1)}), bf16[32,40,512]{2,1,0:T(8,128)(2,1)S(1)}, u32[]{:S(2)}, u32[]{:S(2)}) %all-to-all-start) | async-done | bytes 1310752 | tf_op jit(solution)/shard_map/all_to_all | solution.py:480
  61.5 10.9 %shard_map.134 = (bf16[1280,512]{1,0:T(8,128)(2,1)S(1)}, bf16[128,512]{1,0:T(8,128)(2,1)S(1)}, bf16[128,1024]{1,0:T(8,128)(2,1)S(1)}, bf16[1024,512]{1,0:T(8,128)(2,1)S(1)}) custom-call(f32[8]{0:T(128)S(1)} %copy-done.1, s32[2]{0:T(128)S(1)} %pad_add_fusion.1.place_ref, bf16[1280,512]{1,0:T(8,128)(2,1)S(1)} %bitcast.31, bf16[128,2048]{1,0:T(8,128)(2,1)} %copy-done.5, ...), custom_call_target="tpu_custom_call" | custom-call | flops 4000000000 | bytes 8524328 | tf_op jit(solution)/shard_map/pallas_call | solution.py:349
  72.4 43.4 %all_to_all.10 = bf16[32,40,512]{2,1,0:T(8,128)(2,1)S(1)} all-to-all(bf16[32,40,512]{2,1,0:T(8,128)(2,1)S(1)} %bitcast.32), channel_id=1, replica_groups=mesh['fsdp'=16,'tok'=32] {'tok'}, dimensions={0} | all-to-all | bytes 2621440 | tf_op jit(solution)/shard_map/all_to_all | solution.py:511
  116.3 3.3 %collective-permute-start.7 = (bf16[128,512]{1,0:T(8,128)(2,1)S(1)}, bf16[128,512]{1,0:T(8,128)(2,1)S(1)}, u32[]{:S(2)}, u32[]{:S(2)}) collective-permute-start(bf16[128,512]{1,0:T(8,128)(2,1)S(1)} %get-tuple-element.19), channel_id=1, source_target_pairs={{0,24},{1,25},{2,26},{3,27},{4,28},{5,29},{6,30},{7,31},{8,16},{9,... | collective-permute-start | bytes 393224 | tf_op jit(solution)/shard_map/ppermute | solution.py:528
  119.7 1.2 shard_map.135
  120.8 3.5 %collective-permute-done.7.recv_ref = bf16[128,512]{1,0:T(8,128)(2,1)S(1)} collective-permute-done((bf16[128,512]{1,0:T(8,128)(2,1)S(1)}, bf16[128,512]{1,0:T(8,128)(2,1)S(1)}, u32[]{:S(2)}, u32[]{:S(2)}) %collective-permute-start.7) | collective-permute-done | bytes 131104 | tf_op jit(solution)/shard_map/ppermute | solution.py:528
  124.4 0.9 shard_map.137
  (55 shorter events, 3.0 us)
Async XLA Ops:
  2.0 7.4 %collective-permute-start.1 = (bf16[64,2048]{1,0:T(8,128)(2,1)S(1)}, bf16[64,2048]{1,0:T(8,128)(2,1)S(1)}, u32[]{:S(2)}, u32[]{:S(2)}) collective-permute-start(bf16[64,2048]{1,0:T(8,128)(2,1)S(1)} %get-tuple-element.13), channel_id=1, source_target_pairs={{0,32},{32,0},{64,96},{96,64},{128,160},{160,128},{192,224},{224,1... | collective-permute-start | bytes 786440 | tf_op jit(solution)/shard_map/ppermute | solution.py:369
  3.9 9.0 %collective-permute-start = (bf16[128,512]{1,0:T(8,128)(2,1)S(1)}, bf16[128,512]{1,0:T(8,128)(2,1)S(1)}, u32[]{:S(2)}, u32[]{:S(2)}) collective-permute-start(bf16[128,512]{1,0:T(8,128)(2,1)S(1)} %get-tuple-element.12), channel_id=1, source_target_pairs={{0,24},{1,25},{2,26},{3,27},{4,28},{5,29},{6,30},{7,31},{8,16},{9,... | collective-permute-start | bytes 393224 | tf_op jit(solution)/shard_map/ppermute | solution.py:464
  9.5 17.9 %copy-start.5 = (bf16[128,2048]{1,0:T(8,128)(2,1)}, bf16[128,2048]{1,0:T(8,128)(2,1)S(1)}, u32[]{:S(2)}) copy-start(bf16[128,2048]{1,0:T(8,128)(2,1)S(1)} %pad_maximum_fusion.chip_any) | copy-start | bytes 1572868
  9.5 20.5 %collective-permute-start.3 = (bf16[128,2048]{1,0:T(8,128)(2,1)S(1)}, bf16[128,2048]{1,0:T(8,128)(2,1)S(1)}, u32[]{:S(2)}, u32[]{:S(2)}) collective-permute-start(bf16[128,2048]{1,0:T(8,128)(2,1)S(1)} %pad_maximum_fusion.chip_any), channel_id=1, source_target_pairs={{0,128},{32,416},{64,192},{96,480},{128,256},{160,32},{192,320},{2... | collective-permute-start | bytes 1572872 | tf_op jit(solution)/shard_map/ppermute | solution.py:366
  14.5 46.9 %all-to-all-start = ((bf16[32,40,512]{2,1,0:T(8,128)(2,1)}), bf16[32,40,512]{2,1,0:T(8,128)(2,1)S(1)}, u32[]{:S(2)}, u32[]{:S(2)}) async-start(bf16[32,40,512]{2,1,0:T(8,128)(2,1)} %bitcast.7), calls=%async_computation | async-start | bytes 2621440 | tf_op jit(solution)/shard_map/all_to_all | solution.py:480
  27.5 11.1 %collective-permute-start.2 = (bf16[128,2048]{1,0:T(8,128)(2,1)S(1)}, bf16[128,2048]{1,0:T(8,128)(2,1)S(1)}, u32[]{:S(2)}, u32[]{:S(2)}) collective-permute-start(bf16[128,2048]{1,0:T(8,128)(2,1)S(1)} %pad_maximum_fusion.chip_any), channel_id=1, source_target_pairs={{0,64},{32,480},{64,128},{96,32},{128,192},{160,96},{192,256},{224... | collective-permute-start | bytes 1572872 | tf_op jit(solution)/shard_map/ppermute | solution.py:366
  30.1 21.7 %copy-start.2 = (bf16[128,2048]{1,0:T(8,128)(2,1)}, bf16[128,2048]{1,0:T(8,128)(2,1)S(1)}, u32[]{:S(2)}) copy-start(bf16[128,2048]{1,0:T(8,128)(2,1)S(1)} %collective-permute-done.3.refs_1_) | copy-start | bytes 1572868
  30.1 21.7 %collective-permute-start.4 = (bf16[128,2048]{1,0:T(8,128)(2,1)S(1)}, bf16[128,2048]{1,0:T(8,128)(2,1)S(1)}, u32[]{:S(2)}, u32[]{:S(2)}) collective-permute-start(bf16[128,2048]{1,0:T(8,128)(2,1)S(1)} %collective-permute-done.3.refs_1_), channel_id=1, source_target_pairs={{0,64},{32,480},{64,128},{96,32},{128,192},{160,96},{192,256},{224... | collective-permute-start | bytes 1572872 | tf_op jit(solution)/shard_map/ppermute | solution.py:366
  32.7 24.1 %copy-start.8 = (bf16[1024]{0:T(1024)(128)(2,1)S(1)}, bf16[1024]{0:T(1024)(128)(2,1)}, u32[]{:S(2)}) copy-start(bf16[1024]{0:T(1024)(128)(2,1)} %param.17) | copy-start | bytes 6148
  32.7 24.6 %copy-start.9 = (s32[1,64]{1,0:T(1,128)S(1)}, s32[1,64]{1,0:T(1,128)}, u32[]{:S(2)}) copy-start(s32[1,64]{1,0:T(1,128)} %param.16) | copy-start | bytes 772
  32.7 25.4 %copy-start.7 = (s32[1,4096]{1,0:T(1,128)S(1)}, s32[1,4096]{1,0:T(1,128)}, u32[]{:S(2)}) copy-start(s32[1,4096]{1,0:T(1,128)} %param.14) | copy-start | bytes 49156
  32.7 28.7 %copy-start.1 = (f32[8]{0:T(128)S(1)}, f32[8]{0:T(128)}, u32[]{:S(2)}) copy-start(f32[8]{0:T(128)} %sharp_ref.1) | copy-start | bytes 100
  32.8 19.0 %collective-permute-start.5 = (bf16[64,2048]{1,0:T(8,128)(2,1)S(1)}, bf16[64,2048]{1,0:T(8,128)(2,1)S(1)}, u32[]{:S(2)}, u32[]{:S(2)}) collective-permute-start(bf16[64,2048]{1,0:T(8,128)(2,1)S(1)} %slice_select_fusion), channel_id=1, source_target_pairs={{0,128},{32,416},{64,192},{96,480},{128,256},{160,32},{192,320},{2... | collective-permute-start | bytes 786440 | tf_op jit(solution)/shard_map/ppermute | solution.py:366
  38.5 13.2 %copy-start.3 = (bf16[128,2048]{1,0:T(8,128)(2,1)}, bf16[128,2048]{1,0:T(8,128)(2,1)S(1)}, u32[]{:S(2)}) copy-start(bf16[128,2048]{1,0:T(8,128)(2,1)S(1)} %collective-permute-done.2.refs_0_) | copy-start | bytes 1572868
  51.8 0.7 copy-start.6
  52.5 0.8 copy-start.4
  54.8 6.7 %collective-permute-start.6 = (bf16[448,2048]{1,0:T(8,128)(2,1)S(1)}, bf16[448,2048]{1,0:T(8,128)(2,1)}, u32[]{:S(2)}, u32[]{:S(2)}) collective-permute-start(bf16[448,2048]{1,0:T(8,128)(2,1)S(1)} %shard_map.133.mine_any), channel_id=1, source_target_pairs={{0,32},{32,0},{64,96},{96,64},{128,160},{160,128},{192,224},{224,1... | collective-permute-start | bytes 5505032 | tf_op jit(solution)/shard_map/ppermute | solution.py:384
  115.8 8.6 %copy-start = (s32[1,1,128]{2,1,0:T(1,128)S(1)}, s32[1,1,128]{2,1,0:T(1,128)}, u32[]{:S(2)}) copy-start(s32[1,1,128]{2,1,0:T(1,128)} %param.13) | copy-start | bytes 1540
  116.3 8.1 %collective-permute-start.7 = (bf16[128,512]{1,0:T(8,128)(2,1)S(1)}, bf16[128,512]{1,0:T(8,128)(2,1)S(1)}, u32[]{:S(2)}, u32[]{:S(2)}) collective-permute-start(bf16[128,512]{1,0:T(8,128)(2,1)S(1)} %get-tuple-element.19), channel_id=1, source_target_pairs={{0,24},{1,25},{2,26},{3,27},{4,28},{5,29},{6,30},{7,31},{8,16},{9,... | collective-permute-start | bytes 393224 | tf_op jit(solution)/shard_map/ppermute | solution.py:528

commit v6 on v5

--- a/solution.py
+++ b/solution.py
@@ -64,8 +64,7 @@
     return dot(a, high, dims) + dot(a, low, dims)
 
 
-def one_hot(row_ref, rows):
-    idx = row_ref[...]
+def one_hot(idx, rows):
     iota = lax.broadcasted_iota(jnp.int32, (rows, idx.shape[1]), 0)
     return jnp.where(iota == idx, 1.0, 0.0).astype(BF16)
 
@@ -96,7 +95,7 @@
         copy.start()
     for copy in copies:
         copy.wait()
-    a = dot(one_hot(order_ref, TOK), x_ref[...], TN).astype(BF16)
+    a = dot(one_hot(order_ref[...], TOK), x_ref[...], TN).astype(BF16)
     lower = side_ref[0] == 0
     left, right = a[:, :HALF], a[:, HALF:]
     keep_ref[...] = jnp.where(lower, left, right)
@@ -116,17 +115,39 @@
         copy.wait()
 
 
+def targets(lists):
+    blocks = SHARDS * NB
+    row = lax.broadcasted_iota(jnp.int32, (16, blocks), 0)
+    named = lax.broadcasted_iota(jnp.int32, (16, blocks), 1)
+    for m in range(KN):
+        named = jnp.where(row == m + 1, lists[m : m + 1, :], named)
+    first = ((named & 1) * TOK + (named >> 1) * CHUNK).astype(F32).astype(BF16)
+    column = lax.broadcasted_iota(jnp.int32, (1, SHARDS * PACK), 1)
+    item = column % PACK // CHUNK
+    block = column // PACK * NB + item // SLOTS
+    mine = lax.broadcasted_iota(jnp.int32, (blocks, SHARDS * PACK), 0) == block
+    spread = dot(first, jnp.where(mine, 1.0, 0.0).astype(BF16), NN)
+    total = (column % CHUNK).astype(F32)
+    for m in range(SLOTS):
+        total = total + jnp.where(item % SLOTS == m, spread[m : m + 1, :], 0.0)
+    return total.astype(jnp.int32)
+
+
+def target_kernel(lists_ref, target_ref):
+    target_ref[...] = targets(lists_ref[...])
+
+
 def pack_kernel(side_ref, target_ref, keep_ref, recv_ref, out_ref):
     lower = side_ref[0] == 0
     keep, recv = keep_ref[...], recv_ref[...]
     table = jnp.concatenate(
         [jnp.where(lower, keep, recv), jnp.where(lower, recv, keep)], axis=0
     )
-    out_ref[...] = dot(one_hot(target_ref, 2 * TOK), table, TN).astype(BF16)
+    out_ref[...] = dot(one_hot(target_ref[...], 2 * TOK), table, TN).astype(BF16)
 
 
 def collect_kernel(side_ref, target_ref, in_ref, keep_ref, send_ref):
-    total = dot(one_hot(target_ref, 2 * TOK), in_ref[...], NN).astype(BF16)
+    total = dot(one_hot(target_ref[...], 2 * TOK), in_ref[...], NN).astype(BF16)
     lower = side_ref[0] == 0
     even, odd = total[:TOK], total[TOK:]
     keep_ref[...] = jnp.where(lower, even, odd)
@@ -139,7 +160,7 @@
     both = jnp.concatenate(
         [jnp.where(lower, keep, recv), jnp.where(lower, recv, keep)], axis=1
     )
-    out_ref[...] = dot(one_hot(order_ref, TOK), both, NN).astype(BF16)
+    out_ref[...] = dot(one_hot(order_ref[...], TOK), both, NN).astype(BF16)
 
 
 def source(dest):
@@ -466,9 +487,8 @@
     lists = bordering_tiles[0].reshape(SHARDS, NB, KN)
     own_blocks = jnp.arange(SHARDS * NB, dtype=jnp.int32).reshape(SHARDS, NB, 1)
     named = jnp.concatenate([own_blocks, lists], axis=2).reshape(SHARDS, ITEMS)
-    target = (named % 2) * TOK + (named // 2) * CHUNK
-    target = (target[:, :, None] + jnp.arange(CHUNK, dtype=jnp.int32)).reshape(
-        1, SHARDS * PACK
+    (target,) = call(
+        target_kernel, [(1, SHARDS * PACK, jnp.int32)], (bordering_tiles[0].T,), [VM], 6 * 10**9
     )
     (packed,) = call(
         pack_kernel,

time: 126 us -> 126 us (level)
    unnamed x22 -> x24, local copies, waits for them, and re-layouts: 2.84 us -> 2.16 us
    pallas_call x7 -> x8, Pallas kernels: 18 us -> 18.2 us  [call(): pl.pallas_call(kernel, out_shape=[place(o[:2], o[2] if len(o) > 2 else BF...]
  transfers between devices with their start and end apart: 9 -> 9, of which waited for: 5 -> 5; matrix products, arithmetic and copies ran while one was open for 3% -> 2% of each run, Pallas kernels for 3% -> 4%
where the time goes in v6:
time: 126 us; the launch traced here: 125 us
  blocking collectives  43.4 us (34%)
  starting transfers between devices  35.5 us (28%)
  waiting for transfers between devices  23 us (18%)
  Pallas kernels  18.2 us (14%)
  local copies, waits for them, and re-layouts  2.8 us (2%)
  other arithmetic  1.4 us (1%)
    all_to_all x1, blocking collectives, body(): lax.all_to_all(leaving.reshape(SHARDS, PACK, HALF), 'tok', split_axis=0,...  43.4 us
    pallas_call x8, Pallas kernels, call(): pl.pallas_call(kernel, out_shape=[place(o[:2], o[2] if len(o) > 2 else BF...  18.2 us
    ppermute x4, waiting for transfers between devices, onward(): return lax.ppermute(part, 'fsdp', pairs)  16.2 us
    all_to_all x1, starting transfers between devices, body(): lax.all_to_all(packed.reshape(SHARDS, PACK, HALF), 'tok', split_axis=0, c...  12.9 us
    ppermute x4, starting transfers between devices, onward(): return lax.ppermute(part, 'fsdp', pairs)  10.7 us
    ppermute x2, starting transfers between devices, body(): recv = lax.ppermute(send, 'tok', partner)  8.01 us
    ppermute x2, waiting for transfers between devices, body(): recv = lax.ppermute(send, 'tok', partner)  4.79 us
  transfers between devices with their start and end apart: 9, of which 5 were waited for; matrix products, arithmetic and copies ran while one was open for 2% of the time, Pallas kernels for 4%

profile of v6, /device:TPU:40, one launch (start us, length us, event | category | flops | bytes accessed | tf_op | source)
XLA Modules:
  0.0 125.3 jit_solution(1896143087134491513)
XLA Ops:
  0.7 1.3 %shard_map.132 = (bf16[128,512]{1,0:T(8,128)(2,1)S(1)}, bf16[128,512]{1,0:T(8,128)(2,1)S(1)}, bf16[64,2048]{1,0:T(8,128)(2,1)S(1)}) custom-call(s32[1]{0:T(128)} %bitcast.2.side_ref, s32[1,128]{1,0:T(1,128)} %bitcast.37, bf16[128,1024]{1,0:T(8,128)(2,1)} %bitcast.39, bf16[64,512]{1,0:T(8,128)(2,1)} %wq_hbm.1, bf16[64,512]{1,0:T(8,128)(2,1)} %wk_hbm.1, ...), custom_call_target="tpu_custom_call" | custom-call | flops 33554432 | bytes 1049092 | tf_op jit(solution)/shard_map/pallas_call | solution.py:370
  2.0 1.9 %collective-permute-start.1 = (bf16[64,2048]{1,0:T(8,128)(2,1)S(1)}, bf16[64,2048]{1,0:T(8,128)(2,1)S(1)}, u32[]{:S(2)}, u32[]{:S(2)}) collective-permute-start(bf16[64,2048]{1,0:T(8,128)(2,1)S(1)} %get-tuple-element.13), channel_id=1, source_target_pairs={{0,32},{32,0},{64,96},{96,64},{128,160},{160,128},{192,224},{224,1... | collective-permute-start | bytes 786440 | tf_op jit(solution)/shard_map/ppermute | solution.py:390
  3.9 4.7 %collective-permute-start = (bf16[128,512]{1,0:T(8,128)(2,1)S(1)}, bf16[128,512]{1,0:T(8,128)(2,1)S(1)}, u32[]{:S(2)}, u32[]{:S(2)}) collective-permute-start(bf16[128,512]{1,0:T(8,128)(2,1)S(1)} %get-tuple-element.12), channel_id=1, source_target_pairs={{0,24},{1,25},{2,26},{3,27},{4,28},{5,29},{6,30},{7,31},{8,16},{9,... | collective-permute-start | bytes 393224 | tf_op jit(solution)/shard_map/ppermute | solution.py:485
  8.7 2.7 %collective-permute-start.3 = (bf16[128,2048]{1,0:T(8,128)(2,1)S(1)}, bf16[128,2048]{1,0:T(8,128)(2,1)S(1)}, u32[]{:S(2)}, u32[]{:S(2)}) collective-permute-start(bf16[128,2048]{1,0:T(8,128)(2,1)S(1)} %pad_maximum_fusion.chip_any), channel_id=1, source_target_pairs={{0,128},{32,416},{64,192},{96,480},{128,256},{160,32},{192,320},{2... | collective-permute-start | bytes 1572872 | tf_op jit(solution)/shard_map/ppermute | solution.py:387
  11.7 1.3 collective-permute-done.recv_ref
  12.9 1.6 %shard_map.133 = bf16[1280,512]{1,0:T(8,128)(2,1)} custom-call(s32[1]{0:T(128)} %bitcast.2.side_ref, s32[1,1280]{1,0:T(1,128)S(1)} %shard_map.131.target_ref, bf16[128,512]{1,0:T(8,128)(2,1)S(1)} %get-tuple-element.11.keep_ref, bf16[128,512]{1,0:T(8,128)(2,1)S(1)} %collective-permute-done.recv_ref), custom_call_target="tpu_custom_call" | custom-call | flops 335544320 | bytes 1577988 | tf_op jit(solution)/shard_map/pallas_call | solution.py:370
  14.5 12.9 %all-to-all-start = ((bf16[32,40,512]{2,1,0:T(8,128)(2,1)}), bf16[32,40,512]{2,1,0:T(8,128)(2,1)S(1)}, u32[]{:S(2)}, u32[]{:S(2)}) async-start(bf16[32,40,512]{2,1,0:T(8,128)(2,1)} %bitcast.8), calls=%async_computation | async-start | bytes 2621440 | tf_op jit(solution)/shard_map/all_to_all | solution.py:500
  27.5 2.6 %collective-permute-start.2 = (bf16[128,2048]{1,0:T(8,128)(2,1)S(1)}, bf16[128,2048]{1,0:T(8,128)(2,1)S(1)}, u32[]{:S(2)}, u32[]{:S(2)}) collective-permute-start(bf16[128,2048]{1,0:T(8,128)(2,1)S(1)} %pad_maximum_fusion.chip_any), channel_id=1, source_target_pairs={{0,64},{32,480},{64,128},{96,32},{128,192},{160,96},{192,256},{224... | collective-permute-start | bytes 1572872 | tf_op jit(solution)/shard_map/ppermute | solution.py:387
  30.1 2.6 %collective-permute-start.4 = (bf16[128,2048]{1,0:T(8,128)(2,1)S(1)}, bf16[128,2048]{1,0:T(8,128)(2,1)S(1)}, u32[]{:S(2)}, u32[]{:S(2)}) collective-permute-start(bf16[128,2048]{1,0:T(8,128)(2,1)S(1)} %collective-permute-done.3.refs_1_), channel_id=1, source_target_pairs={{0,64},{32,480},{64,128},{96,32},{128,192},{160,96},{192,256},{224... | collective-permute-start | bytes 1572872 | tf_op jit(solution)/shard_map/ppermute | solution.py:387
  32.8 2.8 %collective-permute-start.5 = (bf16[64,2048]{1,0:T(8,128)(2,1)S(1)}, bf16[64,2048]{1,0:T(8,128)(2,1)S(1)}, u32[]{:S(2)}, u32[]{:S(2)}) collective-permute-start(bf16[64,2048]{1,0:T(8,128)(2,1)S(1)} %slice_select_fusion), channel_id=1, source_target_pairs={{0,128},{32,416},{64,192},{96,480},{128,256},{160,32},{192,320},{2... | collective-permute-start | bytes 786440 | tf_op jit(solution)/shard_map/ppermute | solution.py:387
  35.6 2.9 %collective-permute-done.2.refs_0_ = bf16[128,2048]{1,0:T(8,128)(2,1)S(1)} collective-permute-done((bf16[128,2048]{1,0:T(8,128)(2,1)S(1)}, bf16[128,2048]{1,0:T(8,128)(2,1)S(1)}, u32[]{:S(2)}, u32[]{:S(2)}) %collective-permute-start.2) | collective-permute-done | bytes 524320 | tf_op jit(solution)/shard_map/ppermute | solution.py:387
  38.5 13.2 %collective-permute-done.5.refs_3_ = bf16[64,2048]{1,0:T(8,128)(2,1)S(1)} collective-permute-done((bf16[64,2048]{1,0:T(8,128)(2,1)S(1)}, bf16[64,2048]{1,0:T(8,128)(2,1)S(1)}, u32[]{:S(2)}, u32[]{:S(2)}) %collective-permute-start.5) | collective-permute-done | bytes 262176 | tf_op jit(solution)/shard_map/ppermute | solution.py:387
  51.8 0.7 copy-done.7
  52.5 0.8 copy-done.5
  53.3 1.5 %shard_map.134.mine_any = bf16[448,2048]{1,0:T(8,128)(2,1)S(1)} custom-call(bf16[128,2048]{1,0:T(8,128)(2,1)} %copy-done.4, bf16[128,2048]{1,0:T(8,128)(2,1)} %copy-done.3, bf16[128,2048]{1,0:T(8,128)(2,1)} %copy-done.5, bf16[64,2048]{1,0:T(8,128)(2,1)} %copy-done.7), custom_call_target="tpu_custom_call" | custom-call | tf_op jit(solution)/shard_map/pallas_call | solution.py:370
  54.8 1.9 %collective-permute-start.6 = (bf16[448,2048]{1,0:T(8,128)(2,1)S(1)}, bf16[448,2048]{1,0:T(8,128)(2,1)}, u32[]{:S(2)}, u32[]{:S(2)}) collective-permute-start(bf16[448,2048]{1,0:T(8,128)(2,1)S(1)} %shard_map.134.mine_any), channel_id=1, source_target_pairs={{0,32},{32,0},{64,96},{96,64},{128,160},{160,128},{192,224},{224,1... | collective-permute-start | bytes 5505032 | tf_op jit(solution)/shard_map/ppermute | solution.py:405
  57.4 0.7 reduce.7
  59.4 2.0 %all-to-all-done = bf16[32,40,512]{2,1,0:T(8,128)(2,1)S(1)} async-done(((bf16[32,40,512]{2,1,0:T(8,128)(2,1)}), bf16[32,40,512]{2,1,0:T(8,128)(2,1)S(1)}, u32[]{:S(2)}, u32[]{:S(2)}) %all-to-all-start) | async-done | bytes 1310752 | tf_op jit(solution)/shard_map/all_to_all | solution.py:500
  61.5 10.9 %shard_map.135 = (bf16[1280,512]{1,0:T(8,128)(2,1)S(1)}, bf16[128,512]{1,0:T(8,128)(2,1)S(1)}, bf16[128,1024]{1,0:T(8,128)(2,1)S(1)}, bf16[1024,512]{1,0:T(8,128)(2,1)S(1)}) custom-call(f32[8]{0:T(128)S(1)} %copy-done.2, s32[2]{0:T(128)S(1)} %pad_add_fusion.1.place_ref, bf16[1280,512]{1,0:T(8,128)(2,1)S(1)} %bitcast.34, bf16[128,2048]{1,0:T(8,128)(2,1)} %copy-done.6, ...), custom_call_target="tpu_custom_call" | custom-call | flops 4000000000 | bytes 8524328 | tf_op jit(solution)/shard_map/pallas_call | solution.py:370
  72.4 43.4 %all_to_all.10 = bf16[32,40,512]{2,1,0:T(8,128)(2,1)S(1)} all-to-all(bf16[32,40,512]{2,1,0:T(8,128)(2,1)S(1)} %bitcast.35), channel_id=1, replica_groups=mesh['fsdp'=16,'tok'=32] {'tok'}, dimensions={0} | all-to-all | bytes 2621440 | tf_op jit(solution)/shard_map/all_to_all | solution.py:531
  116.3 3.3 %collective-permute-start.7 = (bf16[128,512]{1,0:T(8,128)(2,1)S(1)}, bf16[128,512]{1,0:T(8,128)(2,1)S(1)}, u32[]{:S(2)}, u32[]{:S(2)}) collective-permute-start(bf16[128,512]{1,0:T(8,128)(2,1)S(1)} %get-tuple-element.19), channel_id=1, source_target_pairs={{0,24},{1,25},{2,26},{3,27},{4,28},{5,29},{6,30},{7,31},{8,16},{9,... | collective-permute-start | bytes 393224 | tf_op jit(solution)/shard_map/ppermute | solution.py:548
  119.7 1.2 shard_map.136
  120.8 3.5 %collective-permute-done.7.recv_ref = bf16[128,512]{1,0:T(8,128)(2,1)S(1)} collective-permute-done((bf16[128,512]{1,0:T(8,128)(2,1)S(1)}, bf16[128,512]{1,0:T(8,128)(2,1)S(1)}, u32[]{:S(2)}, u32[]{:S(2)}) %collective-permute-start.7) | collective-permute-done | bytes 131104 | tf_op jit(solution)/shard_map/ppermute | solution.py:548
  124.4 0.9 shard_map.138
  (54 shorter events, 2.9 us)
Async XLA Ops:
  0.6 10.8 %copy-start = (s32[1,64,4]{1,2,0:T(4,128)S(1)}, s32[1,64,4]{1,2,0:T(4,128)}, u32[]{:S(2)}) copy-start(s32[1,64,4]{1,2,0:T(4,128)} %param.15) | copy-start | bytes 3076
  2.0 6.6 %collective-permute-start.1 = (bf16[64,2048]{1,0:T(8,128)(2,1)S(1)}, bf16[64,2048]{1,0:T(8,128)(2,1)S(1)}, u32[]{:S(2)}, u32[]{:S(2)}) collective-permute-start(bf16[64,2048]{1,0:T(8,128)(2,1)S(1)} %get-tuple-element.13), channel_id=1, source_target_pairs={{0,32},{32,0},{64,96},{96,64},{128,160},{160,128},{192,224},{224,1... | collective-permute-start | bytes 786440 | tf_op jit(solution)/shard_map/ppermute | solution.py:390
  3.9 9.0 %collective-permute-start = (bf16[128,512]{1,0:T(8,128)(2,1)S(1)}, bf16[128,512]{1,0:T(8,128)(2,1)S(1)}, u32[]{:S(2)}, u32[]{:S(2)}) collective-permute-start(bf16[128,512]{1,0:T(8,128)(2,1)S(1)} %get-tuple-element.12), channel_id=1, source_target_pairs={{0,24},{1,25},{2,26},{3,27},{4,28},{5,29},{6,30},{7,31},{8,16},{9,... | collective-permute-start | bytes 393224 | tf_op jit(solution)/shard_map/ppermute | solution.py:485
  8.7 18.7 %copy-start.6 = (bf16[128,2048]{1,0:T(8,128)(2,1)}, bf16[128,2048]{1,0:T(8,128)(2,1)S(1)}, u32[]{:S(2)}) copy-start(bf16[128,2048]{1,0:T(8,128)(2,1)S(1)} %pad_maximum_fusion.chip_any) | copy-start | bytes 1572868
  8.7 21.3 %collective-permute-start.3 = (bf16[128,2048]{1,0:T(8,128)(2,1)S(1)}, bf16[128,2048]{1,0:T(8,128)(2,1)S(1)}, u32[]{:S(2)}, u32[]{:S(2)}) collective-permute-start(bf16[128,2048]{1,0:T(8,128)(2,1)S(1)} %pad_maximum_fusion.chip_any), channel_id=1, source_target_pairs={{0,128},{32,416},{64,192},{96,480},{128,256},{160,32},{192,320},{2... | collective-permute-start | bytes 1572872 | tf_op jit(solution)/shard_map/ppermute | solution.py:387
  14.5 46.9 %all-to-all-start = ((bf16[32,40,512]{2,1,0:T(8,128)(2,1)}), bf16[32,40,512]{2,1,0:T(8,128)(2,1)S(1)}, u32[]{:S(2)}, u32[]{:S(2)}) async-start(bf16[32,40,512]{2,1,0:T(8,128)(2,1)} %bitcast.8), calls=%async_computation | async-start | bytes 2621440 | tf_op jit(solution)/shard_map/all_to_all | solution.py:500
  27.5 11.1 %collective-permute-start.2 = (bf16[128,2048]{1,0:T(8,128)(2,1)S(1)}, bf16[128,2048]{1,0:T(8,128)(2,1)S(1)}, u32[]{:S(2)}, u32[]{:S(2)}) collective-permute-start(bf16[128,2048]{1,0:T(8,128)(2,1)S(1)} %pad_maximum_fusion.chip_any), channel_id=1, source_target_pairs={{0,64},{32,480},{64,128},{96,32},{128,192},{160,96},{192,256},{224... | collective-permute-start | bytes 1572872 | tf_op jit(solution)/shard_map/ppermute | solution.py:387
  30.1 21.7 %copy-start.3 = (bf16[128,2048]{1,0:T(8,128)(2,1)}, bf16[128,2048]{1,0:T(8,128)(2,1)S(1)}, u32[]{:S(2)}) copy-start(bf16[128,2048]{1,0:T(8,128)(2,1)S(1)} %collective-permute-done.3.refs_1_) | copy-start | bytes 1572868
  30.1 21.7 %collective-permute-start.4 = (bf16[128,2048]{1,0:T(8,128)(2,1)S(1)}, bf16[128,2048]{1,0:T(8,128)(2,1)S(1)}, u32[]{:S(2)}, u32[]{:S(2)}) collective-permute-start(bf16[128,2048]{1,0:T(8,128)(2,1)S(1)} %collective-permute-done.3.refs_1_), channel_id=1, source_target_pairs={{0,64},{32,480},{64,128},{96,32},{128,192},{160,96},{192,256},{224... | collective-permute-start | bytes 1572872 | tf_op jit(solution)/shard_map/ppermute | solution.py:387
  32.7 24.2 %copy-start.9 = (bf16[1024]{0:T(1024)(128)(2,1)S(1)}, bf16[1024]{0:T(1024)(128)(2,1)}, u32[]{:S(2)}) copy-start(bf16[1024]{0:T(1024)(128)(2,1)} %param.17) | copy-start | bytes 6148
  32.7 24.7 %copy-start.10 = (s32[1,64]{1,0:T(1,128)S(1)}, s32[1,64]{1,0:T(1,128)}, u32[]{:S(2)}) copy-start(s32[1,64]{1,0:T(1,128)} %param.16) | copy-start | bytes 772
  32.7 25.5 %copy-start.8 = (s32[1,4096]{1,0:T(1,128)S(1)}, s32[1,4096]{1,0:T(1,128)}, u32[]{:S(2)}) copy-start(s32[1,4096]{1,0:T(1,128)} %param.14) | copy-start | bytes 49156
  32.7 28.7 %copy-start.2 = (f32[8]{0:T(128)S(1)}, f32[8]{0:T(128)}, u32[]{:S(2)}) copy-start(f32[8]{0:T(128)} %sharp_ref.1) | copy-start | bytes 100
  32.8 19.0 %collective-permute-start.5 = (bf16[64,2048]{1,0:T(8,128)(2,1)S(1)}, bf16[64,2048]{1,0:T(8,128)(2,1)S(1)}, u32[]{:S(2)}, u32[]{:S(2)}) collective-permute-start(bf16[64,2048]{1,0:T(8,128)(2,1)S(1)} %slice_select_fusion), channel_id=1, source_target_pairs={{0,128},{32,416},{64,192},{96,480},{128,256},{160,32},{192,320},{2... | collective-permute-start | bytes 786440 | tf_op jit(solution)/shard_map/ppermute | solution.py:387
  38.5 13.2 %copy-start.4 = (bf16[128,2048]{1,0:T(8,128)(2,1)}, bf16[128,2048]{1,0:T(8,128)(2,1)S(1)}, u32[]{:S(2)}) copy-start(bf16[128,2048]{1,0:T(8,128)(2,1)S(1)} %collective-permute-done.2.refs_0_) | copy-start | bytes 1572868
  51.8 0.7 copy-start.7
  52.5 0.8 copy-start.5
  54.8 6.7 %collective-permute-start.6 = (bf16[448,2048]{1,0:T(8,128)(2,1)S(1)}, bf16[448,2048]{1,0:T(8,128)(2,1)}, u32[]{:S(2)}, u32[]{:S(2)}) collective-permute-start(bf16[448,2048]{1,0:T(8,128)(2,1)S(1)} %shard_map.134.mine_any), channel_id=1, source_target_pairs={{0,32},{32,0},{64,96},{96,64},{128,160},{160,128},{192,224},{224,1... | collective-permute-start | bytes 5505032 | tf_op jit(solution)/shard_map/ppermute | solution.py:405
  115.8 8.6 %copy-start.1 = (s32[1,1,128]{2,1,0:T(1,128)S(1)}, s32[1,1,128]{2,1,0:T(1,128)}, u32[]{:S(2)}) copy-start(s32[1,1,128]{2,1,0:T(1,128)} %param.13) | copy-start | bytes 1540
  116.3 8.1 %collective-permute-start.7 = (bf16[128,512]{1,0:T(8,128)(2,1)S(1)}, bf16[128,512]{1,0:T(8,128)(2,1)S(1)}, u32[]{:S(2)}, u32[]{:S(2)}) collective-permute-start(bf16[128,512]{1,0:T(8,128)(2,1)S(1)} %get-tuple-element.19), channel_id=1, source_target_pairs={{0,24},{1,25},{2,26},{3,27},{4,28},{5,29},{6,30},{7,31},{8,16},{9,... | collective-permute-start | bytes 393224 | tf_op jit(solution)/shard_map/ppermute | solution.py:548

commit v7 on v5

--- a/solution.py
+++ b/solution.py
@@ -33,6 +33,7 @@
 SHARE = 64
 CHIP = 2 * SHARE
 HOPS = 3
+PARTS = 5
 
 norm_eps = 1e-05
 head_eps = 1e-06
@@ -116,13 +117,28 @@
         copy.wait()
 
 
-def pack_kernel(side_ref, target_ref, keep_ref, recv_ref, out_ref):
+def pack_kernel(side_ref, target_ref, keep_ref, recv_ref, out_hbm, part_ref, sems):
     lower = side_ref[0] == 0
     keep, recv = keep_ref[...], recv_ref[...]
     table = jnp.concatenate(
         [jnp.where(lower, keep, recv), jnp.where(lower, recv, keep)], axis=0
     )
-    out_ref[...] = dot(one_hot(target_ref, 2 * TOK), table, TN).astype(BF16)
+    rows = SHARDS * PACK // PARTS
+    pick = one_hot(target_ref, 2 * TOK)
+    copies = []
+    for n in range(PARTS):
+        at = slice(n * rows, (n + 1) * rows)
+        part_ref[at, :] = dot(pick[:, at], table, TN).astype(BF16)
+        copies.append(
+            pltpu.make_async_copy(
+                part_ref.at[pl.ds(n * rows, rows), :],
+                out_hbm.at[pl.ds(n * rows, rows), :],
+                sems.at[n],
+            )
+        )
+        copies[-1].start()
+    for copy in copies:
+        copy.wait()
 
 
 def collect_kernel(side_ref, target_ref, in_ref, keep_ref, send_ref):
@@ -171,8 +187,7 @@
     normed_ref,
     rstd_ref,
     xn_ref,
-    k_ref,
-    v_ref,
+    kv_ref,
     gkv_ref,
     gq_ref,
     gh_ref,
@@ -223,8 +238,7 @@
     for copy in copies:
         copy.wait()
     xn = xn_ref[...]
-    k_ref[...] = dot(xn, w_ref[:, HDT : 2 * HDT], NN).astype(BF16)
-    v_ref[...] = dot(xn, w_ref[:, 2 * HDT : 3 * HDT], NN).astype(BF16)
+    kv_ref[...] = dot(xn, w_ref[:, HDT : 3 * HDT], NN).astype(BF16)
     xn_own = jnp.concatenate([xn_ref[pl.ds(b * KEYS, BLOCK), :] for b in range(NB)], axis=0)
     queries = dot(xn_own, w_ref[:, :HDT], NN).astype(BF16)
     up = rolled(up_ref[...])
@@ -257,7 +271,7 @@
     for b in range(NB):
         keys = pl.ds(b * KEYS, KEYS)
         own = slice(b * BLOCK, (b + 1) * BLOCK)
-        kf = k_ref[keys, :].astype(F32)
+        kf = kv_ref[keys, :HDT].astype(F32)
         norm2 = split_dot(head_pick, kf * kf, NT, 1)
         inv_k = 1.0 / jnp.sqrt(norm2 + head_eps)
         allowed = (seen_ref[b : b + 1, :] > 0.0) | diagonal
@@ -266,8 +280,8 @@
             lanes = slice(g * GL, (g + 1) * GL)
             qm = spread(queries[own, lanes])
             gm = spread(grad_attn[own, lanes])
-            k4 = k_ref[keys, lanes]
-            v4 = v_ref[keys, lanes]
+            k4 = kv_ref[keys, lanes]
+            v4 = kv_ref[keys, HDT + g * GL : HDT + (g + 1) * GL]
             qf = qm.astype(F32)
             inv_q = 1.0 / jnp.sqrt(jnp.sum(qf * qf, axis=1, keepdims=True) + head_eps)
             sharp = jnp.concatenate(
@@ -408,8 +422,7 @@
             pltpu.VMEM((ROWS, D), F32),
             pltpu.VMEM((ROWS, 128), F32),
             pltpu.VMEM((ROWS, D), BF16),
-            pltpu.VMEM((ROWS, HDT), BF16),
-            pltpu.VMEM((ROWS, HDT), BF16),
+            pltpu.VMEM((ROWS, D), BF16),
             pltpu.VMEM((ROWS, D), BF16),
             pltpu.VMEM((TOK, HDT), BF16),
             pltpu.VMEM((ROWS, D), F32),
@@ -476,6 +489,11 @@
         (side, target, keep, recv),
         [SM, VM, VM, VM],
         2 * SHARDS * PACK * 2 * TOK * HALF,
+        scratch=[
+            pltpu.VMEM((SHARDS * PACK, HALF), BF16),
+            pltpu.SemaphoreType.DMA((PARTS,)),
+        ],
+        out_spec=HB_SPEC,
     )
     arrived = lax.all_to_all(
         packed.reshape(SHARDS, PACK, HALF), "tok", split_axis=0, concat_axis=0, tiled=True

time: 126 us -> 126 us (level)
  no operation moved by 1% of the time
where the time goes in v7:
time: 126 us; the launch traced here: 125 us
  blocking collectives  43.4 us (34%)
  starting transfers between devices  35.5 us (28%)
  waiting for transfers between devices  22.2 us (18%)
  Pallas kernels  17.8 us (14%)
  local copies, waits for them, and re-layouts  3.7 us (3%)
  other arithmetic  1.54 us (1%)
    all_to_all x1, blocking collectives, body(): lax.all_to_all(leaving.reshape(SHARDS, PACK, HALF), 'tok', split_axis=0,...  43.4 us
    pallas_call x7, Pallas kernels, call(): pl.pallas_call(kernel, out_shape=[place(o[:2], o[2] if len(o) > 2 else BF...  17.8 us
    ppermute x4, waiting for transfers between devices, onward(): return lax.ppermute(part, 'fsdp', pairs)  16.2 us
    all_to_all x1, starting transfers between devices, body(): lax.all_to_all(packed.reshape(SHARDS, PACK, HALF), 'tok', split_axis=0, c...  12.9 us
    ppermute x4, starting transfers between devices, onward(): return lax.ppermute(part, 'fsdp', pairs)  10.7 us
    ppermute x2, starting transfers between devices, body(): recv = lax.ppermute(send, 'tok', partner)  8.01 us
    ppermute x2, waiting for transfers between devices, body(): recv = lax.ppermute(send, 'tok', partner)  3.64 us
    unnamed x22, local copies, waits for them, and re-layouts  2.84 us
  transfers between devices with their start and end apart: 9, of which 5 were waited for; matrix products, arithmetic and copies ran while one was open for 3% of the time, Pallas kernels for 3%

profile of v7, /device:TPU:40, one launch (start us, length us, event | category | flops | bytes accessed | tf_op | source)
XLA Modules:
  0.0 125.1 jit_solution(14899930359925570669)
XLA Ops:
  0.6 1.3 %shard_map.131 = (bf16[128,512]{1,0:T(8,128)(2,1)S(1)}, bf16[128,512]{1,0:T(8,128)(2,1)S(1)}, bf16[64,2048]{1,0:T(8,128)(2,1)S(1)}) custom-call(s32[1]{0:T(128)} %bitcast.2.side_ref, s32[1,128]{1,0:T(1,128)} %bitcast.33, bf16[128,1024]{1,0:T(8,128)(2,1)} %bitcast.36, bf16[64,512]{1,0:T(8,128)(2,1)} %wq_hbm.1, bf16[64,512]{1,0:T(8,128)(2,1)} %wk_hbm.1, ...), custom_call_target="tpu_custom_call" | custom-call | flops 33554432 | bytes 1049092 | tf_op jit(solution)/shard_map/pallas_call | solution.py:363
  2.0 1.9 %collective-permute-start.1 = (bf16[64,2048]{1,0:T(8,128)(2,1)S(1)}, bf16[64,2048]{1,0:T(8,128)(2,1)S(1)}, u32[]{:S(2)}, u32[]{:S(2)}) collective-permute-start(bf16[64,2048]{1,0:T(8,128)(2,1)S(1)} %get-tuple-element.13), channel_id=1, source_target_pairs={{0,32},{32,0},{64,96},{96,64},{128,160},{160,128},{192,224},{224,1... | collective-permute-start | bytes 786440 | tf_op jit(solution)/shard_map/ppermute | solution.py:383
  3.9 4.7 %collective-permute-start = (bf16[128,512]{1,0:T(8,128)(2,1)S(1)}, bf16[128,512]{1,0:T(8,128)(2,1)S(1)}, u32[]{:S(2)}, u32[]{:S(2)}) collective-permute-start(bf16[128,512]{1,0:T(8,128)(2,1)S(1)} %get-tuple-element.12), channel_id=1, source_target_pairs={{0,24},{1,25},{2,26},{3,27},{4,28},{5,29},{6,30},{7,31},{8,16},{9,... | collective-permute-start | bytes 393224 | tf_op jit(solution)/shard_map/ppermute | solution.py:477
  8.6 0.8 copy.33
  9.5 2.7 %collective-permute-start.3 = (bf16[128,2048]{1,0:T(8,128)(2,1)S(1)}, bf16[128,2048]{1,0:T(8,128)(2,1)S(1)}, u32[]{:S(2)}, u32[]{:S(2)}) collective-permute-start(bf16[128,2048]{1,0:T(8,128)(2,1)S(1)} %pad_maximum_fusion.chip_any), channel_id=1, source_target_pairs={{0,128},{32,416},{64,192},{96,480},{128,256},{160,32},{192,320},{2... | collective-permute-start | bytes 1572872 | tf_op jit(solution)/shard_map/ppermute | solution.py:380
  12.9 1.4 %shard_map.132 = bf16[1280,512]{1,0:T(8,128)(2,1)} custom-call(s32[1]{0:T(128)} %bitcast.2.side_ref, s32[1,1280]{1,0:T(1,128)S(1)} %add.66.target_ref, bf16[128,512]{1,0:T(8,128)(2,1)S(1)} %get-tuple-element.11.keep_ref, bf16[128,512]{1,0:T(8,128)(2,1)S(1)} %collective-permute-done.recv_ref), custom_call_target="tpu_custom_call" | custom-call | flops 335544320 | bytes 1577988 | tf_op jit(solution)/shard_map/pallas_call | solution.py:363
  14.3 12.9 %all-to-all-start = ((bf16[32,40,512]{2,1,0:T(8,128)(2,1)}), bf16[32,40,512]{2,1,0:T(8,128)(2,1)S(1)}, u32[]{:S(2)}, u32[]{:S(2)}) async-start(bf16[32,40,512]{2,1,0:T(8,128)(2,1)} %bitcast.35), calls=%async_computation | async-start | bytes 2621440 | tf_op jit(solution)/shard_map/all_to_all | solution.py:498
  27.2 2.6 %collective-permute-start.2 = (bf16[128,2048]{1,0:T(8,128)(2,1)S(1)}, bf16[128,2048]{1,0:T(8,128)(2,1)S(1)}, u32[]{:S(2)}, u32[]{:S(2)}) collective-permute-start(bf16[128,2048]{1,0:T(8,128)(2,1)S(1)} %pad_maximum_fusion.chip_any), channel_id=1, source_target_pairs={{0,64},{32,480},{64,128},{96,32},{128,192},{160,96},{192,256},{224... | collective-permute-start | bytes 1572872 | tf_op jit(solution)/shard_map/ppermute | solution.py:380
  29.9 2.6 %collective-permute-start.4 = (bf16[128,2048]{1,0:T(8,128)(2,1)S(1)}, bf16[128,2048]{1,0:T(8,128)(2,1)S(1)}, u32[]{:S(2)}, u32[]{:S(2)}) collective-permute-start(bf16[128,2048]{1,0:T(8,128)(2,1)S(1)} %collective-permute-done.3.refs_1_), channel_id=1, source_target_pairs={{0,64},{32,480},{64,128},{96,32},{128,192},{160,96},{192,256},{224... | collective-permute-start | bytes 1572872 | tf_op jit(solution)/shard_map/ppermute | solution.py:380
  32.6 2.8 %collective-permute-start.5 = (bf16[64,2048]{1,0:T(8,128)(2,1)S(1)}, bf16[64,2048]{1,0:T(8,128)(2,1)S(1)}, u32[]{:S(2)}, u32[]{:S(2)}) collective-permute-start(bf16[64,2048]{1,0:T(8,128)(2,1)S(1)} %slice_select_fusion), channel_id=1, source_target_pairs={{0,128},{32,416},{64,192},{96,480},{128,256},{160,32},{192,320},{2... | collective-permute-start | bytes 786440 | tf_op jit(solution)/shard_map/ppermute | solution.py:380
  35.4 3.0 %collective-permute-done.2.refs_0_ = bf16[128,2048]{1,0:T(8,128)(2,1)S(1)} collective-permute-done((bf16[128,2048]{1,0:T(8,128)(2,1)S(1)}, bf16[128,2048]{1,0:T(8,128)(2,1)S(1)}, u32[]{:S(2)}, u32[]{:S(2)}) %collective-permute-start.2) | collective-permute-done | bytes 524320 | tf_op jit(solution)/shard_map/ppermute | solution.py:380
  38.3 13.2 %collective-permute-done.5.refs_3_ = bf16[64,2048]{1,0:T(8,128)(2,1)S(1)} collective-permute-done((bf16[64,2048]{1,0:T(8,128)(2,1)S(1)}, bf16[64,2048]{1,0:T(8,128)(2,1)S(1)}, u32[]{:S(2)}, u32[]{:S(2)}) %collective-permute-start.5) | collective-permute-done | bytes 262176 | tf_op jit(solution)/shard_map/ppermute | solution.py:380
  51.6 0.7 copy-done.6
  52.3 0.8 copy-done.4
  53.1 1.5 %shard_map.133.mine_any = bf16[448,2048]{1,0:T(8,128)(2,1)S(1)} custom-call(bf16[128,2048]{1,0:T(8,128)(2,1)} %copy-done.3, bf16[128,2048]{1,0:T(8,128)(2,1)} %copy-done.2, bf16[128,2048]{1,0:T(8,128)(2,1)} %copy-done.4, bf16[64,2048]{1,0:T(8,128)(2,1)} %copy-done.6), custom_call_target="tpu_custom_call" | custom-call | tf_op jit(solution)/shard_map/pallas_call | solution.py:363
  54.5 1.9 %collective-permute-start.6 = (bf16[448,2048]{1,0:T(8,128)(2,1)S(1)}, bf16[448,2048]{1,0:T(8,128)(2,1)}, u32[]{:S(2)}, u32[]{:S(2)}) collective-permute-start(bf16[448,2048]{1,0:T(8,128)(2,1)S(1)} %shard_map.133.mine_any), channel_id=1, source_target_pairs={{0,32},{32,0},{64,96},{96,64},{128,160},{160,128},{192,224},{224,1... | collective-permute-start | bytes 5505032 | tf_op jit(solution)/shard_map/ppermute | solution.py:398
  57.1 0.7 reduce.7
  58.9 2.3 %all-to-all-done = bf16[32,40,512]{2,1,0:T(8,128)(2,1)S(1)} async-done(((bf16[32,40,512]{2,1,0:T(8,128)(2,1)}), bf16[32,40,512]{2,1,0:T(8,128)(2,1)S(1)}, u32[]{:S(2)}, u32[]{:S(2)}) %all-to-all-start) | async-done | bytes 1310752 | tf_op jit(solution)/shard_map/all_to_all | solution.py:498
  61.2 11.0 %shard_map.134 = (bf16[1280,512]{1,0:T(8,128)(2,1)S(1)}, bf16[128,512]{1,0:T(8,128)(2,1)S(1)}, bf16[128,1024]{1,0:T(8,128)(2,1)S(1)}, bf16[1024,512]{1,0:T(8,128)(2,1)S(1)}) custom-call(f32[8]{0:T(128)S(1)} %copy-done.1, s32[2]{0:T(128)S(1)} %pad_add_fusion.1.place_ref, bf16[1280,512]{1,0:T(8,128)(2,1)S(1)} %bitcast.31, bf16[128,2048]{1,0:T(8,128)(2,1)} %copy-done.5, ...), custom_call_target="tpu_custom_call" | custom-call | flops 4000000000 | bytes 8524328 | tf_op jit(solution)/shard_map/pallas_call | solution.py:363
  72.2 43.4 %all_to_all.10 = bf16[32,40,512]{2,1,0:T(8,128)(2,1)S(1)} all-to-all(bf16[32,40,512]{2,1,0:T(8,128)(2,1)S(1)} %bitcast.32), channel_id=1, replica_groups=mesh['fsdp'=16,'tok'=32] {'tok'}, dimensions={0} | all-to-all | bytes 2621440 | tf_op jit(solution)/shard_map/all_to_all | solution.py:529
  116.1 3.3 %collective-permute-start.7 = (bf16[128,512]{1,0:T(8,128)(2,1)S(1)}, bf16[128,512]{1,0:T(8,128)(2,1)S(1)}, u32[]{:S(2)}, u32[]{:S(2)}) collective-permute-start(bf16[128,512]{1,0:T(8,128)(2,1)S(1)} %get-tuple-element.19), channel_id=1, source_target_pairs={{0,24},{1,25},{2,26},{3,27},{4,28},{5,29},{6,30},{7,31},{8,16},{9,... | collective-permute-start | bytes 393224 | tf_op jit(solution)/shard_map/ppermute | solution.py:546
  119.5 1.2 shard_map.135
  120.7 3.5 %collective-permute-done.7.recv_ref = bf16[128,512]{1,0:T(8,128)(2,1)S(1)} collective-permute-done((bf16[128,512]{1,0:T(8,128)(2,1)S(1)}, bf16[128,512]{1,0:T(8,128)(2,1)S(1)}, u32[]{:S(2)}, u32[]{:S(2)}) %collective-permute-start.7) | collective-permute-done | bytes 131104 | tf_op jit(solution)/shard_map/ppermute | solution.py:546
  124.2 0.9 shard_map.137
  (55 shorter events, 3.0 us)
Async XLA Ops:
  2.0 7.4 %collective-permute-start.1 = (bf16[64,2048]{1,0:T(8,128)(2,1)S(1)}, bf16[64,2048]{1,0:T(8,128)(2,1)S(1)}, u32[]{:S(2)}, u32[]{:S(2)}) collective-permute-start(bf16[64,2048]{1,0:T(8,128)(2,1)S(1)} %get-tuple-element.13), channel_id=1, source_target_pairs={{0,32},{32,0},{64,96},{96,64},{128,160},{160,128},{192,224},{224,1... | collective-permute-start | bytes 786440 | tf_op jit(solution)/shard_map/ppermute | solution.py:383
  3.9 9.0 %collective-permute-start = (bf16[128,512]{1,0:T(8,128)(2,1)S(1)}, bf16[128,512]{1,0:T(8,128)(2,1)S(1)}, u32[]{:S(2)}, u32[]{:S(2)}) collective-permute-start(bf16[128,512]{1,0:T(8,128)(2,1)S(1)} %get-tuple-element.12), channel_id=1, source_target_pairs={{0,24},{1,25},{2,26},{3,27},{4,28},{5,29},{6,30},{7,31},{8,16},{9,... | collective-permute-start | bytes 393224 | tf_op jit(solution)/shard_map/ppermute | solution.py:477
  9.5 17.7 %copy-start.5 = (bf16[128,2048]{1,0:T(8,128)(2,1)}, bf16[128,2048]{1,0:T(8,128)(2,1)S(1)}, u32[]{:S(2)}) copy-start(bf16[128,2048]{1,0:T(8,128)(2,1)S(1)} %pad_maximum_fusion.chip_any) | copy-start | bytes 1572868
  9.5 20.3 %collective-permute-start.3 = (bf16[128,2048]{1,0:T(8,128)(2,1)S(1)}, bf16[128,2048]{1,0:T(8,128)(2,1)S(1)}, u32[]{:S(2)}, u32[]{:S(2)}) collective-permute-start(bf16[128,2048]{1,0:T(8,128)(2,1)S(1)} %pad_maximum_fusion.chip_any), channel_id=1, source_target_pairs={{0,128},{32,416},{64,192},{96,480},{128,256},{160,32},{192,320},{2... | collective-permute-start | bytes 1572872 | tf_op jit(solution)/shard_map/ppermute | solution.py:380
  14.3 46.9 %all-to-all-start = ((bf16[32,40,512]{2,1,0:T(8,128)(2,1)}), bf16[32,40,512]{2,1,0:T(8,128)(2,1)S(1)}, u32[]{:S(2)}, u32[]{:S(2)}) async-start(bf16[32,40,512]{2,1,0:T(8,128)(2,1)} %bitcast.35), calls=%async_computation | async-start | bytes 2621440 | tf_op jit(solution)/shard_map/all_to_all | solution.py:498
  27.2 11.1 %collective-permute-start.2 = (bf16[128,2048]{1,0:T(8,128)(2,1)S(1)}, bf16[128,2048]{1,0:T(8,128)(2,1)S(1)}, u32[]{:S(2)}, u32[]{:S(2)}) collective-permute-start(bf16[128,2048]{1,0:T(8,128)(2,1)S(1)} %pad_maximum_fusion.chip_any), channel_id=1, source_target_pairs={{0,64},{32,480},{64,128},{96,32},{128,192},{160,96},{192,256},{224... | collective-permute-start | bytes 1572872 | tf_op jit(solution)/shard_map/ppermute | solution.py:380
  29.9 21.7 %copy-start.2 = (bf16[128,2048]{1,0:T(8,128)(2,1)}, bf16[128,2048]{1,0:T(8,128)(2,1)S(1)}, u32[]{:S(2)}) copy-start(bf16[128,2048]{1,0:T(8,128)(2,1)S(1)} %collective-permute-done.3.refs_1_) | copy-start | bytes 1572868
  29.9 21.7 %collective-permute-start.4 = (bf16[128,2048]{1,0:T(8,128)(2,1)S(1)}, bf16[128,2048]{1,0:T(8,128)(2,1)S(1)}, u32[]{:S(2)}, u32[]{:S(2)}) collective-permute-start(bf16[128,2048]{1,0:T(8,128)(2,1)S(1)} %collective-permute-done.3.refs_1_), channel_id=1, source_target_pairs={{0,64},{32,480},{64,128},{96,32},{128,192},{160,96},{192,256},{224... | collective-permute-start | bytes 1572872 | tf_op jit(solution)/shard_map/ppermute | solution.py:380
  32.5 24.1 %copy-start.8 = (bf16[1024]{0:T(1024)(128)(2,1)S(1)}, bf16[1024]{0:T(1024)(128)(2,1)}, u32[]{:S(2)}) copy-start(bf16[1024]{0:T(1024)(128)(2,1)} %param.17) | copy-start | bytes 6148
  32.5 24.6 %copy-start.9 = (s32[1,64]{1,0:T(1,128)S(1)}, s32[1,64]{1,0:T(1,128)}, u32[]{:S(2)}) copy-start(s32[1,64]{1,0:T(1,128)} %param.16) | copy-start | bytes 772
  32.5 25.4 %copy-start.7 = (s32[1,4096]{1,0:T(1,128)S(1)}, s32[1,4096]{1,0:T(1,128)}, u32[]{:S(2)}) copy-start(s32[1,4096]{1,0:T(1,128)} %param.14) | copy-start | bytes 49156
  32.5 28.7 %copy-start.1 = (f32[8]{0:T(128)S(1)}, f32[8]{0:T(128)}, u32[]{:S(2)}) copy-start(f32[8]{0:T(128)} %sharp_ref.1) | copy-start | bytes 100
  32.6 19.0 %collective-permute-start.5 = (bf16[64,2048]{1,0:T(8,128)(2,1)S(1)}, bf16[64,2048]{1,0:T(8,128)(2,1)S(1)}, u32[]{:S(2)}, u32[]{:S(2)}) collective-permute-start(bf16[64,2048]{1,0:T(8,128)(2,1)S(1)} %slice_select_fusion), channel_id=1, source_target_pairs={{0,128},{32,416},{64,192},{96,480},{128,256},{160,32},{192,320},{2... | collective-permute-start | bytes 786440 | tf_op jit(solution)/shard_map/ppermute | solution.py:380
  38.3 13.2 %copy-start.3 = (bf16[128,2048]{1,0:T(8,128)(2,1)}, bf16[128,2048]{1,0:T(8,128)(2,1)S(1)}, u32[]{:S(2)}) copy-start(bf16[128,2048]{1,0:T(8,128)(2,1)S(1)} %collective-permute-done.2.refs_0_) | copy-start | bytes 1572868
  51.6 0.7 copy-start.6
  52.3 0.8 copy-start.4
  54.5 6.7 %collective-permute-start.6 = (bf16[448,2048]{1,0:T(8,128)(2,1)S(1)}, bf16[448,2048]{1,0:T(8,128)(2,1)}, u32[]{:S(2)}, u32[]{:S(2)}) collective-permute-start(bf16[448,2048]{1,0:T(8,128)(2,1)S(1)} %shard_map.133.mine_any), channel_id=1, source_target_pairs={{0,32},{32,0},{64,96},{96,64},{128,160},{160,128},{192,224},{224,1... | collective-permute-start | bytes 5505032 | tf_op jit(solution)/shard_map/ppermute | solution.py:398
  115.6 8.6 %copy-start = (s32[1,1,128]{2,1,0:T(1,128)S(1)}, s32[1,1,128]{2,1,0:T(1,128)}, u32[]{:S(2)}) copy-start(s32[1,1,128]{2,1,0:T(1,128)} %param.13) | copy-start | bytes 1540
  116.1 8.1 %collective-permute-start.7 = (bf16[128,512]{1,0:T(8,128)(2,1)S(1)}, bf16[128,512]{1,0:T(8,128)(2,1)S(1)}, u32[]{:S(2)}, u32[]{:S(2)}) collective-permute-start(bf16[128,512]{1,0:T(8,128)(2,1)S(1)} %get-tuple-element.19), channel_id=1, source_target_pairs={{0,24},{1,25},{2,26},{3,27},{4,28},{5,29},{6,30},{7,31},{8,16},{9,... | collective-permute-start | bytes 393224 | tf_op jit(solution)/shard_map/ppermute | solution.py:546

commit v8 on v5

--- a/solution.py
+++ b/solution.py
@@ -357,7 +357,7 @@
     )(*args)
 
 
-def gather_weights(share, place):
+def gather_weights(share, place, recv):
     members = 2 * CHIPS
     sibling = [(i, i ^ 1) for i in range(members)]
 
@@ -370,6 +370,7 @@
     chip = jnp.concatenate(
         [jnp.where(first, share, beside), jnp.where(first, beside, share)], axis=0
     )
+    chip, recv = lax.optimization_barrier((chip, recv))
     near, far = onward(chip, 1), onward(chip, 2)
     half = jnp.where(first, far[:SHARE], far[SHARE:])
     pieces = [near, far, onward(far, 1), onward(half, 2)]
@@ -381,7 +382,7 @@
         0,
         scratch=[pltpu.SemaphoreType.DMA((HOPS + 1,))],
     )
-    return chip, mine, lax.ppermute(mine, "fsdp", sibling)
+    return chip, mine, lax.ppermute(mine, "fsdp", sibling), recv
 
 
 def main_call(sharpness_coefficient, place, arrived, chip, mine, other, upstream_derivative, gain, seen):
@@ -460,8 +461,8 @@
     )
     member = lax.axis_index("fsdp").astype(jnp.int32)
     place = jnp.stack([member // 2, member % 2])
-    chip, mine, other = gather_weights(share, place)
     recv = lax.ppermute(send, "tok", partner)
+    chip, mine, other, recv = gather_weights(share, place, recv)
 
     lists = bordering_tiles[0].reshape(SHARDS, NB, KN)
     own_blocks = jnp.arange(SHARDS * NB, dtype=jnp.int32).reshape(SHARDS, NB, 1)

time: 126 us -> 131 us (1.040)
  the two profiles are of different devices: /device:TPU:40 before, /device:TPU:64 now
where the time goes in v8:
time: 131 us
  blocking collectives  40.4 us (31%)
  starting transfers between devices  39.4 us (30%)
  waiting for transfers between devices  25.7 us (20%)
  Pallas kernels  17.9 us (14%)
  local copies, waits for them, and re-layouts  3.71 us (3%)
  other arithmetic  2.35 us (2%)
    all_to_all x1, blocking collectives, body(): lax.all_to_all(leaving.reshape(SHARDS, PACK, HALF), 'tok', split_axis=0,...  40.4 us
    pallas_call x7, Pallas kernels, call(): pl.pallas_call(kernel, out_shape=[place(o[:2], o[2] if len(o) > 2 else BF...  17.9 us
    ppermute x4, starting transfers between devices, onward(): return lax.ppermute(part, 'fsdp', pairs)  15.5 us
    all_to_all x1, starting transfers between devices, body(): lax.all_to_all(packed.reshape(SHARDS, PACK, HALF), 'tok', split_axis=0, c...  12.3 us
    ppermute x4, waiting for transfers between devices, onward(): return lax.ppermute(part, 'fsdp', pairs)  10.3 us
    all_to_all x1, waiting for transfers between devices, body(): lax.all_to_all(packed.reshape(SHARDS, PACK, HALF), 'tok', split_axis=0, c...  9.01 us
    ppermute x2, starting transfers between devices, body(): recv = lax.ppermute(send, 'tok', partner)  7.74 us
    ppermute x2, waiting for transfers between devices, body(): recv = lax.ppermute(send, 'tok', partner)  6.41 us
  transfers between devices with their start and end apart: 9, of which 4 were waited for; matrix products, arithmetic and copies ran while one was open for 4% of the time, Pallas kernels for 3%

profile of v8, /device:TPU:64, one launch (start us, length us, event | category | flops | bytes accessed | tf_op | source)
XLA Modules:
  0.0 130.7 jit_solution(7231940562788281058)
XLA Ops:
  0.6 1.3 %shard_map.131 = (bf16[128,512]{1,0:T(8,128)(2,1)S(1)}, bf16[128,512]{1,0:T(8,128)(2,1)S(1)}, bf16[64,2048]{1,0:T(8,128)(2,1)S(1)}) custom-call(s32[1]{0:T(128)} %bitcast.2.side_ref, s32[1,128]{1,0:T(1,128)} %bitcast.33, bf16[128,1024]{1,0:T(8,128)(2,1)} %bitcast.35, bf16[64,512]{1,0:T(8,128)(2,1)} %wq_hbm.1, bf16[64,512]{1,0:T(8,128)(2,1)} %wk_hbm.1, ...), custom_call_target="tpu_custom_call" | custom-call | flops 33554432 | bytes 1049092 | tf_op jit(solution)/shard_map/pallas_call | solution.py:349
  2.0 1.9 %collective-permute-start = (bf16[64,2048]{1,0:T(8,128)(2,1)S(1)}, bf16[64,2048]{1,0:T(8,128)(2,1)S(1)}, u32[]{:S(2)}, u32[]{:S(2)}) collective-permute-start(bf16[64,2048]{1,0:T(8,128)(2,1)S(1)} %get-tuple-element.14), channel_id=1, source_target_pairs={{0,32},{32,0},{64,96},{96,64},{128,160},{160,128},{192,224},{224,1... | collective-permute-start | bytes 786440 | tf_op jit(solution)/shard_map/ppermute | solution.py:369
  3.9 4.7 %collective-permute-start.1 = (bf16[128,512]{1,0:T(8,128)(2,1)S(1)}, bf16[128,512]{1,0:T(8,128)(2,1)S(1)}, u32[]{:S(2)}, u32[]{:S(2)}) collective-permute-start(bf16[128,512]{1,0:T(8,128)(2,1)S(1)} %get-tuple-element.15), channel_id=1, source_target_pairs={{0,24},{1,25},{2,26},{3,27},{4,28},{5,29},{6,30},{7,31},{8,16},{9,... | collective-permute-start | bytes 393224 | tf_op jit(solution)/shard_map/ppermute | solution.py:464
  8.6 0.8 copy.33
  9.5 0.9 pad_maximum_fusion.chip_any
  10.3 2.6 %collective-permute-done.1.recv_ref = bf16[128,512]{1,0:T(8,128)(2,1)S(1)} collective-permute-done((bf16[128,512]{1,0:T(8,128)(2,1)S(1)}, bf16[128,512]{1,0:T(8,128)(2,1)S(1)}, u32[]{:S(2)}, u32[]{:S(2)}) %collective-permute-start.1) | collective-permute-done | bytes 131104 | tf_op jit(solution)/shard_map/ppermute | solution.py:464
  12.9 4.5 %collective-permute-start.3 = (bf16[128,2048]{1,0:T(8,128)(2,1)}, bf16[128,2048]{1,0:T(8,128)(2,1)S(1)}, u32[]{:S(2)}, u32[]{:S(2)}) collective-permute-start(bf16[128,2048]{1,0:T(8,128)(2,1)} %pad_maximum_fusion.chip_any), channel_id=1, source_target_pairs={{0,128},{32,416},{64,192},{96,480},{128,256},{160,32},{192,320},{2... | collective-permute-start | bytes 1572872 | tf_op jit(solution)/shard_map/ppermute | solution.py:366
  18.0 3.5 %collective-permute-start.2 = (bf16[128,2048]{1,0:T(8,128)(2,1)}, bf16[128,2048]{1,0:T(8,128)(2,1)S(1)}, u32[]{:S(2)}, u32[]{:S(2)}) collective-permute-start(bf16[128,2048]{1,0:T(8,128)(2,1)} %pad_maximum_fusion.chip_any), channel_id=1, source_target_pairs={{0,64},{32,480},{64,128},{96,32},{128,192},{160,96},{192,256},{224... | collective-permute-start | bytes 1572872 | tf_op jit(solution)/shard_map/ppermute | solution.py:366
  21.5 1.6 %shard_map.132 = bf16[1280,512]{1,0:T(8,128)(2,1)} custom-call(s32[1]{0:T(128)} %bitcast.2.side_ref, s32[1,1280]{1,0:T(1,128)S(1)} %add.66.target_ref, bf16[128,512]{1,0:T(8,128)(2,1)S(1)} %get-tuple-element.13.keep_ref, bf16[128,512]{1,0:T(8,128)(2,1)S(1)} %collective-permute-done.1.recv_ref), custom_call_target="tpu_custom_call" | custom-call | flops 335544320 | bytes 1577988 | tf_op jit(solution)/shard_map/pallas_call | solution.py:349
  23.1 12.3 %all-to-all-start = ((bf16[32,40,512]{2,1,0:T(8,128)(2,1)}), bf16[32,40,512]{2,1,0:T(8,128)(2,1)S(1)}, u32[]{:S(2)}, u32[]{:S(2)}) async-start(bf16[32,40,512]{2,1,0:T(8,128)(2,1)} %bitcast.7), calls=%async_computation | async-start | bytes 2621440 | tf_op jit(solution)/shard_map/all_to_all | solution.py:481
  35.5 4.7 %collective-permute-start.4 = (bf16[128,2048]{1,0:T(8,128)(2,1)S(1)}, bf16[128,2048]{1,0:T(8,128)(2,1)S(1)}, u32[]{:S(2)}, u32[]{:S(2)}) collective-permute-start(bf16[128,2048]{1,0:T(8,128)(2,1)S(1)} %collective-permute-done.3.refs_1_), channel_id=1, source_target_pairs={{0,64},{32,480},{64,128},{96,32},{128,192},{160,96},{192,256},{224... | collective-permute-start | bytes 1572872 | tf_op jit(solution)/shard_map/ppermute | solution.py:366
  40.2 2.8 %collective-permute-start.5 = (bf16[64,2048]{1,0:T(8,128)(2,1)S(1)}, bf16[64,2048]{1,0:T(8,128)(2,1)S(1)}, u32[]{:S(2)}, u32[]{:S(2)}) collective-permute-start(bf16[64,2048]{1,0:T(8,128)(2,1)S(1)} %slice_select_fusion), channel_id=1, source_target_pairs={{0,128},{32,416},{64,192},{96,480},{128,256},{160,32},{192,320},{2... | collective-permute-start | bytes 786440 | tf_op jit(solution)/shard_map/ppermute | solution.py:366
  43.1 10.3 %collective-permute-done.5.refs_3_ = bf16[64,2048]{1,0:T(8,128)(2,1)S(1)} collective-permute-done((bf16[64,2048]{1,0:T(8,128)(2,1)S(1)}, bf16[64,2048]{1,0:T(8,128)(2,1)S(1)}, u32[]{:S(2)}, u32[]{:S(2)}) %collective-permute-start.5) | collective-permute-done | bytes 262176 | tf_op jit(solution)/shard_map/ppermute | solution.py:366
  53.4 0.7 copy-done.5
  54.1 0.8 copy-done.4
  54.9 1.5 %shard_map.133.mine_any = bf16[448,2048]{1,0:T(8,128)(2,1)S(1)} custom-call(bf16[128,2048]{1,0:T(8,128)(2,1)} %copy-done.3, bf16[128,2048]{1,0:T(8,128)(2,1)} %copy-done.2, bf16[128,2048]{1,0:T(8,128)(2,1)} %copy-done.4, bf16[64,2048]{1,0:T(8,128)(2,1)} %copy-done.5), custom_call_target="tpu_custom_call" | custom-call | tf_op jit(solution)/shard_map/pallas_call | solution.py:349
  56.4 1.9 %collective-permute-start.6 = (bf16[448,2048]{1,0:T(8,128)(2,1)S(1)}, bf16[448,2048]{1,0:T(8,128)(2,1)}, u32[]{:S(2)}, u32[]{:S(2)}) collective-permute-start(bf16[448,2048]{1,0:T(8,128)(2,1)S(1)} %shard_map.133.mine_any), channel_id=1, source_target_pairs={{0,32},{32,0},{64,96},{96,64},{128,160},{160,128},{192,224},{224,1... | collective-permute-start | bytes 5505032 | tf_op jit(solution)/shard_map/ppermute | solution.py:385
  60.8 9.0 %all-to-all-done = bf16[32,40,512]{2,1,0:T(8,128)(2,1)S(1)} async-done(((bf16[32,40,512]{2,1,0:T(8,128)(2,1)}), bf16[32,40,512]{2,1,0:T(8,128)(2,1)S(1)}, u32[]{:S(2)}, u32[]{:S(2)}) %all-to-all-start) | async-done | bytes 1310752 | tf_op jit(solution)/shard_map/all_to_all | solution.py:481
  69.8 10.9 %shard_map.134 = (bf16[1280,512]{1,0:T(8,128)(2,1)S(1)}, bf16[128,512]{1,0:T(8,128)(2,1)S(1)}, bf16[128,1024]{1,0:T(8,128)(2,1)S(1)}, bf16[1024,512]{1,0:T(8,128)(2,1)S(1)}) custom-call(f32[8]{0:T(128)S(1)} %copy-done.1, s32[2]{0:T(128)S(1)} %pad_add_fusion.1.place_ref, bf16[1280,512]{1,0:T(8,128)(2,1)S(1)} %bitcast.31, ...), custom_call_target="tpu_custom_call" | custom-call | flops 4000000000 | bytes 8524328 | tf_op jit(solution)/shard_map/pallas_call | solution.py:349
  80.7 40.4 %all_to_all.10 = bf16[32,40,512]{2,1,0:T(8,128)(2,1)S(1)} all-to-all(bf16[32,40,512]{2,1,0:T(8,128)(2,1)S(1)} %bitcast.32), channel_id=1, replica_groups=mesh['fsdp'=16,'tok'=32] {'tok'}, dimensions={0} | all-to-all | bytes 2621440 | tf_op jit(solution)/shard_map/all_to_all | solution.py:512
  121.7 3.1 %collective-permute-start.7 = (bf16[128,512]{1,0:T(8,128)(2,1)S(1)}, bf16[128,512]{1,0:T(8,128)(2,1)S(1)}, u32[]{:S(2)}, u32[]{:S(2)}) collective-permute-start(bf16[128,512]{1,0:T(8,128)(2,1)S(1)} %get-tuple-element.23), channel_id=1, source_target_pairs={{0,24},{1,25},{2,26},{3,27},{4,28},{5,29},{6,30},{7,31},{8,16},{9,... | collective-permute-start | bytes 393224 | tf_op jit(solution)/shard_map/ppermute | solution.py:529
  124.8 1.2 shard_map.135
  126.0 3.8 %collective-permute-done.7.recv_ref = bf16[128,512]{1,0:T(8,128)(2,1)S(1)} collective-permute-done((bf16[128,512]{1,0:T(8,128)(2,1)S(1)}, bf16[128,512]{1,0:T(8,128)(2,1)S(1)}, u32[]{:S(2)}, u32[]{:S(2)}) %collective-permute-start.7) | collective-permute-done | bytes 131104 | tf_op jit(solution)/shard_map/ppermute | solution.py:529
  129.8 0.9 shard_map.137
  (53 shorter events, 3.6 us)
Async XLA Ops:
  2.0 7.4 %collective-permute-start = (bf16[64,2048]{1,0:T(8,128)(2,1)S(1)}, bf16[64,2048]{1,0:T(8,128)(2,1)S(1)}, u32[]{:S(2)}, u32[]{:S(2)}) collective-permute-start(bf16[64,2048]{1,0:T(8,128)(2,1)S(1)} %get-tuple-element.14), channel_id=1, source_target_pairs={{0,32},{32,0},{64,96},{96,64},{128,160},{160,128},{192,224},{224,1... | collective-permute-start | bytes 786440 | tf_op jit(solution)/shard_map/ppermute | solution.py:369
  3.9 9.0 %collective-permute-start.1 = (bf16[128,512]{1,0:T(8,128)(2,1)S(1)}, bf16[128,512]{1,0:T(8,128)(2,1)S(1)}, u32[]{:S(2)}, u32[]{:S(2)}) collective-permute-start(bf16[128,512]{1,0:T(8,128)(2,1)S(1)} %get-tuple-element.15), channel_id=1, source_target_pairs={{0,24},{1,25},{2,26},{3,27},{4,28},{5,29},{6,30},{7,31},{8,16},{9,... | collective-permute-start | bytes 393224 | tf_op jit(solution)/shard_map/ppermute | solution.py:464
  12.9 22.5 %collective-permute-start.3 = (bf16[128,2048]{1,0:T(8,128)(2,1)}, bf16[128,2048]{1,0:T(8,128)(2,1)S(1)}, u32[]{:S(2)}, u32[]{:S(2)}) collective-permute-start(bf16[128,2048]{1,0:T(8,128)(2,1)} %pad_maximum_fusion.chip_any), channel_id=1, source_target_pairs={{0,128},{32,416},{64,192},{96,480},{128,256},{160,32},{192,320},{2... | collective-permute-start | bytes 1572872 | tf_op jit(solution)/shard_map/ppermute | solution.py:366
  18.0 25.1 %collective-permute-start.2 = (bf16[128,2048]{1,0:T(8,128)(2,1)}, bf16[128,2048]{1,0:T(8,128)(2,1)S(1)}, u32[]{:S(2)}, u32[]{:S(2)}) collective-permute-start(bf16[128,2048]{1,0:T(8,128)(2,1)} %pad_maximum_fusion.chip_any), channel_id=1, source_target_pairs={{0,64},{32,480},{64,128},{96,32},{128,192},{160,96},{192,256},{224... | collective-permute-start | bytes 1572872 | tf_op jit(solution)/shard_map/ppermute | solution.py:366
  23.1 46.7 %all-to-all-start = ((bf16[32,40,512]{2,1,0:T(8,128)(2,1)}), bf16[32,40,512]{2,1,0:T(8,128)(2,1)S(1)}, u32[]{:S(2)}, u32[]{:S(2)}) async-start(bf16[32,40,512]{2,1,0:T(8,128)(2,1)} %bitcast.7), calls=%async_computation | async-start | bytes 2621440 | tf_op jit(solution)/shard_map/all_to_all | solution.py:481
  35.4 18.0 %copy-start.2 = (bf16[128,2048]{1,0:T(8,128)(2,1)}, bf16[128,2048]{1,0:T(8,128)(2,1)S(1)}, u32[]{:S(2)}) copy-start(bf16[128,2048]{1,0:T(8,128)(2,1)S(1)} %collective-permute-done.3.refs_1_) | copy-start | bytes 1572868
  35.5 18.0 %collective-permute-start.4 = (bf16[128,2048]{1,0:T(8,128)(2,1)S(1)}, bf16[128,2048]{1,0:T(8,128)(2,1)S(1)}, u32[]{:S(2)}, u32[]{:S(2)}) collective-permute-start(bf16[128,2048]{1,0:T(8,128)(2,1)S(1)} %collective-permute-done.3.refs_1_), channel_id=1, source_target_pairs={{0,64},{32,480},{64,128},{96,32},{128,192},{160,96},{192,256},{224... | collective-permute-start | bytes 1572872 | tf_op jit(solution)/shard_map/ppermute | solution.py:366
  40.2 18.3 %copy-start.7 = (bf16[1024]{0:T(1024)(128)(2,1)S(1)}, bf16[1024]{0:T(1024)(128)(2,1)}, u32[]{:S(2)}) copy-start(bf16[1024]{0:T(1024)(128)(2,1)} %param.17) | copy-start | bytes 6148
  40.2 18.8 %copy-start.8 = (s32[1,64]{1,0:T(1,128)S(1)}, s32[1,64]{1,0:T(1,128)}, u32[]{:S(2)}) copy-start(s32[1,64]{1,0:T(1,128)} %param.16) | copy-start | bytes 772
  40.2 19.6 %copy-start.6 = (s32[1,4096]{1,0:T(1,128)S(1)}, s32[1,4096]{1,0:T(1,128)}, u32[]{:S(2)}) copy-start(s32[1,4096]{1,0:T(1,128)} %param.14) | copy-start | bytes 49156
  40.2 29.6 %copy-start.1 = (f32[8]{0:T(128)S(1)}, f32[8]{0:T(128)}, u32[]{:S(2)}) copy-start(f32[8]{0:T(128)} %sharp_ref.1) | copy-start | bytes 100
  40.2 13.2 %collective-permute-start.5 = (bf16[64,2048]{1,0:T(8,128)(2,1)S(1)}, bf16[64,2048]{1,0:T(8,128)(2,1)S(1)}, u32[]{:S(2)}, u32[]{:S(2)}) collective-permute-start(bf16[64,2048]{1,0:T(8,128)(2,1)S(1)} %slice_select_fusion), channel_id=1, source_target_pairs={{0,128},{32,416},{64,192},{96,480},{128,256},{160,32},{192,320},{2... | collective-permute-start | bytes 786440 | tf_op jit(solution)/shard_map/ppermute | solution.py:366
  43.1 10.3 %copy-start.3 = (bf16[128,2048]{1,0:T(8,128)(2,1)}, bf16[128,2048]{1,0:T(8,128)(2,1)S(1)}, u32[]{:S(2)}) copy-start(bf16[128,2048]{1,0:T(8,128)(2,1)S(1)} %collective-permute-done.2.refs_0_) | copy-start | bytes 1572868
  53.4 0.7 copy-start.5
  54.1 0.8 copy-start.4
  56.4 13.4 %collective-permute-start.6 = (bf16[448,2048]{1,0:T(8,128)(2,1)S(1)}, bf16[448,2048]{1,0:T(8,128)(2,1)}, u32[]{:S(2)}, u32[]{:S(2)}) collective-permute-start(bf16[448,2048]{1,0:T(8,128)(2,1)S(1)} %shard_map.133.mine_any), channel_id=1, source_target_pairs={{0,32},{32,0},{64,96},{96,64},{128,160},{160,128},{192,224},{224,1... | collective-permute-start | bytes 5505032 | tf_op jit(solution)/shard_map/ppermute | solution.py:385
  121.2 8.6 %copy-start = (s32[1,1,128]{2,1,0:T(1,128)S(1)}, s32[1,1,128]{2,1,0:T(1,128)}, u32[]{:S(2)}) copy-start(s32[1,1,128]{2,1,0:T(1,128)} %param.13) | copy-start | bytes 1540
  121.7 8.1 %collective-permute-start.7 = (bf16[128,512]{1,0:T(8,128)(2,1)S(1)}, bf16[128,512]{1,0:T(8,128)(2,1)S(1)}, u32[]{:S(2)}, u32[]{:S(2)}) collective-permute-start(bf16[128,512]{1,0:T(8,128)(2,1)S(1)} %get-tuple-element.23), channel_id=1, source_target_pairs={{0,24},{1,25},{2,26},{3,27},{4,28},{5,29},{6,30},{7,31},{8,16},{9,... | collective-permute-start | bytes 393224 | tf_op jit(solution)/shard_map/ppermute | solution.py:529
